TPU v7x, 32 devices: a whole 2x2x4 slice. The times are simulated.
32 devices in a mesh: dp: 2 (over y), expert: 16 (over z, x, core).
Axes of the slice: x: 2, y: 2, z: 4, core: 2. Of those that a mesh axis runs over, the one named last changes fastest.
Arguments:
- tokens: bfloat16 [1024, 2048], P(('dp', 'expert')), may hold values from -6 to 6
- route_weight: float32 [1024, 8], P(('dp', 'expert')), may hold values from 0.03 to 0.4
- upstream: bfloat16 [1024, 2048], P(('dp', 'expert')), may hold values from -6 to 6
- expert_index: int32 [1024, 8], P(('dp', 'expert')), may hold values from 0 to 15, all different within a row; in each aligned block of 32 rows (0 to 31, 32 to 63, ...) at most 20 rows name the same one
- gate_weight: bfloat16 [16, 2048, 768], P('expert', 'dp'), may hold values from -0.125 to 0.125
- up_weight: bfloat16 [16, 2048, 768], P('expert', 'dp'), may hold values from -0.125 to 0.125
- down_weight: bfloat16 [16, 2048, 768], P('expert', 'dp'), may hold values from -0.21875 to 0.21875
Outputs:
- combined: bfloat16 [1024, 2048], P(('dp', 'expert'))
- token_grad: bfloat16 [1024, 2048], P(('dp', 'expert'))
- route_grad: float32 [1024, 8], P(('dp', 'expert'))
- down_grad: bfloat16 [16, 2048, 768], P('expert', 'dp')
Inputs may be any that keep to these rules, and one draw needn't show every extreme that they name: `expert_index`: each row names 8 different experts. Among the rows of one device no expert is named more than 20 times, and in every draw some device names some expert exactly 20 times.
All inputs are finite; a program needn't handle non-finite values.
Results may differ from a plain program's by a relative error of at most 0.017.
Values may be sent and summed in bfloat16 or wider, within the bound.
No kernel may reach another device: no remote copies, remote signals or barrier semaphores. Data moves between devices by JAX's collectives and lax.ppermute only.
A program may use at most 128 MiB of HBM per device.

v0:
```python
import jax
import jax.numpy as jnp
from jax import lax
from jax.sharding import PartitionSpec as P


def silu_parts(gate_value):
    sigmoid_value = jax.nn.sigmoid(gate_value)
    return (gate_value * sigmoid_value, sigmoid_value * (1.0 + gate_value * (1.0 - sigmoid_value)))


def contract_last(left, right):
    return lax.dot_general(
        left, right, (((1,), (1,)), ((), ())), preferred_element_type=jnp.float32
    )


def contract_first(left, right):
    return lax.dot_general(
        left, right, (((0,), (0,)), ((), ())), preferred_element_type=jnp.float32
    )


def on_device(tokens, route_weight, upstream, expert_index, gate_weight, up_weight, down_weight):
    n_experts = lax.axis_size("expert")
    tok_count, top_count = expert_index.shape
    model_width = tokens.shape[1]
    assignments = tok_count * top_count
    capacity = max(2, (5 * assignments + 4 * n_experts - 1) // (4 * n_experts))
    slot_total = n_experts * capacity
    flat_ids = expert_index.reshape(assignments)
    onehot = (flat_ids[:, None] == jnp.arange(n_experts, dtype=jnp.int32)[None, :]).astype(
        jnp.int32
    )
    earlier = jnp.cumsum(onehot, axis=0) - onehot
    position = flat_ids * capacity + jnp.sum(earlier * onehot, axis=1)
    selector = position[None, :] == jnp.arange(slot_total, dtype=jnp.int32)[:, None]
    select_rows = selector.astype(jnp.bfloat16)
    select_tokens = (
        selector.reshape(slot_total, tok_count, top_count).any(axis=2).astype(jnp.bfloat16)
    )
    send_tokens = jnp.dot(select_tokens, tokens, preferred_element_type=jnp.float32).astype(
        jnp.bfloat16
    )
    send_tokens = send_tokens.reshape(n_experts, capacity, model_width)
    grad_rows = (route_weight[:, :, None] * upstream[:, None, :].astype(jnp.float32)).astype(
        jnp.bfloat16
    )
    grad_rows = grad_rows.reshape(assignments, model_width)
    send_grads = jnp.dot(select_rows, grad_rows, preferred_element_type=jnp.float32).astype(
        jnp.bfloat16
    )
    send_grads = send_grads.reshape(n_experts, capacity, model_width)
    routed_tokens, routed_grads = (
        lax.all_to_all(send_tokens, "expert", split_axis=0, concat_axis=0, tiled=True),
        lax.all_to_all(send_grads, "expert", split_axis=0, concat_axis=0, tiled=True),
    )
    routed_tokens = routed_tokens.reshape(slot_total, model_width)
    gathered = (
        lax.all_gather(gate_weight, "dp", axis=1, tiled=True),
        lax.all_gather(up_weight, "dp", axis=1, tiled=True),
        lax.all_gather(down_weight, "dp", axis=1, tiled=True),
    )
    w_gate, w_up, w_down = (gathered[0][0], gathered[1][0], gathered[2][0])
    gate_value = jnp.dot(routed_tokens, w_gate, preferred_element_type=jnp.float32)
    up_value = jnp.dot(routed_tokens, w_up, preferred_element_type=jnp.float32)
    activated, slope_value = silu_parts(gate_value)
    hidden = (activated * up_value).astype(jnp.bfloat16)
    expert_out = contract_last(hidden, w_down).astype(jnp.bfloat16)
    returned = lax.all_to_all(
        expert_out.reshape(n_experts, capacity, model_width),
        "expert",
        split_axis=0,
        concat_axis=0,
        tiled=True,
    )
    out_rows = contract_first(select_rows, returned.reshape(slot_total, model_width))
    out_rows = out_rows.reshape(tok_count, top_count, model_width)
    combined = jnp.sum(route_weight[:, :, None] * out_rows, axis=1).astype(jnp.bfloat16)
    route_grad = jnp.sum(out_rows * upstream[:, None, :].astype(jnp.float32), axis=2)
    routed_grads = routed_grads.reshape(slot_total, model_width)
    hidden_grad = jnp.dot(routed_grads, w_down, preferred_element_type=jnp.float32)
    down_grad = lax.psum_scatter(
        contract_first(routed_grads, hidden).astype(jnp.bfloat16),
        "dp",
        scatter_dimension=0,
        tiled=True,
    )[None]
    gate_grad = (hidden_grad * up_value * slope_value).astype(jnp.bfloat16)
    up_grad = (hidden_grad * activated).astype(jnp.bfloat16)
    row_grad = (contract_last(gate_grad, w_gate) + contract_last(up_grad, w_up)).astype(
        jnp.bfloat16
    )
    returned_grads = lax.all_to_all(
        row_grad.reshape(n_experts, capacity, model_width),
        "expert",
        split_axis=0,
        concat_axis=0,
        tiled=True,
    )
    token_grad = contract_first(
        select_tokens, returned_grads.reshape(slot_total, model_width)
    ).astype(jnp.bfloat16)
    return (combined, token_grad, route_grad, down_grad)


def solution(mesh):
    return jax.shard_map(
        on_device,
        mesh=mesh,
        in_specs=(
            P(("dp", "expert"), None),
            P(("dp", "expert"), None),
            P(("dp", "expert"), None),
            P(("dp", "expert"), None),
            P("expert", "dp", None),
            P("expert", "dp", None),
            P("expert", "dp", None),
        ),
        out_specs=(
            P(("dp", "expert"), None),
            P(("dp", "expert"), None),
            P(("dp", "expert"), None),
            P("expert", "dp", None),
        ),
        check_vma=False,
    )
```

profile of v0, /device:TPU:0, one launch (start us, length us, event | category | flops | bytes accessed | tf_op | source)
XLA Modules:
  0.0 241.4 jit_solution(8416025536137067177)
XLA Ops:
  7.2 0.0 copy-start
  7.2 0.0 all-gather.4.cloned.1.call-start
  7.2 0.0 copy-start.7
  7.2 0.7 all-gather.4.cloned.1.call-update
  7.9 0.0 all-gather.6.cloned.1.call-start
  8.0 0.7 all-gather.6.cloned.1.call-update
  8.7 0.0 copy-done.7
  8.7 0.1 copy.28
  8.8 0.1 reshape.95
  8.8 0.1 eq.65
  8.9 0.6 reduce-window.6
  9.5 0.2 slice_reduce_fusion
  9.8 0.1 fusion.36
  9.9 0.1 reduce_sum.30
  10.0 0.0 copy-start.5
  10.0 0.2 fusion.30
  10.2 0.0 copy-done
  10.2 0.6 convolution_convert_fusion.2
  10.7 1.3 reshape.97
  12.0 0.0 copy-done.5
  12.0 7.5 %all-to-all-start = ((bf16[16,20,2048]{2,1,0:T(8,128)(2,1)}), bf16[16,20,2048]{2,1,0:T(8,128)(2,1)S(1)}, u32[]{:S(2)}, u32[]{:S(2)}) async-start(bf16[16,20,2048]{2,1,0:T(8,128)(2,1)} %reshape.97), calls=%async_computation | async-start | bytes 3145728 | tf_op jit(solution)/shard_map/all_to_all | solution.py:55
  19.5 0.0 copy-done.4
  19.6 0.0 copy-done.8
  19.6 0.1 copy.27
  19.7 0.1 mul.81
  19.7 0.5 copy-done.6
  20.3 0.6 convolution_convert_fusion.1
  20.9 1.3 reshape.101
  22.2 29.3 %all-to-all-done = bf16[16,20,2048]{2,1,0:T(8,128)(2,1)S(1)} async-done(((bf16[16,20,2048]{2,1,0:T(8,128)(2,1)}), bf16[16,20,2048]{2,1,0:T(8,128)(2,1)S(1)}, u32[]{:S(2)}, u32[]{:S(2)}) %all-to-all-start) | async-done | bytes 1310752 | tf_op jit(solution)/shard_map/all_to_all | solution.py:55
  51.5 9.1 %all-to-all-start.2 = ((bf16[16,20,2048]{2,1,0:T(8,128)(2,1)}), bf16[16,20,2048]{2,1,0:T(8,128)(2,1)S(1)}, u32[]{:S(2)}, u32[]{:S(2)}) async-start(bf16[16,20,2048]{2,1,0:T(8,128)(2,1)} %reshape.101), calls=%async_computation.2 | async-start | bytes 3145728 | tf_op jit(solution)/shard_map/all_to_all | solution.py:56
  60.6 0.0 all-gather.8.cloned.1.call-start
  60.7 0.7 all-gather.8.cloned.1.call-update
  61.4 0.0 reduce-scatter.2.cloned.1.call-start
  61.4 1.2 reshape.98
  62.6 30.0 %all-to-all-done.2 = bf16[16,20,2048]{2,1,0:T(8,128)(2,1)S(1)} async-done(((bf16[16,20,2048]{2,1,0:T(8,128)(2,1)}), bf16[16,20,2048]{2,1,0:T(8,128)(2,1)S(1)}, u32[]{:S(2)}, u32[]{:S(2)}) %all-to-all-start.2) | async-done | bytes 1310752 | tf_op jit(solution)/shard_map/all_to_all | solution.py:56
  92.6 0.3 reshape.102
  92.9 0.0 copy-start.1
  92.9 0.0 copy-start.3
  92.9 0.0 all-gather.4.cloned.1.call-done
  93.0 4.9 %fusion.10 = f32[320,768]{1,0:T(8,128)} fusion(bf16[320,2048]{1,0:T(8,128)(2,1)} %reshape.98, bf16[1,2048,768]{2,1,0:T(8,128)(2,1)} %all-gather.4.cloned.1.call-done), kind=kOutput, calls=%fused_computation.11 | convolution fusion | flops 1006632960 | bytes 5439488 | tf_op jit(solution)/shard_map/dot_general | solution.py:65
  97.9 5.9 %all-gather.6.cloned.1.call-done = bf16[1,2048,768]{2,1,0:T(8,128)(2,1)} async-done(((bf16[1,1024,768]{2,1,0:T(8,128)(2,1)}), bf16[1,2048,768]{2,1,0:T(8,128)(2,1)}) %all-gather.6.cloned.1.call-update) | async-done | bytes 3145744 | tf_op jit(solution)/shard_map/all_gather | solution.py:61
  103.7 0.0 copy-done.3
  103.7 4.3 %multiply_convert_fusion.2 = (bf16[320,768]{1,0:T(8,128)(2,1)S(1)}, f32[320,768]{1,0:T(8,128)}) fusion(f32[320,768]{1,0:T(8,128)} %fusion.10, bf16[320,2048]{1,0:T(8,128)(2,1)S(1)} %copy-done.3, bf16[1,2048,768]{2,1,0:T(8,128)(2,1)} %all-gather.6.cloned.1.call-done), kind=kOutput, calls=%fused_computation.27 | convolution fusion | flops 1008107520 | bytes 6914048 | tf_op jit(solution)/shard_map/dot_general | solution.py:66
  108.1 0.0 copy-done.1
  108.1 3.5 %convolution_convert_fusion = bf16[2048,768]{1,0:T(8,128)(2,1)} fusion(bf16[320,2048]{1,0:T(8,128)(2,1)S(1)} %reshape.102, bf16[320,768]{1,0:T(8,128)(2,1)S(1)} %get-tuple-element.14), kind=kOutput, calls=%fused_computation | convolution fusion | flops 1008205824 | bytes 4947968 | tf_op jit(solution)/shard_map/dot_general | solution.py:19
  111.6 0.0 reduce-scatter.2.cloned.1.call-update
  111.6 38.6 %all-gather.8.cloned.1.call-done = bf16[1,2048,768]{2,1,0:T(8,128)(2,1)} async-done(((bf16[1,1024,768]{2,1,0:T(8,128)(2,1)}), bf16[1,2048,768]{2,1,0:T(8,128)(2,1)}) %all-gather.8.cloned.1.call-update) | async-done | bytes 3145744 | tf_op jit(solution)/shard_map/all_gather | solution.py:62
  150.3 3.1 %fusion.18 = bf16[320,2048]{1,0:T(8,128)(2,1)S(1)} fusion(bf16[320,768]{1,0:T(8,128)(2,1)S(1)} %get-tuple-element.14, bf16[1,2048,768]{2,1,0:T(8,128)(2,1)} %all-gather.8.cloned.1.call-done), kind=kOutput, calls=%fused_computation.15 | convolution fusion | flops 1007288320 | bytes 4947968 | tf_op jit(solution)/shard_map/dot_general | solution.py:13
  153.4 1.3 reshape.99
  154.7 5.7 %all-to-all-start.1 = ((bf16[16,20,2048]{2,1,0:T(8,128)(2,1)}), bf16[16,20,2048]{2,1,0:T(8,128)(2,1)S(1)}, u32[]{:S(2)}, u32[]{:S(2)}) async-start(bf16[16,20,2048]{2,1,0:T(8,128)(2,1)} %reshape.99), calls=%async_computation.1 | async-start | bytes 3145728 | tf_op jit(solution)/shard_map/all_to_all | solution.py:70
  160.5 3.2 %fusion = f32[320,768]{1,0:T(8,128)S(1)} fusion(bf16[320,2048]{1,0:T(8,128)(2,1)S(1)} %copy-done.2, bf16[1,2048,768]{2,1,0:T(8,128)(2,1)} %all-gather.8.cloned.1.call-done), kind=kOutput, calls=%fused_computation.1 | convolution fusion | flops 1006632960 | bytes 5439488 | tf_op jit(solution)/shard_map/dot_general | solution.py:82
  163.8 1.2 fusion.4
  165.0 0.6 copy-done.9
  165.6 0.3 copy-done.12
  165.9 1.4 fusion.15
  167.3 1.3 reshape.103
  168.6 23.8 %all-to-all-done.1 = bf16[16,20,2048]{2,1,0:T(8,128)(2,1)S(1)} async-done(((bf16[16,20,2048]{2,1,0:T(8,128)(2,1)}), bf16[16,20,2048]{2,1,0:T(8,128)(2,1)S(1)}, u32[]{:S(2)}, u32[]{:S(2)}) %all-to-all-start.1) | async-done | bytes 1310752 | tf_op jit(solution)/shard_map/all_to_all | solution.py:70
  192.4 9.1 %all-to-all-start.3 = ((bf16[16,20,2048]{2,1,0:T(8,128)(2,1)}), bf16[16,20,2048]{2,1,0:T(8,128)(2,1)S(1)}, u32[]{:S(2)}, u32[]{:S(2)}) async-start(bf16[16,20,2048]{2,1,0:T(8,128)(2,1)} %reshape.103), calls=%async_computation.3 | async-start | bytes 3145728 | tf_op jit(solution)/shard_map/all_to_all | solution.py:94
  201.5 1.2 reshape.105
  202.8 3.2 %multiply_reduce_fusion = (f32[32,8]{1,0:T(8,128)S(1)}, bf16[32,2048]{1,0:T(8,128)(2,1)}) fusion(f32[32,2048]{1,0:T(8,128)S(1)} %convert_element_type.54, f32[32,8]{1,0:T(8,128)} %copy-done.6, bf16[320,2048,1]{1,0,2:T(8,128)(2,1)} %reshape.105, s32[32,8]{1,0:T(8,128)} %copy-done.5), kind=kOutput, calls=%fused_computation.21 | convolution fusion | flops 337657600 | bytes 1707008 | tf_op jit(solution)/shard_map/dot_general | solution.py:19
  205.9 0.7 copy.33
  206.6 26.9 %all-to-all-done.3 = bf16[16,20,2048]{2,1,0:T(8,128)(2,1)S(1)} async-done(((bf16[16,20,2048]{2,1,0:T(8,128)(2,1)}), bf16[16,20,2048]{2,1,0:T(8,128)(2,1)S(1)}, u32[]{:S(2)}, u32[]{:S(2)}) %all-to-all-start.3) | async-done | bytes 1310752 | tf_op jit(solution)/shard_map/all_to_all | solution.py:94
  233.5 0.3 reshape.104
  233.8 1.0 convolution_convert_fusion.3
  (18 shorter events, 0.1 us)
Async XLA Ops:
  7.2 3.0 %copy-start = (bf16[32,2048]{1,0:T(8,128)(2,1)S(1)}, bf16[32,2048]{1,0:T(8,128)(2,1)}, u32[]{:S(2)}) copy-start(bf16[32,2048]{1,0:T(8,128)(2,1)} %param.7) | copy-start | bytes 393220
  7.2 85.8 %all-gather.4.cloned.1.call-start = ((), (), s32[]{:S(2)}) async-start(), calls=%async_computation.5 | async-start | bytes 4718592 | tf_op jit(solution)/shard_map/all_gather | solution.py:60
  7.2 1.4 copy-start.7
  7.9 95.8 %all-gather.6.cloned.1.call-start = ((), (), s32[]{:S(2)}) async-start(), calls=%async_computation.6 | async-start | bytes 4718592 | tf_op jit(solution)/shard_map/all_gather | solution.py:61
  10.0 2.1 copy-start.5
  12.0 7.5 %copy-start.4 = (bf16[32,2048]{1,0:T(8,128)(2,1)S(1)}, bf16[32,2048]{1,0:T(8,128)(2,1)}, u32[]{:S(2)}) copy-start(bf16[32,2048]{1,0:T(8,128)(2,1)} %param.9) | copy-start | bytes 393220
  12.0 7.5 %copy-start.8 = (f32[32,8]{0,1:T(8,128)S(1)}, f32[32,8]{0,1:T(8,128)}, u32[]{:S(2)}) copy-start(f32[32,8]{0,1:T(8,128)} %param.8) | copy-start | bytes 3076
  12.0 39.5 %all-to-all-start = ((bf16[16,20,2048]{2,1,0:T(8,128)(2,1)}), bf16[16,20,2048]{2,1,0:T(8,128)(2,1)S(1)}, u32[]{:S(2)}, u32[]{:S(2)}) async-start(bf16[16,20,2048]{2,1,0:T(8,128)(2,1)} %reshape.97), calls=%async_computation | async-start | bytes 3145728 | tf_op jit(solution)/shard_map/all_to_all | solution.py:55
  19.7 0.6 copy-start.6
  51.5 41.1 %all-to-all-start.2 = ((bf16[16,20,2048]{2,1,0:T(8,128)(2,1)}), bf16[16,20,2048]{2,1,0:T(8,128)(2,1)S(1)}, u32[]{:S(2)}, u32[]{:S(2)}) async-start(bf16[16,20,2048]{2,1,0:T(8,128)(2,1)} %reshape.101), calls=%async_computation.2 | async-start | bytes 3145728 | tf_op jit(solution)/shard_map/all_to_all | solution.py:56
  60.6 89.6 %all-gather.8.cloned.1.call-start = ((), (), s32[]{:S(2)}) async-start(), calls=%async_computation.7 | async-start | bytes 4718592 | tf_op jit(solution)/shard_map/all_gather | solution.py:62
  61.4 173.5 %reduce-scatter.2.cloned.1.call-start = ((), (), s32[]{:S(2)}) async-start(), calls=%async_computation.8 | async-start | bytes 4718592 | tf_op jit(solution)/shard_map/reduce_scatter | solution.py:83
  92.9 15.2 %copy-start.1 = (bf16[320,2048]{1,0:T(8,128)(2,1)}, bf16[320,2048]{1,0:T(8,128)(2,1)S(1)}, u32[]{:S(2)}) copy-start(bf16[320,2048]{1,0:T(8,128)(2,1)S(1)} %reshape.102) | copy-start | bytes 3932164
  92.9 10.8 %copy-start.3 = (bf16[320,2048]{1,0:T(8,128)(2,1)S(1)}, bf16[320,2048]{1,0:T(8,128)(2,1)}, u32[]{:S(2)}) copy-start(bf16[320,2048]{1,0:T(8,128)(2,1)} %reshape.98) | copy-start | bytes 3932164
  154.7 5.8 %copy-start.2 = (bf16[320,2048]{1,0:T(8,128)(2,1)S(1)}, bf16[320,2048]{1,0:T(8,128)(2,1)}, u32[]{:S(2)}) copy-start(bf16[320,2048]{1,0:T(8,128)(2,1)} %copy-done.1) | copy-start | bytes 3932164
  154.7 37.7 %all-to-all-start.1 = ((bf16[16,20,2048]{2,1,0:T(8,128)(2,1)}), bf16[16,20,2048]{2,1,0:T(8,128)(2,1)S(1)}, u32[]{:S(2)}, u32[]{:S(2)}) async-start(bf16[16,20,2048]{2,1,0:T(8,128)(2,1)} %reshape.99), calls=%async_computation.1 | async-start | bytes 3145728 | tf_op jit(solution)/shard_map/all_to_all | solution.py:70
  160.5 3.3 %copy-start.10 = (bf16[1,2048,768]{2,1,0:T(8,128)(2,1)S(1)}, bf16[1,2048,768]{2,1,0:T(8,128)(2,1)}, u32[]{:S(2)}) copy-start(bf16[1,2048,768]{2,1,0:T(8,128)(2,1)} %all-gather.6.cloned.1.call-done) | copy-start | bytes 9437188
  160.5 3.3 %copy-start.11 = (f32[320,768]{1,0:T(8,128)S(1)}, f32[320,768]{1,0:T(8,128)}, u32[]{:S(2)}) copy-start(f32[320,768]{1,0:T(8,128)} %fusion.10) | copy-start | bytes 2949124
  163.8 1.9 copy-start.9
  163.8 2.1 copy-start.12
  192.4 41.1 %all-to-all-start.3 = ((bf16[16,20,2048]{2,1,0:T(8,128)(2,1)}), bf16[16,20,2048]{2,1,0:T(8,128)(2,1)S(1)}, u32[]{:S(2)}, u32[]{:S(2)}) async-start(bf16[16,20,2048]{2,1,0:T(8,128)(2,1)} %reshape.103), calls=%async_computation.3 | async-start | bytes 3145728 | tf_op jit(solution)/shard_map/all_to_all | solution.py:94
Sparse Core Ops, SparseCore 0:
  9.6 47.6 all-gather.3
  58.8 44.9 all-gather.5
  105.3 44.9 all-gather.7
  152.9 43.3 reduce-scatter.1
where the time goes:
time: 245 us; the launch traced here: 241 us
  waiting for transfers between devices  157 us (64%)
  starting transfers between devices  31.6 us (13%)
  matrix products  27 us (11%)
  between operations  14 us (6%)
  local copies, waits for them, and re-layouts  11 us (4%)
    all_gather x1, waiting for transfers between devices, on_device(): lax.all_gather(down_weight, 'dp', axis=1, tiled=True)  38.6 us
    all_to_all x1, waiting for transfers between devices, on_device(): lax.all_to_all(send_grads, 'expert', split_axis=0, concat_axis=0, tiled=T...  30 us
    all_to_all x1, waiting for transfers between devices, on_device(): lax.all_to_all(send_tokens, 'expert', split_axis=0, concat_axis=0, tiled=...  29.3 us
    all_to_all x1, waiting for transfers between devices, on_device(): lax.all_to_all(row_grad.reshape(n_experts, capacity, model_width), 'exper...  26.9 us
    all_to_all x1, waiting for transfers between devices, on_device(): lax.all_to_all(expert_out.reshape(n_experts, capacity, model_width), 'exp...  23.8 us
    all_to_all x1, starting transfers between devices, on_device(): lax.all_to_all(send_grads, 'expert', split_axis=0, concat_axis=0, tiled=T...  9.11 us
    all_to_all x1, starting transfers between devices, on_device(): lax.all_to_all(row_grad.reshape(n_experts, capacity, model_width), 'exper...  9.11 us
    dot_general x3, matrix products, contract_first(): lax.dot_general(left, right, (((0,), (0,)), ((), ())), preferred_element_...  7.67 us
  transfers between devices with their start and end apart: 8, of which 6 were waited for; matrix products, arithmetic and copies ran while one was open for 16% of the time, Pallas kernels for 0%

commit v1 on v0

v1 whole, which is shorter than its diff:
```python
import functools

import jax
import jax.numpy as jnp
from jax import lax
from jax.experimental import pallas as pl
from jax.experimental.pallas import tpu as pltpu
from jax.sharding import PartitionSpec as P

BF16 = jnp.bfloat16
F32 = jnp.float32
LANES = 128
CORE, SIDE = 2, 2
VMEM = pl.BlockSpec(memory_space=pltpu.VMEM)
SMEM = pl.BlockSpec(memory_space=pltpu.SMEM)
PARAMS = pltpu.CompilerParams(vmem_limit_bytes=32 * 1024 * 1024)


def dot_of(left, right, left_dim, right_dim):
    return lax.dot_general(
        left, right, (((left_dim,), (right_dim,)), ((), ())), preferred_element_type=F32
    )


def call(body, out_shapes, args, flops=0):
    moved = sum(a.size * a.dtype.itemsize for a in args)
    return pl.pallas_call(
        body,
        out_shape=[jax.ShapeDtypeStruct(s, t) for s, t in out_shapes],
        in_specs=[SMEM] + [VMEM] * (len(args) - 1),
        out_specs=[VMEM] * len(out_shapes),
        compiler_params=PARAMS,
        cost_estimate=pl.CostEstimate(flops=flops, bytes_accessed=moved, transcendentals=0),
    )(*args)


def pack_kernel(n_dp, n_experts, half, ids, tok_ref, up_ref, rw_ref, idx_ref, *outs):
    rows, top = idx_ref.shape
    extra = outs[0].shape[1] - 2 * half
    lane = lax.broadcasted_iota(jnp.int32, (rows, extra), 1)
    high_at, low_at = jnp.zeros((rows, extra), F32), jnp.zeros((rows, extra), F32)
    for k in range(top):
        named = idx_ref[:, k : k + 1]
        weight = rw_ref[:, k : k + 1]
        high_at = jnp.where(lane == named, weight, high_at)
        low_at = jnp.where(lane == named + n_experts, weight, low_at)
    low_at = low_at - low_at.astype(BF16).astype(F32)
    routing = (high_at + low_at).astype(BF16)
    for s, out in enumerate(outs):
        owner = lax.rem(ids[0] + s, n_dp)
        at = pl.ds(pl.multiple_of(owner * half, LANES), half)
        out[:, :half] = tok_ref[:, at]
        out[:, half : 2 * half] = up_ref[:, at]
        out[:, 2 * half :] = routing


def forward_kernel(n_dp, n_experts, tok, cap, ids, near, side, core, wg, wu, wd, part, up_rows, sel, weight):
    half, ff = wg.shape
    data = jnp.concatenate([near[...], side[...], core[...]], axis=0)
    total, rows = data.shape[0], sel.shape[0]
    routing = data[:, 2 * half :]
    lane = lax.broadcasted_iota(jnp.int32, (8, routing.shape[1]), 1)
    pick = jnp.where((lane == ids[1]) | (lane == ids[1] + n_experts), 1.0, 0.0).astype(BF16)
    w_row = dot_of(pick, routing, 1, 1)
    chosen = w_row > 0.0
    before = lax.broadcasted_iota(jnp.int32, (total, total), 0)
    after = lax.broadcasted_iota(jnp.int32, (total, total), 1)
    earlier = jnp.where((before < after) & (before // tok == after // tok), 1.0, 0.0).astype(BF16)
    slot = dot_of(jnp.where(chosen, 1.0, 0.0).astype(BF16), earlier, 1, 0)
    block = lax.broadcasted_iota(jnp.int32, (8, total), 1) // tok
    shift = block % n_dp
    source = ids[0] - shift
    source = jnp.where(source < 0, source + n_dp, source)
    place = jnp.where(chosen, slot.astype(jnp.int32) + cap * (block - shift + source), -1)
    picked = lax.broadcasted_iota(jnp.int32, (rows, total), 0) == place[:1]
    chooser = jnp.where(picked, 1.0, 0.0).astype(BF16)
    sel[...] = chooser
    w_col = jnp.sum(jnp.where(picked, w_row[:1], 0.0), axis=1, keepdims=True)
    weight[...] = jnp.broadcast_to(w_col, weight.shape)
    tok_rows = dot_of(chooser, data[:, :half], 1, 0).astype(BF16)
    grad_rows = dot_of(chooser, data[:, half : 2 * half], 1, 0).astype(BF16)
    up_rows[...] = grad_rows
    part[:, :ff] = dot_of(tok_rows, wg[...], 1, 0).astype(BF16)
    part[:, ff : 2 * ff] = dot_of(tok_rows, wu[...], 1, 0).astype(BF16)
    part[:, 2 * ff :] = dot_of(grad_rows, wd[...], 1, 0).astype(BF16)


def backward_kernel(n_experts, n_parts, ids, *refs):
    parts = refs[:n_parts]
    sel, weight, wg, wu, wd, keep, send, hidden_rows = refs[n_parts:]
    half, ff = wg.shape
    whole = parts[0][...].astype(F32)
    for other in parts[1:]:
        whole = whole + other[...].astype(F32)
    gate, up, grad = whole[:, :ff], whole[:, ff : 2 * ff], whole[:, 2 * ff :]
    w_col = weight[:, :1]
    sig = 1.0 / (1.0 + jnp.exp(-gate))
    act = gate * sig
    hidden = act * up
    route = jnp.sum(hidden * grad, axis=1, keepdims=True)
    grad = grad * w_col
    weighted = (hidden * w_col).astype(BF16)
    hidden_rows[...] = weighted
    gate_grad = (grad * up * (sig * (1.0 + gate * (1.0 - sig)))).astype(BF16)
    up_grad = (grad * act).astype(BF16)
    lane = lax.broadcasted_iota(jnp.int32, (whole.shape[0], keep.shape[1] - 2 * half), 1)
    high = route.astype(BF16).astype(F32)
    columns = jnp.where(lane == ids[1], high, jnp.where(lane == ids[1] + n_experts, route - high, 0.0))
    spread = jnp.concatenate([weighted, gate_grad, up_grad, columns.astype(BF16)], axis=1)
    spread = dot_of(sel[...], spread, 0, 0).astype(BF16)
    out = dot_of(spread[:, :ff], wd[...], 1, 1)
    back = dot_of(spread[:, ff : 2 * ff], wg[...], 1, 1)
    back = back + dot_of(spread[:, 2 * ff : 3 * ff], wu[...], 1, 1)
    tops = keep.shape[0]
    for ref, rows in ((keep, slice(0, tops)), (send, slice(tops, 2 * tops))):
        ref[:, :half] = out[rows].astype(BF16)
        ref[:, half : 2 * half] = back[rows].astype(BF16)
        ref[:, 2 * half :] = spread[rows, 3 * ff :]


def down_kernel(chunks, ids, *refs):
    up_rows = jnp.concatenate([r[...] for r in refs[:chunks]], axis=0)
    hidden = jnp.concatenate([r[...] for r in refs[chunks : 2 * chunks]], axis=0)
    refs[2 * chunks][...] = dot_of(up_rows, hidden, 0, 0).astype(BF16)


def final_kernel(n_dp, n_experts, half, ids, own, idx_ref, *refs):
    others, (comb, grad, route) = refs[: n_dp - 1], refs[n_dp - 1 :]
    for s in range(n_dp):
        owner = lax.rem(ids[0] + s, n_dp)
        at = pl.ds(pl.multiple_of(owner * half, LANES), half)
        source = own if s == 0 else others[s - 1]
        comb[:, at] = source[:, :half]
        grad[:, at] = source[:, half : 2 * half]
    columns = own[:, 2 * half :].astype(F32)
    lane = lax.broadcasted_iota(jnp.int32, columns.shape, 1)
    rows, top = route.shape
    slot = lax.broadcasted_iota(jnp.int32, (rows, top), 1)
    result = jnp.zeros((rows, top), F32)
    for k in range(top):
        named = idx_ref[:, k : k + 1]
        mine = (lane == named) | (lane == named + n_experts)
        value = jnp.sum(jnp.where(mine, columns, 0.0), axis=1, keepdims=True)
        result = jnp.where(slot == k, value, result)
    route[...] = result


def added(left, right):
    return (left.astype(F32) + right.astype(F32)).astype(BF16)


def on_device(tokens, route_weight, upstream, expert_index, gate_weight, up_weight, down_weight):
    n_experts, n_dp = lax.axis_size("expert"), lax.axis_size("dp")
    tok, top = expert_index.shape
    width = tokens.shape[1]
    wg, wu, wd = gate_weight[0], up_weight[0], down_weight[0]
    half, ff = wg.shape
    cap = max(2, (5 * tok * top + 4 * n_experts - 1) // (4 * n_experts))
    extra = -(-2 * n_experts // LANES) * LANES
    layers = n_experts // (SIDE * CORE)
    wide = 2 * half + extra
    group = n_dp * tok
    rows = CORE * SIDE * n_dp * cap
    total = CORE * SIDE * group
    ids = jnp.stack([lax.axis_index("dp"), lax.axis_index("expert")]).astype(jnp.int32)

    def dp_shift(x, s):
        return lax.ppermute(x, "dp", [(i, (i + s) % n_dp) for i in range(n_dp)])

    def layer_shift(x, k):
        step = SIDE * CORE * k
        return lax.ppermute(x, "expert", [(i, (i + step) % n_experts) for i in range(n_experts)])

    def swap(x, bit):
        return lax.ppermute(x, "expert", [(i, i ^ bit) for i in range(n_experts)])

    blocks = call(
        functools.partial(pack_kernel, n_dp, n_experts, half),
        [((tok, wide), BF16)] * n_dp,
        (ids, tokens, upstream, route_weight, expert_index),
    )
    mine = jnp.concatenate([blocks[0]] + [dp_shift(blocks[s], s) for s in range(1, n_dp)], axis=0)

    order = [0]
    for k in range(1, layers // 2 + 1):
        order += [k] if 2 * k == layers else [k, layers - k]
    order = order[:layers]

    near = {k: mine if k == 0 else layer_shift(mine, k) for k in order}
    parts, kept = {}, {}
    for k in order:
        side = swap(near[k], CORE)
        core = swap(jnp.concatenate([near[k], side], axis=0), 1)
        part, up_rows, sel, weight = call(
            functools.partial(forward_kernel, n_dp, n_experts, tok, cap),
            [
                ((rows, 3 * ff), BF16),
                ((rows, half), BF16),
                ((rows, total), BF16),
                ((rows, LANES), F32),
            ],
            (ids, near[k], side, core, wg, wu, wd),
            flops=2 * rows * half * 3 * ff + 4 * rows * total * half,
        )
        parts[k] = [part] + [dp_shift(part, s) for s in range(1, n_dp)]
        kept[k] = (up_rows, sel, weight)

    hidden_rows, sums = {}, {}
    for k in order:
        up_rows, sel, weight = kept[k]
        keep, send, hidden_rows[k] = call(
            functools.partial(backward_kernel, n_experts, n_dp),
            [((total // 2, wide), BF16), ((total // 2, wide), BF16), ((rows, ff), BF16)],
            (ids, *parts[k], sel, weight, wg, wu, wd),
            flops=2 * total * half * 3 * ff + 2 * rows * total * 3 * ff,
        )
        back = swap(send, 1)
        outward = swap(added(keep[group:], back[group:]), CORE)
        partial = added(added(keep[:group], back[:group]), outward)
        sums[k] = partial if k == 0 else layer_shift(partial, -k)

    (down_grad,) = call(
        functools.partial(down_kernel, layers),
        [((half, ff), BF16)],
        (ids, *[kept[k][0] for k in order], *[hidden_rows[k] for k in order]),
        flops=2 * layers * rows * half * ff,
    )
    result = sums[0].astype(F32)
    for k in order[1:]:
        result = result + sums[k].astype(F32)
    result = result.astype(BF16)
    others = [dp_shift(result[s * tok : (s + 1) * tok, : 2 * half], -s) for s in range(1, n_dp)]
    combined, token_grad, route_grad = call(
        functools.partial(final_kernel, n_dp, n_experts, half),
        [((tok, width), BF16), ((tok, width), BF16), ((tok, top), F32)],
        (ids, result[:tok], expert_index, *others),
    )
    return (combined, token_grad, route_grad, down_grad[None])


def solution(mesh):
    return jax.shard_map(
        on_device,
        mesh=mesh,
        in_specs=(
            P(("dp", "expert"), None),
            P(("dp", "expert"), None),
            P(("dp", "expert"), None),
            P(("dp", "expert"), None),
            P("expert", "dp", None),
            P("expert", "dp", None),
            P("expert", "dp", None),
        ),
        out_specs=(
            P(("dp", "expert"), None),
            P(("dp", "expert"), None),
            P(("dp", "expert"), None),
            P("expert", "dp", None),
        ),
        check_vma=False,
    )
```

time: 245 us -> 174 us (0.71); the launches traced: 241 us -> 174 us
  waiting for transfers between devices: 157 us -> 114 us
  matrix products: 27 us -> 0 us
  Pallas kernels: 0 us -> 24.2 us
  between operations: 14 us -> 0.91 us
  local copies, waits for them, and re-layouts: 11 us -> 4.05 us
    ppermute x0 -> x28, waiting for transfers between devices: none -> 114 us  [the longest x6 52.4 us: dp_shift(): return lax.ppermute(x, 'dp', [(i, (i + s) % n_dp) for i in range(n_dp)])]
    all_to_all x4 -> x0, waiting for transfers between devices: 110 us -> none  [the longest x1 30 us: on_device(): lax.all_to_all(send_grads, 'expert', split_axis=0, concat_axis=0, tiled=T...]
    all_gather x3 -> x0, waiting for transfers between devices: 44.5 us -> none  [the longest x1 38.6 us: on_device(): lax.all_gather(down_weight, 'dp', axis=1, tiled=True)]
    all_to_all x4 -> x0, starting transfers between devices: 31.4 us -> none  [the longest x1 9.11 us: on_device(): lax.all_to_all(send_grads, 'expert', split_axis=0, concat_axis=0, tiled=T...]
    ppermute x0 -> x28, starting transfers between devices: none -> 29.8 us  [the longest x6 10.9 us: layer_shift(): lax.ppermute(x, 'expert', [(i, (i + step) % n_experts) for i in range(n_e...]
    dot_general x11 -> x0, matrix products: 27 us -> none  [the longest x3 7.67 us: contract_first(): lax.dot_general(left, right, (((0,), (0,)), ((), ())), preferred_element_...]
    pallas_call x0 -> x11, Pallas kernels: none -> 24.2 us  [call(): pl.pallas_call(body, out_shape=[jax.ShapeDtypeStruct(s, t) for s, t in ou...]
    reshape x9 -> x0, local copies, waits for them, and re-layouts: 8.32 us -> none  [the longest x1 1.32 us: on_device(): expert_out.reshape(n_experts, capacity, model_width)]
  transfers between devices with their start and end apart: 8 -> 28, of which waited for: 6 -> 15; matrix products, arithmetic and copies ran while one was open for 16% -> 0% of each run, Pallas kernels for 0% -> 12%
where the time goes in v1:
time: 174 us
  waiting for transfers between devices  114 us (66%)
  starting transfers between devices  29.8 us (17%)
  Pallas kernels  24.2 us (14%)
  local copies, waits for them, and re-layouts  4.05 us (2%)
    ppermute x6, waiting for transfers between devices, dp_shift(): return lax.ppermute(x, 'dp', [(i, (i + s) % n_dp) for i in range(n_dp)])  52.4 us
    ppermute x16, waiting for transfers between devices, swap(): return lax.ppermute(x, 'expert', [(i, i ^ bit) for i in range(n_experts)])  35.2 us
    ppermute x6, waiting for transfers between devices, layer_shift(): lax.ppermute(x, 'expert', [(i, (i + step) % n_experts) for i in range(n_e...  26.3 us
    pallas_call x11, Pallas kernels, call(): pl.pallas_call(body, out_shape=[jax.ShapeDtypeStruct(s, t) for s, t in ou...  24.2 us
    ppermute x6, starting transfers between devices, layer_shift(): lax.ppermute(x, 'expert', [(i, (i + step) % n_experts) for i in range(n_e...  10.9 us
    ppermute x16, starting transfers between devices, swap(): return lax.ppermute(x, 'expert', [(i, i ^ bit) for i in range(n_experts)])  9.93 us
    ppermute x6, starting transfers between devices, dp_shift(): return lax.ppermute(x, 'dp', [(i, (i + s) % n_dp) for i in range(n_dp)])  8.94 us
    unnamed x14, local copies, waits for them, and re-layouts  4.02 us
  transfers between devices with their start and end apart: 28, of which 15 were waited for; matrix products, arithmetic and copies ran while one was open for 0% of the time, Pallas kernels for 12%

profile of v1, /device:TPU:0, one launch (start us, length us, event | category | flops | bytes accessed | tf_op | source)
XLA Modules:
  0.0 173.8 jit_solution(3183310170381561675)
XLA Ops:
  0.6 0.8 copy.11.rw_ref
  1.4 0.8 copy.12.idx_ref
  2.2 0.1 pad_add_fusion.ids
  2.2 0.9 copy-done.3
  3.1 0.9 copy-done.4
  4.0 0.7 shard_map.102
  4.8 3.0 %collective-permute-start = (bf16[32,2176]{1,0:T(8,128)(2,1)S(1)}, bf16[32,2176]{1,0:T(8,128)(2,1)S(1)}, u32[]{:S(2)}, u32[]{:S(2)}) collective-permute-start(bf16[32,2176]{1,0:T(8,128)(2,1)S(1)} %get-tuple-element.38), channel_id=1, source_target_pairs={{0,16},{16,0},{1,17},{17,1},{2,18},{18,2},{3,19},{19,3},{4,20},{20... | collective-permute-start | bytes 417800 | tf_op jit(solution)/shard_map/ppermute | solution.py:168
  7.8 3.7 %collective-permute-done = bf16[32,2176]{1,0:T(8,128)(2,1)S(1)} collective-permute-done((bf16[32,2176]{1,0:T(8,128)(2,1)S(1)}, bf16[32,2176]{1,0:T(8,128)(2,1)S(1)}, u32[]{:S(2)}, u32[]{:S(2)}) %collective-permute-start) | collective-permute-done | bytes 139296 | tf_op jit(solution)/shard_map/ppermute | solution.py:168
  11.5 2.9 %collective-permute-start.20 = (bf16[64,2176]{1,0:T(8,128)(2,1)S(1)}, bf16[64,2176]{1,0:T(8,128)(2,1)S(1)}, u32[]{:S(2)}, u32[]{:S(2)}) collective-permute-start(bf16[64,2176]{1,0:T(8,128)(2,1)S(1)} %constant_dynamic-update-slice_fusion.near), channel_id=1, source_target_pairs={{0,8},{1,9},{2,10},{3,11},{4,12},{5,13},{6,14},{7,15},{8,0},{9,1},... | collective-permute-start | bytes 835592 | tf_op jit(solution)/shard_map/ppermute | solution.py:172
  14.4 1.5 collective-permute-start.1
  15.9 1.3 collective-permute-start.13
  17.2 0.7 collective-permute-start.6
  17.9 15.5 %collective-permute-done.20.near = bf16[64,2176]{1,0:T(8,128)(2,1)S(1)} collective-permute-done((bf16[64,2176]{1,0:T(8,128)(2,1)S(1)}, bf16[64,2176]{1,0:T(8,128)(2,1)S(1)}, u32[]{:S(2)}, u32[]{:S(2)}) %collective-permute-start.20) | collective-permute-done | bytes 278560 | tf_op jit(solution)/shard_map/ppermute | solution.py:172
  33.4 1.5 collective-permute-start.21
  34.9 0.1 collective-permute-start.2
  35.0 0.6 collective-permute-start.14
  35.6 1.5 collective-permute-start.7
  37.1 4.7 %collective-permute-done.21.side = bf16[64,2176]{1,0:T(8,128)(2,1)S(1)} collective-permute-done((bf16[64,2176]{1,0:T(8,128)(2,1)S(1)}, bf16[64,2176]{1,0:T(8,128)(2,1)S(1)}, u32[]{:S(2)}, u32[]{:S(2)}) %collective-permute-start.21) | collective-permute-done | bytes 278560 | tf_op jit(solution)/shard_map/ppermute | solution.py:175
  41.8 0.1 collective-permute-start.22
  41.9 5.8 %collective-permute-done.14.side = bf16[64,2176]{1,0:T(8,128)(2,1)S(1)} collective-permute-done((bf16[64,2176]{1,0:T(8,128)(2,1)S(1)}, bf16[64,2176]{1,0:T(8,128)(2,1)S(1)}, u32[]{:S(2)}, u32[]{:S(2)}) %collective-permute-start.14) | collective-permute-done | bytes 278560 | tf_op jit(solution)/shard_map/ppermute | solution.py:175
  47.8 0.1 collective-permute-start.15
  47.8 4.0 %collective-permute-done.7.side = bf16[64,2176]{1,0:T(8,128)(2,1)S(1)} collective-permute-done((bf16[64,2176]{1,0:T(8,128)(2,1)S(1)}, bf16[64,2176]{1,0:T(8,128)(2,1)S(1)}, u32[]{:S(2)}, u32[]{:S(2)}) %collective-permute-start.7) | collective-permute-done | bytes 278560 | tf_op jit(solution)/shard_map/ppermute | solution.py:175
  51.9 0.1 collective-permute-start.8
  52.0 1.9 %shard_map.103 = (bf16[160,2304]{1,0:T(8,128)(2,1)S(1)}, bf16[160,1024]{1,0:T(8,128)(2,1)S(1)}, bf16[160,256]{1,0:T(8,128)(2,1)S(1)}, f32[160,128]{1,0:T(8,128)S(1)}) custom-call(s32[2]{0:T(128)S(1)} %pad_add_fusion.ids, bf16[64,2176]{1,0:T(8,128)(2,1)S(1)} %constant_dynamic-update-slice_fusion.near, bf16[64,2176]{1,0:T(8,128)(2,1)S(1)} %collective-permute-done.1.side, ...), custom_call_target="tpu_custom_call" | custom-call | flops 922746880 | bytes 5832712 | tf_op jit(solution)/shard_map/pallas_call | solution.py:27
  54.0 1.6 collective-permute-start.3
  55.6 1.9 %shard_map.109 = (bf16[160,2304]{1,0:T(8,128)(2,1)S(1)}, bf16[160,1024]{1,0:T(8,128)(2,1)S(1)}, bf16[160,256]{1,0:T(8,128)(2,1)S(1)}, f32[160,128]{1,0:T(8,128)S(1)}) custom-call(s32[2]{0:T(128)S(1)} %pad_add_fusion.ids, bf16[64,2176]{1,0:T(8,128)(2,1)S(1)} %collective-permute-done.20.near, bf16[64,2176]{1,0:T(8,128)(2,1)S(1)} %collective-permute-done.21.side, ...), custom_call_target="tpu_custom_call" | custom-call | flops 922746880 | bytes 5832712 | tf_op jit(solution)/shard_map/pallas_call | solution.py:27
  57.5 0.6 collective-permute-start.23
  58.0 1.9 %shard_map.107 = (bf16[160,2304]{1,0:T(8,128)(2,1)S(1)}, bf16[160,1024]{1,0:T(8,128)(2,1)S(1)}, bf16[160,256]{1,0:T(8,128)(2,1)S(1)}, f32[160,128]{1,0:T(8,128)S(1)}) custom-call(s32[2]{0:T(128)S(1)} %pad_add_fusion.ids, bf16[64,2176]{1,0:T(8,128)(2,1)S(1)} %collective-permute-done.13.near, bf16[64,2176]{1,0:T(8,128)(2,1)S(1)} %collective-permute-done.14.side, ...), custom_call_target="tpu_custom_call" | custom-call | flops 922746880 | bytes 5832712 | tf_op jit(solution)/shard_map/pallas_call | solution.py:27
  60.0 1.6 collective-permute-start.16
  61.6 1.9 %shard_map.105 = (bf16[160,2304]{1,0:T(8,128)(2,1)S(1)}, bf16[160,1024]{1,0:T(8,128)(2,1)S(1)}, bf16[160,256]{1,0:T(8,128)(2,1)S(1)}, f32[160,128]{1,0:T(8,128)S(1)}) custom-call(s32[2]{0:T(128)S(1)} %pad_add_fusion.ids, bf16[64,2176]{1,0:T(8,128)(2,1)S(1)} %collective-permute-done.6.near, bf16[64,2176]{1,0:T(8,128)(2,1)S(1)} %collective-permute-done.7.side, ...), custom_call_target="tpu_custom_call" | custom-call | flops 922746880 | bytes 5832712 | tf_op jit(solution)/shard_map/pallas_call | solution.py:27
  63.5 0.6 collective-permute-start.9
  64.1 9.3 %collective-permute-done.3.refs_1_ = bf16[160,2304]{1,0:T(8,128)(2,1)S(1)} collective-permute-done((bf16[160,2304]{1,0:T(8,128)(2,1)S(1)}, bf16[160,2304]{1,0:T(8,128)(2,1)S(1)}, u32[]{:S(2)}, u32[]{:S(2)}) %collective-permute-start.3) | collective-permute-done | bytes 737312 | tf_op jit(solution)/shard_map/ppermute | solution.py:168
  73.3 2.7 %shard_map.104 = (bf16[128,2176]{1,0:T(8,128)(2,1)S(1)}, bf16[128,2176]{1,0:T(8,128)(2,1)S(1)}, bf16[160,768]{1,0:T(8,128)(2,1)S(1)}) custom-call(s32[2]{0:T(128)S(1)} %pad_add_fusion.ids, bf16[160,2304]{1,0:T(8,128)(2,1)S(1)} %get-tuple-element.39.refs_0_, bf16[160,2304]{1,0:T(8,128)(2,1)S(1)} %collective-permute-done.3.refs_1_, ...), custom_call_target="tpu_custom_call" | custom-call | flops 1396703232 | bytes 6357000 | tf_op jit(solution)/shard_map/pallas_call | solution.py:27
  76.0 0.1 collective-permute-start.4
  76.1 13.1 %collective-permute-done.23.refs_1_ = bf16[160,2304]{1,0:T(8,128)(2,1)S(1)} collective-permute-done((bf16[160,2304]{1,0:T(8,128)(2,1)S(1)}, bf16[160,2304]{1,0:T(8,128)(2,1)S(1)}, u32[]{:S(2)}, u32[]{:S(2)}) %collective-permute-start.23) | collective-permute-done | bytes 737312 | tf_op jit(solution)/shard_map/ppermute | solution.py:168
  89.1 2.6 %shard_map.110 = (bf16[128,2176]{1,0:T(8,128)(2,1)S(1)}, bf16[128,2176]{1,0:T(8,128)(2,1)S(1)}, bf16[160,768]{1,0:T(8,128)(2,1)S(1)}) custom-call(s32[2]{0:T(128)S(1)} %pad_add_fusion.ids, bf16[160,2304]{1,0:T(8,128)(2,1)S(1)} %get-tuple-element.54.refs_0_, bf16[160,2304]{1,0:T(8,128)(2,1)S(1)} %collective-permute-done.23.refs_1_, ...), custom_call_target="tpu_custom_call" | custom-call | flops 1396703232 | bytes 6357000 | tf_op jit(solution)/shard_map/pallas_call | solution.py:27
  91.8 0.1 collective-permute-start.24
  91.9 13.1 %collective-permute-done.16.refs_1_ = bf16[160,2304]{1,0:T(8,128)(2,1)S(1)} collective-permute-done((bf16[160,2304]{1,0:T(8,128)(2,1)S(1)}, bf16[160,2304]{1,0:T(8,128)(2,1)S(1)}, u32[]{:S(2)}, u32[]{:S(2)}) %collective-permute-start.16) | collective-permute-done | bytes 737312 | tf_op jit(solution)/shard_map/ppermute | solution.py:168
  104.9 2.7 %shard_map.108 = (bf16[128,2176]{1,0:T(8,128)(2,1)S(1)}, bf16[128,2176]{1,0:T(8,128)(2,1)S(1)}, bf16[160,768]{1,0:T(8,128)(2,1)S(1)}) custom-call(s32[2]{0:T(128)S(1)} %pad_add_fusion.ids, bf16[160,2304]{1,0:T(8,128)(2,1)S(1)} %get-tuple-element.49.refs_0_, bf16[160,2304]{1,0:T(8,128)(2,1)S(1)} %collective-permute-done.16.refs_1_, ...), custom_call_target="tpu_custom_call" | custom-call | flops 1396703232 | bytes 6357000 | tf_op jit(solution)/shard_map/pallas_call | solution.py:27
  107.6 0.1 collective-permute-start.17
  107.7 12.6 %collective-permute-done.9.refs_1_ = bf16[160,2304]{1,0:T(8,128)(2,1)S(1)} collective-permute-done((bf16[160,2304]{1,0:T(8,128)(2,1)S(1)}, bf16[160,2304]{1,0:T(8,128)(2,1)S(1)}, u32[]{:S(2)}, u32[]{:S(2)}) %collective-permute-start.9) | collective-permute-done | bytes 737312 | tf_op jit(solution)/shard_map/ppermute | solution.py:168
  120.3 2.8 %shard_map.106 = (bf16[128,2176]{1,0:T(8,128)(2,1)S(1)}, bf16[128,2176]{1,0:T(8,128)(2,1)S(1)}, bf16[160,768]{1,0:T(8,128)(2,1)S(1)}) custom-call(s32[2]{0:T(128)S(1)} %pad_add_fusion.ids, bf16[160,2304]{1,0:T(8,128)(2,1)S(1)} %get-tuple-element.44.refs_0_, bf16[160,2304]{1,0:T(8,128)(2,1)S(1)} %collective-permute-done.9.refs_1_, ...), custom_call_target="tpu_custom_call" | custom-call | flops 1396703232 | bytes 6357000 | tf_op jit(solution)/shard_map/pallas_call | solution.py:27
  123.1 0.1 collective-permute-start.10
  123.3 1.5 collective-permute-start.5
  124.9 0.6 collective-permute-start.25
  125.6 1.5 collective-permute-start.18
  127.2 0.6 collective-permute-start.11
  127.8 10.9 %collective-permute-done.25 = bf16[64,2176]{1,0:T(8,128)(2,1)S(1)} collective-permute-done((bf16[64,2176]{1,0:T(8,128)(2,1)S(1)}, bf16[64,2176]{1,0:T(8,128)(2,1)S(1)}, u32[]{:S(2)}, u32[]{:S(2)}) %collective-permute-start.25) | collective-permute-done | bytes 278560 | tf_op jit(solution)/shard_map/ppermute | solution.py:175
  138.8 0.1 add_convert_fusion.1
  138.9 0.1 collective-permute-start.26
  139.0 5.8 %collective-permute-done.18 = bf16[64,2176]{1,0:T(8,128)(2,1)S(1)} collective-permute-done((bf16[64,2176]{1,0:T(8,128)(2,1)S(1)}, bf16[64,2176]{1,0:T(8,128)(2,1)S(1)}, u32[]{:S(2)}, u32[]{:S(2)}) %collective-permute-start.18) | collective-permute-done | bytes 278560 | tf_op jit(solution)/shard_map/ppermute | solution.py:175
  144.8 0.1 add_convert_fusion.4
  144.9 1.6 collective-permute-start.19
  146.4 3.9 %collective-permute-done.11 = bf16[64,2176]{1,0:T(8,128)(2,1)S(1)} collective-permute-done((bf16[64,2176]{1,0:T(8,128)(2,1)S(1)}, bf16[64,2176]{1,0:T(8,128)(2,1)S(1)}, u32[]{:S(2)}, u32[]{:S(2)}) %collective-permute-start.11) | collective-permute-done | bytes 278560 | tf_op jit(solution)/shard_map/ppermute | solution.py:175
  150.3 0.1 add_convert_fusion.7
  150.4 4.4 %collective-permute-start.12 = (bf16[64,2176]{1,0:T(8,128)(2,1)S(1)}, bf16[64,2176]{1,0:T(8,128)(2,1)S(1)}, u32[]{:S(2)}, u32[]{:S(2)}) collective-permute-start(bf16[64,2176]{1,0:T(8,128)(2,1)S(1)} %add_convert_fusion.7), channel_id=1, source_target_pairs={{0,12},{1,13},{2,14},{3,15},{4,0},{5,1},{6,2},{7,3},{8,4},{9,5},{1... | collective-permute-start | bytes 835592 | tf_op jit(solution)/shard_map/ppermute | solution.py:172
  154.8 6.6 %collective-permute-done.26 = bf16[64,2176]{1,0:T(8,128)(2,1)S(1)} collective-permute-done((bf16[64,2176]{1,0:T(8,128)(2,1)S(1)}, bf16[64,2176]{1,0:T(8,128)(2,1)S(1)}, u32[]{:S(2)}, u32[]{:S(2)}) %collective-permute-start.26) | collective-permute-done | bytes 278560 | tf_op jit(solution)/shard_map/ppermute | solution.py:172
  161.4 4.2 %collective-permute-done.12 = bf16[64,2176]{1,0:T(8,128)(2,1)S(1)} collective-permute-done((bf16[64,2176]{1,0:T(8,128)(2,1)S(1)}, bf16[64,2176]{1,0:T(8,128)(2,1)S(1)}, u32[]{:S(2)}, u32[]{:S(2)}) %collective-permute-start.12) | collective-permute-done | bytes 278560 | tf_op jit(solution)/shard_map/ppermute | solution.py:172
  165.6 0.2 add_convert_fusion
  165.9 1.6 collective-permute-start.27
  167.5 3.2 %shard_map.112 = bf16[1024,768]{1,0:T(8,128)(2,1)} custom-call(s32[2]{0:T(128)S(1)} %pad_add_fusion.ids, bf16[160,1024]{1,0:T(8,128)(2,1)S(1)} %get-tuple-element.62.refs_0_, bf16[160,1024]{1,0:T(8,128)(2,1)S(1)} %get-tuple-element.63.refs_1_, bf16[160,1024]{1,0:T(8,128)(2,1)S(1)} %get-tuple-element.64.refs_2_, ...), custom_call_target="tpu_custom_call" | custom-call | flops 1006632960 | bytes 2293768 | tf_op jit(solution)/shard_map/pallas_call | solution.py:27
  170.7 0.7 collective-permute-done.27.refs_0_
  171.4 1.8 %shard_map.111 = (bf16[32,2048]{1,0:T(8,128)(2,1)}, bf16[32,2048]{1,0:T(8,128)(2,1)}, f32[32,8]{1,0:T(8,128)S(1)}) custom-call(s32[2]{0:T(128)S(1)} %pad_add_fusion.ids, bf16[32,2176]{1,0:T(8,128)(2,1)S(1)} %slice.80.own, s32[32,8]{1,0:T(8,128)S(1)} %copy.12.idx_ref, bf16[32,2048]{1,0:T(8,128)(2,1)S(1)} %collective-permute-done.27.refs_0_), custom_call_target="tpu_custom_call" | custom-call | bytes 271368 | tf_op jit(solution)/shard_map/pallas_call | solution.py:27
  173.2 0.7 copy.14
  (33 shorter events, 0.5 us)
Async XLA Ops:
  2.2 0.9 copy-start.3
  3.1 0.9 copy-start.4
  4.8 6.7 %collective-permute-start = (bf16[32,2176]{1,0:T(8,128)(2,1)S(1)}, bf16[32,2176]{1,0:T(8,128)(2,1)S(1)}, u32[]{:S(2)}, u32[]{:S(2)}) collective-permute-start(bf16[32,2176]{1,0:T(8,128)(2,1)S(1)} %get-tuple-element.38), channel_id=1, source_target_pairs={{0,16},{16,0},{1,17},{17,1},{2,18},{18,2},{3,19},{19,3},{4,20},{20... | collective-permute-start | bytes 417800 | tf_op jit(solution)/shard_map/ppermute | solution.py:168
  11.5 40.5 %copy-start.2 = (bf16[1,1024,768]{2,1,0:T(8,128)(2,1)S(1)}, bf16[1,1024,768]{2,1,0:T(8,128)(2,1)}, u32[]{:S(2)}) copy-start(bf16[1,1024,768]{2,1,0:T(8,128)(2,1)} %param.13) | copy-start | bytes 4718596
  11.5 21.9 %collective-permute-start.20 = (bf16[64,2176]{1,0:T(8,128)(2,1)S(1)}, bf16[64,2176]{1,0:T(8,128)(2,1)S(1)}, u32[]{:S(2)}, u32[]{:S(2)}) collective-permute-start(bf16[64,2176]{1,0:T(8,128)(2,1)S(1)} %constant_dynamic-update-slice_fusion.near), channel_id=1, source_target_pairs={{0,8},{1,9},{2,10},{3,11},{4,12},{5,13},{6,14},{7,15},{8,0},{9,1},... | collective-permute-start | bytes 835592 | tf_op jit(solution)/shard_map/ppermute | solution.py:172
  14.4 20.5 %collective-permute-start.1 = (bf16[64,2176]{1,0:T(8,128)(2,1)S(1)}, bf16[64,2176]{1,0:T(8,128)(2,1)S(1)}, u32[]{:S(2)}, u32[]{:S(2)}) collective-permute-start(bf16[64,2176]{1,0:T(8,128)(2,1)S(1)} %constant_dynamic-update-slice_fusion.near), channel_id=1, source_target_pairs={{0,2},{1,3},{2,0},{3,1},{4,6},{5,7},{6,4},{7,5},{8,10},{9,11},{10,... | collective-permute-start | bytes 835592 | tf_op jit(solution)/shard_map/ppermute | solution.py:175
  15.9 19.1 %collective-permute-start.13 = (bf16[64,2176]{1,0:T(8,128)(2,1)S(1)}, bf16[64,2176]{1,0:T(8,128)(2,1)S(1)}, u32[]{:S(2)}, u32[]{:S(2)}) collective-permute-start(bf16[64,2176]{1,0:T(8,128)(2,1)S(1)} %constant_dynamic-update-slice_fusion.near), channel_id=1, source_target_pairs={{0,12},{1,13},{2,14},{3,15},{4,0},{5,1},{6,2},{7,3},{8,4},{9,5},{1... | collective-permute-start | bytes 835592 | tf_op jit(solution)/shard_map/ppermute | solution.py:172
  17.2 18.4 %collective-permute-start.6 = (bf16[64,2176]{1,0:T(8,128)(2,1)S(1)}, bf16[64,2176]{1,0:T(8,128)(2,1)S(1)}, u32[]{:S(2)}, u32[]{:S(2)}) collective-permute-start(bf16[64,2176]{1,0:T(8,128)(2,1)S(1)} %constant_dynamic-update-slice_fusion.near), channel_id=1, source_target_pairs={{0,4},{1,5},{2,6},{3,7},{4,8},{5,9},{6,10},{7,11},{8,12},{9,13},{1... | collective-permute-start | bytes 835592 | tf_op jit(solution)/shard_map/ppermute | solution.py:172
  33.4 8.4 %collective-permute-start.21 = (bf16[64,2176]{1,0:T(8,128)(2,1)S(1)}, bf16[64,2176]{1,0:T(8,128)(2,1)S(1)}, u32[]{:S(2)}, u32[]{:S(2)}) collective-permute-start(bf16[64,2176]{1,0:T(8,128)(2,1)S(1)} %collective-permute-done.20.near), channel_id=1, source_target_pairs={{0,2},{1,3},{2,0},{3,1},{4,6},{5,7},{6,4},{7,5},{8,10},{9,11},{10,... | collective-permute-start | bytes 835592 | tf_op jit(solution)/shard_map/ppermute | solution.py:175
  34.9 17.1 %collective-permute-start.2 = (bf16[128,2176]{1,0:T(8,128)(2,1)S(1)}, bf16[128,2176]{1,0:T(8,128)(2,1)S(1)}, u32[]{:S(2)}, u32[]{:S(2)}) collective-permute-start(bf16[128,2176]{1,0:T(8,128)(2,1)S(1)} %pad_maximum_fusion), channel_id=1, source_target_pairs={{0,1},{1,0},{2,3},{3,2},{4,5},{5,4},{6,7},{7,6},{8,9},{9,8},{10,11... | collective-permute-start | bytes 1671176 | tf_op jit(solution)/shard_map/ppermute | solution.py:175
  35.0 12.7 %collective-permute-start.14 = (bf16[64,2176]{1,0:T(8,128)(2,1)S(1)}, bf16[64,2176]{1,0:T(8,128)(2,1)S(1)}, u32[]{:S(2)}, u32[]{:S(2)}) collective-permute-start(bf16[64,2176]{1,0:T(8,128)(2,1)S(1)} %collective-permute-done.13.near), channel_id=1, source_target_pairs={{0,2},{1,3},{2,0},{3,1},{4,6},{5,7},{6,4},{7,5},{8,10},{9,11},{10,... | collective-permute-start | bytes 835592 | tf_op jit(solution)/shard_map/ppermute | solution.py:175
  35.6 16.2 %collective-permute-start.7 = (bf16[64,2176]{1,0:T(8,128)(2,1)S(1)}, bf16[64,2176]{1,0:T(8,128)(2,1)S(1)}, u32[]{:S(2)}, u32[]{:S(2)}) collective-permute-start(bf16[64,2176]{1,0:T(8,128)(2,1)S(1)} %collective-permute-done.6.near), channel_id=1, source_target_pairs={{0,2},{1,3},{2,0},{3,1},{4,6},{5,7},{6,4},{7,5},{8,10},{9,11},{10,... | collective-permute-start | bytes 835592 | tf_op jit(solution)/shard_map/ppermute | solution.py:175
  41.8 10.3 %copy-start.1 = (bf16[1,1024,768]{2,1,0:T(8,128)(2,1)S(1)}, bf16[1,1024,768]{2,1,0:T(8,128)(2,1)}, u32[]{:S(2)}) copy-start(bf16[1,1024,768]{2,1,0:T(8,128)(2,1)} %param.12) | copy-start | bytes 4718596
  41.8 10.2 %copy-start = (bf16[1,1024,768]{2,1,0:T(8,128)(2,1)S(1)}, bf16[1,1024,768]{2,1,0:T(8,128)(2,1)}, u32[]{:S(2)}) copy-start(bf16[1,1024,768]{2,1,0:T(8,128)(2,1)} %param.11) | copy-start | bytes 4718596
  41.8 13.7 %collective-permute-start.22 = (bf16[128,2176]{1,0:T(8,128)(2,1)S(1)}, bf16[128,2176]{1,0:T(8,128)(2,1)S(1)}, u32[]{:S(2)}, u32[]{:S(2)}) collective-permute-start(bf16[128,2176]{1,0:T(8,128)(2,1)S(1)} %pad_maximum_fusion.3), channel_id=1, source_target_pairs={{0,1},{1,0},{2,3},{3,2},{4,5},{5,4},{6,7},{7,6},{8,9},{9,8},{10,11... | collective-permute-start | bytes 1671176 | tf_op jit(solution)/shard_map/ppermute | solution.py:175
  47.8 10.3 %collective-permute-start.15 = (bf16[128,2176]{1,0:T(8,128)(2,1)S(1)}, bf16[128,2176]{1,0:T(8,128)(2,1)S(1)}, u32[]{:S(2)}, u32[]{:S(2)}) collective-permute-start(bf16[128,2176]{1,0:T(8,128)(2,1)S(1)} %pad_maximum_fusion.2), channel_id=1, source_target_pairs={{0,1},{1,0},{2,3},{3,2},{4,5},{5,4},{6,7},{7,6},{8,9},{9,8},{10,11... | collective-permute-start | bytes 1671176 | tf_op jit(solution)/shard_map/ppermute | solution.py:175
  51.9 9.7 %collective-permute-start.8 = (bf16[128,2176]{1,0:T(8,128)(2,1)S(1)}, bf16[128,2176]{1,0:T(8,128)(2,1)S(1)}, u32[]{:S(2)}, u32[]{:S(2)}) collective-permute-start(bf16[128,2176]{1,0:T(8,128)(2,1)S(1)} %pad_maximum_fusion.1), channel_id=1, source_target_pairs={{0,1},{1,0},{2,3},{3,2},{4,5},{5,4},{6,7},{7,6},{8,9},{9,8},{10,11... | collective-permute-start | bytes 1671176 | tf_op jit(solution)/shard_map/ppermute | solution.py:175
  54.0 19.4 %collective-permute-start.3 = (bf16[160,2304]{1,0:T(8,128)(2,1)S(1)}, bf16[160,2304]{1,0:T(8,128)(2,1)S(1)}, u32[]{:S(2)}, u32[]{:S(2)}) collective-permute-start(bf16[160,2304]{1,0:T(8,128)(2,1)S(1)} %get-tuple-element.39.refs_0_), channel_id=1, source_target_pairs={{0,16},{16,0},{1,17},{17,1},{2,18},{18,2},{3,19},{19,3},{4,20},{20... | collective-permute-start | bytes 2211848 | tf_op jit(solution)/shard_map/ppermute | solution.py:168
  57.5 31.6 %collective-permute-start.23 = (bf16[160,2304]{1,0:T(8,128)(2,1)S(1)}, bf16[160,2304]{1,0:T(8,128)(2,1)S(1)}, u32[]{:S(2)}, u32[]{:S(2)}) collective-permute-start(bf16[160,2304]{1,0:T(8,128)(2,1)S(1)} %get-tuple-element.54.refs_0_), channel_id=1, source_target_pairs={{0,16},{16,0},{1,17},{17,1},{2,18},{18,2},{3,19},{19,3},{4,20},{20... | collective-permute-start | bytes 2211848 | tf_op jit(solution)/shard_map/ppermute | solution.py:168
  60.0 44.9 %collective-permute-start.16 = (bf16[160,2304]{1,0:T(8,128)(2,1)S(1)}, bf16[160,2304]{1,0:T(8,128)(2,1)S(1)}, u32[]{:S(2)}, u32[]{:S(2)}) collective-permute-start(bf16[160,2304]{1,0:T(8,128)(2,1)S(1)} %get-tuple-element.49.refs_0_), channel_id=1, source_target_pairs={{0,16},{16,0},{1,17},{17,1},{2,18},{18,2},{3,19},{19,3},{4,20},{20... | collective-permute-start | bytes 2211848 | tf_op jit(solution)/shard_map/ppermute | solution.py:168
  63.5 56.8 %collective-permute-start.9 = (bf16[160,2304]{1,0:T(8,128)(2,1)S(1)}, bf16[160,2304]{1,0:T(8,128)(2,1)S(1)}, u32[]{:S(2)}, u32[]{:S(2)}) collective-permute-start(bf16[160,2304]{1,0:T(8,128)(2,1)S(1)} %get-tuple-element.44.refs_0_), channel_id=1, source_target_pairs={{0,16},{16,0},{1,17},{17,1},{2,18},{18,2},{3,19},{19,3},{4,20},{20... | collective-permute-start | bytes 2211848 | tf_op jit(solution)/shard_map/ppermute | solution.py:168
  76.0 47.3 %collective-permute-start.4 = (bf16[128,2176]{1,0:T(8,128)(2,1)S(1)}, bf16[128,2176]{1,0:T(8,128)(2,1)S(1)}, u32[]{:S(2)}, u32[]{:S(2)}) collective-permute-start(bf16[128,2176]{1,0:T(8,128)(2,1)S(1)} %get-tuple-element.43), channel_id=1, source_target_pairs={{0,1},{1,0},{2,3},{3,2},{4,5},{5,4},{6,7},{7,6},{8,9},{9,8},{10,11... | collective-permute-start | bytes 1671176 | tf_op jit(solution)/shard_map/ppermute | solution.py:175
  91.8 33.1 %collective-permute-start.24 = (bf16[128,2176]{1,0:T(8,128)(2,1)S(1)}, bf16[128,2176]{1,0:T(8,128)(2,1)S(1)}, u32[]{:S(2)}, u32[]{:S(2)}) collective-permute-start(bf16[128,2176]{1,0:T(8,128)(2,1)S(1)} %get-tuple-element.58), channel_id=1, source_target_pairs={{0,1},{1,0},{2,3},{3,2},{4,5},{5,4},{6,7},{7,6},{8,9},{9,8},{10,11... | collective-permute-start | bytes 1671176 | tf_op jit(solution)/shard_map/ppermute | solution.py:175
  107.6 18.0 %collective-permute-start.17 = (bf16[128,2176]{1,0:T(8,128)(2,1)S(1)}, bf16[128,2176]{1,0:T(8,128)(2,1)S(1)}, u32[]{:S(2)}, u32[]{:S(2)}) collective-permute-start(bf16[128,2176]{1,0:T(8,128)(2,1)S(1)} %get-tuple-element.53), channel_id=1, source_target_pairs={{0,1},{1,0},{2,3},{3,2},{4,5},{5,4},{6,7},{7,6},{8,9},{9,8},{10,11... | collective-permute-start | bytes 1671176 | tf_op jit(solution)/shard_map/ppermute | solution.py:175
  123.1 4.0 %collective-permute-start.10 = (bf16[128,2176]{1,0:T(8,128)(2,1)S(1)}, bf16[128,2176]{1,0:T(8,128)(2,1)S(1)}, u32[]{:S(2)}, u32[]{:S(2)}) collective-permute-start(bf16[128,2176]{1,0:T(8,128)(2,1)S(1)} %get-tuple-element.48), channel_id=1, source_target_pairs={{0,1},{1,0},{2,3},{3,2},{4,5},{5,4},{6,7},{7,6},{8,9},{9,8},{10,11... | collective-permute-start | bytes 1671176 | tf_op jit(solution)/shard_map/ppermute | solution.py:175
  123.3 31.5 %collective-permute-start.5 = (bf16[64,2176]{1,0:T(8,128)(2,1)S(1)}, bf16[64,2176]{1,0:T(8,128)(2,1)S(1)}, u32[]{:S(2)}, u32[]{:S(2)}) collective-permute-start(bf16[64,2176]{1,0:T(8,128)(2,1)S(1)} %add_convert_fusion.11), channel_id=1, source_target_pairs={{0,2},{1,3},{2,0},{3,1},{4,6},{5,7},{6,4},{7,5},{8,10},{9,11},{10,... | collective-permute-start | bytes 835592 | tf_op jit(solution)/shard_map/ppermute | solution.py:175
  124.9 13.9 %collective-permute-start.25 = (bf16[64,2176]{1,0:T(8,128)(2,1)S(1)}, bf16[64,2176]{1,0:T(8,128)(2,1)S(1)}, u32[]{:S(2)}, u32[]{:S(2)}) collective-permute-start(bf16[64,2176]{1,0:T(8,128)(2,1)S(1)} %add_convert_fusion.2), channel_id=1, source_target_pairs={{0,2},{1,3},{2,0},{3,1},{4,6},{5,7},{6,4},{7,5},{8,10},{9,11},{10,... | collective-permute-start | bytes 835592 | tf_op jit(solution)/shard_map/ppermute | solution.py:175
  125.6 19.1 %collective-permute-start.18 = (bf16[64,2176]{1,0:T(8,128)(2,1)S(1)}, bf16[64,2176]{1,0:T(8,128)(2,1)S(1)}, u32[]{:S(2)}, u32[]{:S(2)}) collective-permute-start(bf16[64,2176]{1,0:T(8,128)(2,1)S(1)} %add_convert_fusion.5), channel_id=1, source_target_pairs={{0,2},{1,3},{2,0},{3,1},{4,6},{5,7},{6,4},{7,5},{8,10},{9,11},{10,... | collective-permute-start | bytes 835592 | tf_op jit(solution)/shard_map/ppermute | solution.py:175
  127.2 23.1 %collective-permute-start.11 = (bf16[64,2176]{1,0:T(8,128)(2,1)S(1)}, bf16[64,2176]{1,0:T(8,128)(2,1)S(1)}, u32[]{:S(2)}, u32[]{:S(2)}) collective-permute-start(bf16[64,2176]{1,0:T(8,128)(2,1)S(1)} %add_convert_fusion.8), channel_id=1, source_target_pairs={{0,2},{1,3},{2,0},{3,1},{4,6},{5,7},{6,4},{7,5},{8,10},{9,11},{10,... | collective-permute-start | bytes 835592 | tf_op jit(solution)/shard_map/ppermute | solution.py:175
  138.9 22.5 %collective-permute-start.26 = (bf16[64,2176]{1,0:T(8,128)(2,1)S(1)}, bf16[64,2176]{1,0:T(8,128)(2,1)S(1)}, u32[]{:S(2)}, u32[]{:S(2)}) collective-permute-start(bf16[64,2176]{1,0:T(8,128)(2,1)S(1)} %add_convert_fusion.1), channel_id=1, source_target_pairs={{0,8},{1,9},{2,10},{3,11},{4,12},{5,13},{6,14},{7,15},{8,0},{9,1},... | collective-permute-start | bytes 835592 | tf_op jit(solution)/shard_map/ppermute | solution.py:172
  144.9 16.6 %collective-permute-start.19 = (bf16[64,2176]{1,0:T(8,128)(2,1)S(1)}, bf16[64,2176]{1,0:T(8,128)(2,1)S(1)}, u32[]{:S(2)}, u32[]{:S(2)}) collective-permute-start(bf16[64,2176]{1,0:T(8,128)(2,1)S(1)} %add_convert_fusion.4), channel_id=1, source_target_pairs={{0,4},{1,5},{2,6},{3,7},{4,8},{5,9},{6,10},{7,11},{8,12},{9,13},{1... | collective-permute-start | bytes 835592 | tf_op jit(solution)/shard_map/ppermute | solution.py:172
  150.4 15.2 %collective-permute-start.12 = (bf16[64,2176]{1,0:T(8,128)(2,1)S(1)}, bf16[64,2176]{1,0:T(8,128)(2,1)S(1)}, u32[]{:S(2)}, u32[]{:S(2)}) collective-permute-start(bf16[64,2176]{1,0:T(8,128)(2,1)S(1)} %add_convert_fusion.7), channel_id=1, source_target_pairs={{0,12},{1,13},{2,14},{3,15},{4,0},{5,1},{6,2},{7,3},{8,4},{9,5},{1... | collective-permute-start | bytes 835592 | tf_op jit(solution)/shard_map/ppermute | solution.py:172
  165.9 5.5 %collective-permute-start.27 = (bf16[32,2048]{1,0:T(8,128)(2,1)S(1)}, bf16[32,2048]{1,0:T(8,128)(2,1)S(1)}, u32[]{:S(2)}, u32[]{:S(2)}) collective-permute-start(bf16[32,2048]{1,0:T(8,128)(2,1)S(1)} %slice.81), channel_id=1, source_target_pairs={{0,16},{16,0},{1,17},{17,1},{2,18},{18,2},{3,19},{19,3},{4,20},{20... | collective-permute-start | bytes 393224 | tf_op jit(solution)/shard_map/ppermute | solution.py:168

commit v2 on v1

--- a/solution.py
+++ b/solution.py
@@ -11,9 +11,13 @@
 F32 = jnp.float32
 LANES = 128
 CORE, SIDE = 2, 2
+PIECE_ROWS, PIECE_COLS = 2, 2
+PIECES = PIECE_ROWS * PIECE_COLS
+WINDOW = 2
 VMEM = pl.BlockSpec(memory_space=pltpu.VMEM)
 SMEM = pl.BlockSpec(memory_space=pltpu.SMEM)
 PARAMS = pltpu.CompilerParams(vmem_limit_bytes=32 * 1024 * 1024)
+WIDE = pltpu.CompilerParams(vmem_limit_bytes=60 * 1024 * 1024)
 
 
 def dot_of(left, right, left_dim, right_dim):
@@ -22,39 +26,59 @@
     )
 
 
-def call(body, out_shapes, args, flops=0):
-    moved = sum(a.size * a.dtype.itemsize for a in args)
+def call(body, out_shapes, args, far=(), copies=0, flops=0, params=PARAMS):
+    moved = sum(a.size * a.dtype.itemsize for a in (*args, *far))
     return pl.pallas_call(
         body,
         out_shape=[jax.ShapeDtypeStruct(s, t) for s, t in out_shapes],
-        in_specs=[SMEM] + [VMEM] * (len(args) - 1),
+        in_specs=[SMEM] + [VMEM] * (len(args) - 1) + [pl.BlockSpec(memory_space=pltpu.HBM)] * len(far),
         out_specs=[VMEM] * len(out_shapes),
-        compiler_params=PARAMS,
+        scratch_shapes=[pltpu.SemaphoreType.DMA((copies,))] if copies else [],
+        compiler_params=params,
         cost_estimate=pl.CostEstimate(flops=flops, bytes_accessed=moved, transcendentals=0),
-    )(*args)
-
-
-def pack_kernel(n_dp, n_experts, half, ids, tok_ref, up_ref, rw_ref, idx_ref, *outs):
-    rows, top = idx_ref.shape
+    )(*args, *far)
+
+
+def pack_kernel(n_dp, n_experts, half, ids, rw_ref, idx_ref, tok_ref, up_ref, *refs):
+    outs, sem = refs[:-1], refs[-1]
+    copies = []
+    for s, out in enumerate(outs):
+        owner = lax.rem(ids[0] + s, n_dp)
+        at = pl.ds(pl.multiple_of(owner * half, LANES), half)
+        for which, source in enumerate((tok_ref, up_ref)):
+            target = out.at[:, which * half : (which + 1) * half]
+            copies.append(pltpu.make_async_copy(source.at[:, at], target, sem.at[2 * s + which]))
+    for copy in copies:
+        copy.start()
+    top, rows = idx_ref.shape
     extra = outs[0].shape[1] - 2 * half
-    lane = lax.broadcasted_iota(jnp.int32, (rows, extra), 1)
-    high_at, low_at = jnp.zeros((rows, extra), F32), jnp.zeros((rows, extra), F32)
+    lane = lax.broadcasted_iota(jnp.int32, (extra, rows), 0)
+    high_at, low_at = jnp.zeros((extra, rows), F32), jnp.zeros((extra, rows), F32)
     for k in range(top):
-        named = idx_ref[:, k : k + 1]
-        weight = rw_ref[:, k : k + 1]
+        named = idx_ref[k : k + 1, :]
+        weight = rw_ref[k : k + 1, :]
         high_at = jnp.where(lane == named, weight, high_at)
         low_at = jnp.where(lane == named + n_experts, weight, low_at)
     low_at = low_at - low_at.astype(BF16).astype(F32)
-    routing = (high_at + low_at).astype(BF16)
-    for s, out in enumerate(outs):
-        owner = lax.rem(ids[0] + s, n_dp)
-        at = pl.ds(pl.multiple_of(owner * half, LANES), half)
-        out[:, :half] = tok_ref[:, at]
-        out[:, half : 2 * half] = up_ref[:, at]
-        out[:, 2 * half :] = routing
-
-
-def forward_kernel(n_dp, n_experts, tok, cap, ids, near, side, core, wg, wu, wd, part, up_rows, sel, weight):
+    same = lax.broadcasted_iota(jnp.int32, (extra, extra), 0) == lax.broadcasted_iota(jnp.int32, (extra, extra), 1)
+    turned = dot_of((high_at + low_at).astype(BF16), jnp.where(same, 1.0, 0.0).astype(BF16), 0, 0)
+    for out in outs:
+        out[:, 2 * half :] = turned.astype(BF16)
+    for copy in copies:
+        copy.wait()
+
+
+def load_kernel(ids, *refs):
+    sources, outs, sem = refs[:3], refs[3:6], refs[6]
+    copies = [pltpu.make_async_copy(source, out, sem.at[i]) for i, (source, out) in enumerate(zip(sources, outs))]
+    for copy in copies:
+        copy.start()
+    for copy in copies:
+        copy.wait()
+
+
+def forward_kernel(n_dp, n_experts, tok, cap, ids, near, side, core, wg, wu, wd, *outs):
+    *pieces, up_rows, sel, weight = outs
     half, ff = wg.shape
     data = jnp.concatenate([near[...], side[...], core[...]], axis=0)
     total, rows = data.shape[0], sel.shape[0]
@@ -80,18 +104,24 @@
     tok_rows = dot_of(chooser, data[:, :half], 1, 0).astype(BF16)
     grad_rows = dot_of(chooser, data[:, half : 2 * half], 1, 0).astype(BF16)
     up_rows[...] = grad_rows
-    part[:, :ff] = dot_of(tok_rows, wg[...], 1, 0).astype(BF16)
-    part[:, ff : 2 * ff] = dot_of(tok_rows, wu[...], 1, 0).astype(BF16)
-    part[:, 2 * ff :] = dot_of(grad_rows, wd[...], 1, 0).astype(BF16)
+    sums = [
+        dot_of(left, right[...], 1, 0).astype(BF16)
+        for left, right in ((tok_rows, wg), (tok_rows, wu), (grad_rows, wd))
+    ]
+    part = jnp.concatenate(sums, axis=1)
+    deep, wide = pieces[0].shape
+    for at, piece in enumerate(pieces):
+        r, c = divmod(at, 3 * ff // wide)
+        piece[...] = part[r * deep : (r + 1) * deep, c * wide : (c + 1) * wide]
 
 
 def backward_kernel(n_experts, n_parts, ids, *refs):
-    parts = refs[:n_parts]
-    sel, weight, wg, wu, wd, keep, send, hidden_rows = refs[n_parts:]
+    sel, weight, wg, wu, wd, keep, send, hidden_rows = refs[PIECES * n_parts :]
     half, ff = wg.shape
-    whole = parts[0][...].astype(F32)
-    for other in parts[1:]:
-        whole = whole + other[...].astype(F32)
+    pieces = [sum(ref[...].astype(F32) for ref in refs[at * n_parts : (at + 1) * n_parts]) for at in range(PIECES)]
+    whole = jnp.concatenate(
+        [jnp.concatenate(pieces[at : at + PIECE_COLS], axis=1) for at in range(0, PIECES, PIECE_COLS)], axis=0
+    )
     gate, up, grad = whole[:, :ff], whole[:, ff : 2 * ff], whole[:, 2 * ff :]
     w_col = weight[:, :1]
     sig = 1.0 / (1.0 + jnp.exp(-gate))
@@ -132,17 +162,20 @@
         source = own if s == 0 else others[s - 1]
         comb[:, at] = source[:, :half]
         grad[:, at] = source[:, half : 2 * half]
-    columns = own[:, 2 * half :].astype(F32)
-    lane = lax.broadcasted_iota(jnp.int32, columns.shape, 1)
-    rows, top = route.shape
-    slot = lax.broadcasted_iota(jnp.int32, (rows, top), 1)
-    result = jnp.zeros((rows, top), F32)
+    columns = own[:, 2 * half :]
+    extra = columns.shape[1]
+    same = lax.broadcasted_iota(jnp.int32, (extra, extra), 0) == lax.broadcasted_iota(jnp.int32, (extra, extra), 1)
+    turned = dot_of(jnp.where(same, 1.0, 0.0).astype(BF16), columns, 1, 1)
+    lane = lax.broadcasted_iota(jnp.int32, turned.shape, 0)
+    top = route.shape[0]
     for k in range(top):
-        named = idx_ref[:, k : k + 1]
+        named = idx_ref[k : k + 1, :]
         mine = (lane == named) | (lane == named + n_experts)
-        value = jnp.sum(jnp.where(mine, columns, 0.0), axis=1, keepdims=True)
-        result = jnp.where(slot == k, value, result)
-    route[...] = result
+        route[k : k + 1, :] = jnp.sum(jnp.where(mine, turned, 0.0), axis=0, keepdims=True)
+
+
+def after(x, *earlier):
+    return lax.optimization_barrier((x, *earlier))[0]
 
 
 def added(left, right):
@@ -174,68 +207,88 @@
     def swap(x, bit):
         return lax.ppermute(x, "expert", [(i, i ^ bit) for i in range(n_experts)])
 
+    index_rows = expert_index.T
     blocks = call(
         functools.partial(pack_kernel, n_dp, n_experts, half),
         [((tok, wide), BF16)] * n_dp,
-        (ids, tokens, upstream, route_weight, expert_index),
+        (ids, route_weight.T, index_rows),
+        far=(tokens, upstream),
+        copies=2 * n_dp,
+        params=WIDE,
     )
     mine = jnp.concatenate([blocks[0]] + [dp_shift(blocks[s], s) for s in range(1, n_dp)], axis=0)
-
-    order = [0]
-    for k in range(1, layers // 2 + 1):
-        order += [k] if 2 * k == layers else [k, layers - k]
-    order = order[:layers]
-
-    near = {k: mine if k == 0 else layer_shift(mine, k) for k in order}
-    parts, kept = {}, {}
-    for k in order:
-        side = swap(near[k], CORE)
-        core = swap(jnp.concatenate([near[k], side], axis=0), 1)
-        part, up_rows, sel, weight = call(
+    wg, wu, wd = call(load_kernel, [((half, ff), BF16)] * 3, (ids,), far=(wg, wu, wd), copies=3)
+
+    near, sides, parts, kept, crossed = [mine], [], [], [], []
+    hidden_rows, partials, homes = [], [], []
+    order = [k for k in (0, 2, 1, 3) if k < layers] + list(range(4, layers))
+
+    def over_dp(part):
+        if len(crossed) >= WINDOW:
+            part = after(part, crossed[-WINDOW])
+        others = [dp_shift(part, s) for s in range(1, n_dp)]
+        crossed.extend(others[-1:])
+        return [part] + others
+
+    def forward(i):
+        sides.append(swap(near[i], CORE))
+        both = jnp.concatenate([near[i], sides[i]], axis=0)
+        if i + 1 < layers:
+            near.append(layer_shift(after(mine, near[i]) if i else mine, order[i + 1]))
+        if i == 0:
+            both = after(both, wg, wu, wd)
+        core = swap(both, 1)
+        *pieces, up_rows, sel, weight = call(
             functools.partial(forward_kernel, n_dp, n_experts, tok, cap),
             [
-                ((rows, 3 * ff), BF16),
+                *[((rows // PIECE_ROWS, 3 * ff // PIECE_COLS), BF16)] * PIECES,
                 ((rows, half), BF16),
                 ((rows, total), BF16),
                 ((rows, LANES), F32),
             ],
-            (ids, near[k], side, core, wg, wu, wd),
+            (ids, near[i], sides[i], core, wg, wu, wd),
             flops=2 * rows * half * 3 * ff + 4 * rows * total * half,
         )
-        parts[k] = [part] + [dp_shift(part, s) for s in range(1, n_dp)]
-        kept[k] = (up_rows, sel, weight)
-
-    hidden_rows, sums = {}, {}
-    for k in order:
-        up_rows, sel, weight = kept[k]
-        keep, send, hidden_rows[k] = call(
+        kept.append((up_rows, sel, weight))
+        if i >= 3:
+            pieces = [after(piece, partials[i - 3]) for piece in pieces]
+        parts.append(sum([over_dp(piece) for piece in pieces], []))
+
+    def backward(i):
+        up_rows, sel, weight = kept[i]
+        keep, send, hidden = call(
             functools.partial(backward_kernel, n_experts, n_dp),
             [((total // 2, wide), BF16), ((total // 2, wide), BF16), ((rows, ff), BF16)],
-            (ids, *parts[k], sel, weight, wg, wu, wd),
+            (ids, *parts[i], sel, weight, wg, wu, wd),
             flops=2 * total * half * 3 * ff + 2 * rows * total * 3 * ff,
         )
+        hidden_rows.append(hidden)
         back = swap(send, 1)
         outward = swap(added(keep[group:], back[group:]), CORE)
-        partial = added(added(keep[:group], back[:group]), outward)
-        sums[k] = partial if k == 0 else layer_shift(partial, -k)
+        partials.append(added(added(keep[:group], back[:group]), outward))
+        homes.append(layer_shift(partials[i], -order[i]) if order[i] else partials[i])
+
+    for i in range(layers + 2):
+        if i >= 2:
+            backward(i - 2)
+        if i < layers:
+            forward(i)
 
     (down_grad,) = call(
         functools.partial(down_kernel, layers),
         [((half, ff), BF16)],
-        (ids, *[kept[k][0] for k in order], *[hidden_rows[k] for k in order]),
+        (ids, *[rows_of[0] for rows_of in kept], *hidden_rows),
         flops=2 * layers * rows * half * ff,
     )
-    result = sums[0].astype(F32)
-    for k in order[1:]:
-        result = result + sums[k].astype(F32)
+    result = sum(partial.astype(F32) for partial in homes)
     result = result.astype(BF16)
     others = [dp_shift(result[s * tok : (s + 1) * tok, : 2 * half], -s) for s in range(1, n_dp)]
     combined, token_grad, route_grad = call(
         functools.partial(final_kernel, n_dp, n_experts, half),
-        [((tok, width), BF16), ((tok, width), BF16), ((tok, top), F32)],
-        (ids, result[:tok], expert_index, *others),
-    )
-    return (combined, token_grad, route_grad, down_grad[None])
+        [((tok, width), BF16), ((tok, width), BF16), ((top, tok), F32)],
+        (ids, result[:tok], index_rows, *others),
+    )
+    return (combined, token_grad, route_grad.T, down_grad[None])
 
 
 def solution(mesh):

time: 174 us -> 146 us (0.84)
  waiting for transfers between devices: 114 us -> 72 us
  starting transfers between devices: 29.8 us -> 38.8 us
  Pallas kernels: 24.2 us -> 26.2 us
  local copies, waits for them, and re-layouts: 4.05 us -> 5.84 us
    ppermute x6 -> x18, waiting for transfers between devices: 52.4 us -> 28.2 us  [dp_shift(): return lax.ppermute(x, 'dp', [(i, (i + s) % n_dp) for i in range(n_dp)])]
    ppermute x6 -> x18, starting transfers between devices: 8.94 us -> 23.1 us  [dp_shift(): return lax.ppermute(x, 'dp', [(i, (i + s) % n_dp) for i in range(n_dp)])]
    ppermute x16, waiting for transfers between devices: 35.2 us -> 21.1 us  [swap(): return lax.ppermute(x, 'expert', [(i, i ^ bit) for i in range(n_experts)])]
    ppermute x6, starting transfers between devices: 10.9 us -> 5.66 us  [layer_shift(): lax.ppermute(x, 'expert', [(i, (i + step) % n_experts) for i in range(n_e...]
    ppermute x6, waiting for transfers between devices: 26.3 us -> 22.6 us  [layer_shift(): lax.ppermute(x, 'expert', [(i, (i + step) % n_experts) for i in range(n_e...]
    pallas_call x11 -> x12, Pallas kernels: 24.2 us -> 26.2 us  [call(): pl.pallas_call(body, out_shape=[jax.ShapeDtypeStruct(s, t) for s, t in ou...]
    unnamed x14 -> x13, local copies, waits for them, and re-layouts: 4.02 us -> 5.8 us
  transfers between devices with their start and end apart: 28 -> 40, of which waited for: 15 -> 23; matrix products, arithmetic and copies ran while one was open for 0% -> 1% of each run, Pallas kernels for 12% -> 15%
where the time goes in v2:
time: 146 us
  waiting for transfers between devices  72 us (49%)
  starting transfers between devices  38.8 us (27%)
  Pallas kernels  26.2 us (18%)
  local copies, waits for them, and re-layouts  5.84 us (4%)
  other arithmetic  1.77 us (1%)
    ppermute x18, waiting for transfers between devices, dp_shift(): return lax.ppermute(x, 'dp', [(i, (i + s) % n_dp) for i in range(n_dp)])  28.2 us
    pallas_call x12, Pallas kernels, call(): pl.pallas_call(body, out_shape=[jax.ShapeDtypeStruct(s, t) for s, t in ou...  26.2 us
    ppermute x18, starting transfers between devices, dp_shift(): return lax.ppermute(x, 'dp', [(i, (i + s) % n_dp) for i in range(n_dp)])  23.1 us
    ppermute x6, waiting for transfers between devices, layer_shift(): lax.ppermute(x, 'expert', [(i, (i + step) % n_experts) for i in range(n_e...  22.6 us
    ppermute x16, waiting for transfers between devices, swap(): return lax.ppermute(x, 'expert', [(i, i ^ bit) for i in range(n_experts)])  21.1 us
    ppermute x16, starting transfers between devices, swap(): return lax.ppermute(x, 'expert', [(i, i ^ bit) for i in range(n_experts)])  10 us
    unnamed x13, local copies, waits for them, and re-layouts  5.8 us
    ppermute x6, starting transfers between devices, layer_shift(): lax.ppermute(x, 'expert', [(i, (i + step) % n_experts) for i in range(n_e...  5.66 us
  transfers between devices with their start and end apart: 40, of which 23 were waited for; matrix products, arithmetic and copies ran while one was open for 1% of the time, Pallas kernels for 15%

profile of v2, /device:TPU:0, one launch (start us, length us, event | category | flops | bytes accessed | tf_op | source)
XLA Modules:
  0.0 145.5 jit_solution(603196802454227203)
XLA Ops:
  0.6 0.6 pad_add_fusion.ids
  1.2 2.4 %shard_map.102 = (bf16[32,2176]{1,0:T(8,128)(2,1)}, bf16[32,2176]{1,0:T(8,128)(2,1)}) custom-call(s32[2]{0:T(128)} %pad_add_fusion.ids, f32[8,32]{1,0:T(8,128)} %bitcast.15, s32[8,32]{1,0:T(8,128)} %bitcast.12, bf16[32,2048]{1,0:T(8,128)(2,1)} %tok_ref.1, bf16[32,2048]{1,0:T(8,128)(2,1)} %up_ref.1), custom_call_target="tpu_custom_call" | custom-call | bytes 264200 | tf_op jit(solution)/shard_map/pallas_call | solution.py:31
  3.6 3.0 %collective-permute-start = (bf16[32,2176]{1,0:T(8,128)(2,1)}, bf16[32,2176]{1,0:T(8,128)(2,1)S(1)}, u32[]{:S(2)}, u32[]{:S(2)}) collective-permute-start(bf16[32,2176]{1,0:T(8,128)(2,1)} %get-tuple-element.74), channel_id=1, source_target_pairs={{0,16},{16,0},{1,17},{17,1},{2,18},{18,2},{3,19},{19,3},{4,20},{20... | collective-permute-start | bytes 417800 | tf_op jit(solution)/shard_map/ppermute | solution.py:201
  6.7 0.9 constant_dynamic-update-slice_fusion.1
  7.6 3.0 %collective-permute-done = bf16[32,2176]{1,0:T(8,128)(2,1)S(1)} collective-permute-done((bf16[32,2176]{1,0:T(8,128)(2,1)}, bf16[32,2176]{1,0:T(8,128)(2,1)S(1)}, u32[]{:S(2)}, u32[]{:S(2)}) %collective-permute-start) | collective-permute-done | bytes 139296 | tf_op jit(solution)/shard_map/ppermute | solution.py:201
  10.6 2.9 %collective-permute-start.9 = (bf16[64,2176]{1,0:T(8,128)(2,1)S(1)}, bf16[64,2176]{1,0:T(8,128)(2,1)S(1)}, u32[]{:S(2)}, u32[]{:S(2)}) collective-permute-start(bf16[64,2176]{1,0:T(8,128)(2,1)S(1)} %constant_dynamic-update-slice_fusion.near), channel_id=1, source_target_pairs={{0,8},{1,9},{2,10},{3,11},{4,12},{5,13},{6,14},{7,15},{8,0},{9,1},... | collective-permute-start | bytes 835592 | tf_op jit(solution)/shard_map/ppermute | solution.py:205
  13.4 1.5 %collective-permute-start.1 = (bf16[64,2176]{1,0:T(8,128)(2,1)S(1)}, bf16[64,2176]{1,0:T(8,128)(2,1)S(1)}, u32[]{:S(2)}, u32[]{:S(2)}) collective-permute-start(bf16[64,2176]{1,0:T(8,128)(2,1)S(1)} %constant_dynamic-update-slice_fusion.near), channel_id=1, source_target_pairs={{0,2},{1,3},{2,0},{3,1},{4,6},{5,7},{6,4},{7,5},{8,10},{9,11},{10,... | collective-permute-start | bytes 835592 | tf_op jit(solution)/shard_map/ppermute | solution.py:208
  14.9 1.4 copy-done
  16.3 1.4 copy-done.1
  17.7 1.4 copy-done.2
  19.1 0.7 copy-done.3
  19.8 0.9 shard_map.103
  20.7 4.6 %collective-permute-done.9.near = bf16[64,2176]{1,0:T(8,128)(2,1)S(1)} collective-permute-done((bf16[64,2176]{1,0:T(8,128)(2,1)S(1)}, bf16[64,2176]{1,0:T(8,128)(2,1)S(1)}, u32[]{:S(2)}, u32[]{:S(2)}) %collective-permute-start.9) | collective-permute-done | bytes 278560 | tf_op jit(solution)/shard_map/ppermute | solution.py:205
  25.3 0.6 collective-permute-start.19
  25.9 1.5 %collective-permute-start.10 = (bf16[64,2176]{1,0:T(8,128)(2,1)S(1)}, bf16[64,2176]{1,0:T(8,128)(2,1)S(1)}, u32[]{:S(2)}, u32[]{:S(2)}) collective-permute-start(bf16[64,2176]{1,0:T(8,128)(2,1)S(1)} %collective-permute-done.9.near), channel_id=1, source_target_pairs={{0,2},{1,3},{2,0},{3,1},{4,6},{5,7},{6,4},{7,5},{8,10},{9,11},{10,... | collective-permute-start | bytes 835592 | tf_op jit(solution)/shard_map/ppermute | solution.py:208
  27.5 8.0 %collective-permute-done.19.near = bf16[64,2176]{1,0:T(8,128)(2,1)S(1)} collective-permute-done((bf16[64,2176]{1,0:T(8,128)(2,1)S(1)}, bf16[64,2176]{1,0:T(8,128)(2,1)S(1)}, u32[]{:S(2)}, u32[]{:S(2)}) %collective-permute-start.19) | collective-permute-done | bytes 278560 | tf_op jit(solution)/shard_map/ppermute | solution.py:205
  35.6 1.7 %collective-permute-start.29 = (bf16[64,2176]{1,0:T(8,128)(2,1)S(1)}, bf16[64,2176]{1,0:T(8,128)(2,1)S(1)}, u32[]{:S(2)}, u32[]{:S(2)}) collective-permute-start(bf16[64,2176]{1,0:T(8,128)(2,1)S(1)} %constant_dynamic-update-slice_fusion.near), channel_id=1, source_target_pairs={{0,12},{1,13},{2,14},{3,15},{4,0},{5,1},{6,2},{7,3},{8,4},{9,5},{1... | collective-permute-start | bytes 835592 | tf_op jit(solution)/shard_map/ppermute | solution.py:205
  37.3 1.5 %collective-permute-start.20 = (bf16[64,2176]{1,0:T(8,128)(2,1)S(1)}, bf16[64,2176]{1,0:T(8,128)(2,1)S(1)}, u32[]{:S(2)}, u32[]{:S(2)}) collective-permute-start(bf16[64,2176]{1,0:T(8,128)(2,1)S(1)} %collective-permute-done.19.near), channel_id=1, source_target_pairs={{0,2},{1,3},{2,0},{3,1},{4,6},{5,7},{6,4},{7,5},{8,10},{9,11},{10,... | collective-permute-start | bytes 835592 | tf_op jit(solution)/shard_map/ppermute | solution.py:208
  38.9 1.9 %shard_map.104 = (bf16[80,1152]{1,0:T(8,128)(2,1)S(1)}, bf16[80,1152]{1,0:T(8,128)(2,1)S(1)}, bf16[80,1152]{1,0:T(8,128)(2,1)S(1)}, bf16[80,1152]{1,0:T(8,128)(2...) custom-call(s32[2]{0:T(128)S(1)} %copy-done.3, ...), custom_call_target="tpu_custom_call" | custom-call | flops 922746880 | bytes 5832712 | tf_op jit(solution)/shard_map/pallas_call | solution.py:31
  40.9 1.6 %collective-permute-start.4 = (bf16[80,1152]{1,0:T(8,128)(2,1)S(1)}, bf16[80,1152]{1,0:T(8,128)(2,1)S(1)}, u32[]{:S(2)}, u32[]{:S(2)}) collective-permute-start(bf16[80,1152]{1,0:T(8,128)(2,1)S(1)} %get-tuple-element.80.refs_2_), channel_id=1, source_target_pairs={{0,16},{16,0},{1,17},{17,1},{2,18},{18,2},{3,19},{19,3},{4,20},{20... | collective-permute-start | bytes 552968 | tf_op jit(solution)/shard_map/ppermute | solution.py:201
  43.1 1.6 %collective-permute-start.30 = (bf16[64,2176]{1,0:T(8,128)(2,1)S(1)}, bf16[64,2176]{1,0:T(8,128)(2,1)S(1)}, u32[]{:S(2)}, u32[]{:S(2)}) collective-permute-start(bf16[64,2176]{1,0:T(8,128)(2,1)S(1)} %collective-permute-done.29.near), channel_id=1, source_target_pairs={{0,2},{1,3},{2,0},{3,1},{4,6},{5,7},{6,4},{7,5},{8,10},{9,11},{10,... | collective-permute-start | bytes 835592 | tf_op jit(solution)/shard_map/ppermute | solution.py:208
  44.9 3.5 %collective-permute-done.4.refs_3_ = bf16[80,1152]{1,0:T(8,128)(2,1)S(1)} collective-permute-done((bf16[80,1152]{1,0:T(8,128)(2,1)S(1)}, bf16[80,1152]{1,0:T(8,128)(2,1)S(1)}, u32[]{:S(2)}, u32[]{:S(2)}) %collective-permute-start.4) | collective-permute-done | bytes 184352 | tf_op jit(solution)/shard_map/ppermute | solution.py:201
  48.4 1.5 %collective-permute-start.6 = (bf16[80,1152]{1,0:T(8,128)(2,1)S(1)}, bf16[80,1152]{1,0:T(8,128)(2,1)S(1)}, u32[]{:S(2)}, u32[]{:S(2)}) collective-permute-start(bf16[80,1152]{1,0:T(8,128)(2,1)S(1)} %get-tuple-element.84.refs_6_), channel_id=1, source_target_pairs={{0,16},{16,0},{1,17},{17,1},{2,18},{18,2},{3,19},{19,3},{4,20},{20... | collective-permute-start | bytes 552968 | tf_op jit(solution)/shard_map/ppermute | solution.py:201
  49.9 2.4 %collective-permute-done.3.refs_1_ = bf16[80,1152]{1,0:T(8,128)(2,1)S(1)} collective-permute-done((bf16[80,1152]{1,0:T(8,128)(2,1)S(1)}, bf16[80,1152]{1,0:T(8,128)(2,1)S(1)}, u32[]{:S(2)}, u32[]{:S(2)}) %collective-permute-start.3) | collective-permute-done | bytes 184352 | tf_op jit(solution)/shard_map/ppermute | solution.py:201
  52.3 1.5 %collective-permute-start.5 = (bf16[80,1152]{1,0:T(8,128)(2,1)S(1)}, bf16[80,1152]{1,0:T(8,128)(2,1)S(1)}, u32[]{:S(2)}, u32[]{:S(2)}) collective-permute-start(bf16[80,1152]{1,0:T(8,128)(2,1)S(1)} %get-tuple-element.82.refs_4_), channel_id=1, source_target_pairs={{0,16},{16,0},{1,17},{17,1},{2,18},{18,2},{3,19},{19,3},{4,20},{20... | collective-permute-start | bytes 552968 | tf_op jit(solution)/shard_map/ppermute | solution.py:201
  54.0 1.9 %shard_map.106 = (bf16[80,1152]{1,0:T(8,128)(2,1)S(1)}, bf16[80,1152]{1,0:T(8,128)(2,1)S(1)}, bf16[80,1152]{1,0:T(8,128)(2,1)S(1)}, bf16[80,1152]{1,0:T(8,128)(2...) custom-call(s32[2]{0:T(128)S(1)} %copy-done.3, ...), custom_call_target="tpu_custom_call" | custom-call | flops 922746880 | bytes 5832712 | tf_op jit(solution)/shard_map/pallas_call | solution.py:31
  56.3 1.5 %collective-permute-start.13 = (bf16[80,1152]{1,0:T(8,128)(2,1)S(1)}, bf16[80,1152]{1,0:T(8,128)(2,1)S(1)}, u32[]{:S(2)}, u32[]{:S(2)}) collective-permute-start(bf16[80,1152]{1,0:T(8,128)(2,1)S(1)} %get-tuple-element.92.refs_2_), channel_id=1, source_target_pairs={{0,16},{16,0},{1,17},{17,1},{2,18},{18,2},{3,19},{19,3},{4,20},{20... | collective-permute-start | bytes 552968 | tf_op jit(solution)/shard_map/ppermute | solution.py:201
  57.8 2.4 %collective-permute-done.5.refs_5_ = bf16[80,1152]{1,0:T(8,128)(2,1)S(1)} collective-permute-done((bf16[80,1152]{1,0:T(8,128)(2,1)S(1)}, bf16[80,1152]{1,0:T(8,128)(2,1)S(1)}, u32[]{:S(2)}, u32[]{:S(2)}) %collective-permute-start.5) | collective-permute-done | bytes 184352 | tf_op jit(solution)/shard_map/ppermute | solution.py:201
  60.2 1.5 %collective-permute-start.12 = (bf16[80,1152]{1,0:T(8,128)(2,1)S(1)}, bf16[80,1152]{1,0:T(8,128)(2,1)S(1)}, u32[]{:S(2)}, u32[]{:S(2)}) collective-permute-start(bf16[80,1152]{1,0:T(8,128)(2,1)S(1)} %get-tuple-element.90.refs_0_), channel_id=1, source_target_pairs={{0,16},{16,0},{1,17},{17,1},{2,18},{18,2},{3,19},{19,3},{4,20},{20... | collective-permute-start | bytes 552968 | tf_op jit(solution)/shard_map/ppermute | solution.py:201
  61.7 2.7 %shard_map.105 = (bf16[128,2176]{1,0:T(8,128)(2,1)S(1)}, bf16[128,2176]{1,0:T(8,128)(2,1)S(1)}, bf16[160,768]{1,0:T(8,128)(2,1)S(1)}) custom-call(s32[2]{0:T(128)S(1)} %copy-done.3, bf16[80,1152]{1,0:T(8,128)(2,1)S(1)} %get-tuple-element.79.refs_0_, bf16[80,1152]{1,0:T(8,128)(2,1)S(1)} %collective-permute-done.3.refs_1_, ...), custom_call_target="tpu_custom_call" | custom-call | flops 1396703232 | bytes 6357000 | tf_op jit(solution)/shard_map/pallas_call | solution.py:31
  64.5 1.2 collective-permute-start.15
  65.7 2.1 %collective-permute-done.12.refs_1_ = bf16[80,1152]{1,0:T(8,128)(2,1)S(1)} collective-permute-done((bf16[80,1152]{1,0:T(8,128)(2,1)S(1)}, bf16[80,1152]{1,0:T(8,128)(2,1)S(1)}, u32[]{:S(2)}, u32[]{:S(2)}) %collective-permute-start.12) | collective-permute-done | bytes 184352 | tf_op jit(solution)/shard_map/ppermute | solution.py:201
  67.8 1.9 %collective-permute-start.14 = (bf16[80,1152]{1,0:T(8,128)(2,1)S(1)}, bf16[80,1152]{1,0:T(8,128)(2,1)S(1)}, u32[]{:S(2)}, u32[]{:S(2)}) collective-permute-start(bf16[80,1152]{1,0:T(8,128)(2,1)S(1)} %get-tuple-element.94.refs_4_), channel_id=1, source_target_pairs={{0,16},{16,0},{1,17},{17,1},{2,18},{18,2},{3,19},{19,3},{4,20},{20... | collective-permute-start | bytes 552968 | tf_op jit(solution)/shard_map/ppermute | solution.py:201
  69.6 1.9 %shard_map.108 = (bf16[80,1152]{1,0:T(8,128)(2,1)S(1)}, bf16[80,1152]{1,0:T(8,128)(2,1)S(1)}, bf16[80,1152]{1,0:T(8,128)(2,1)S(1)}, bf16[80,1152]{1,0:T(8,128)(2...) custom-call(s32[2]{0:T(128)S(1)} %copy-done.3, ...), custom_call_target="tpu_custom_call" | custom-call | flops 922746880 | bytes 5832712 | tf_op jit(solution)/shard_map/pallas_call | solution.py:31
  72.0 1.6 %collective-permute-start.23 = (bf16[80,1152]{1,0:T(8,128)(2,1)S(1)}, bf16[80,1152]{1,0:T(8,128)(2,1)S(1)}, u32[]{:S(2)}, u32[]{:S(2)}) collective-permute-start(bf16[80,1152]{1,0:T(8,128)(2,1)S(1)} %get-tuple-element.105.refs_2_), channel_id=1, source_target_pairs={{0,16},{16,0},{1,17},{17,1},{2,18},{18,2},{3,19},{19,3},{4,20},{20... | collective-permute-start | bytes 552968 | tf_op jit(solution)/shard_map/ppermute | solution.py:201
  73.6 2.4 %collective-permute-done.14.refs_5_ = bf16[80,1152]{1,0:T(8,128)(2,1)S(1)} collective-permute-done((bf16[80,1152]{1,0:T(8,128)(2,1)S(1)}, bf16[80,1152]{1,0:T(8,128)(2,1)S(1)}, u32[]{:S(2)}, u32[]{:S(2)}) %collective-permute-start.14) | collective-permute-done | bytes 184352 | tf_op jit(solution)/shard_map/ppermute | solution.py:201
  76.0 1.6 %collective-permute-start.22 = (bf16[80,1152]{1,0:T(8,128)(2,1)S(1)}, bf16[80,1152]{1,0:T(8,128)(2,1)S(1)}, u32[]{:S(2)}, u32[]{:S(2)}) collective-permute-start(bf16[80,1152]{1,0:T(8,128)(2,1)S(1)} %get-tuple-element.103.refs_0_), channel_id=1, source_target_pairs={{0,16},{16,0},{1,17},{17,1},{2,18},{18,2},{3,19},{19,3},{4,20},{20... | collective-permute-start | bytes 552968 | tf_op jit(solution)/shard_map/ppermute | solution.py:201
  77.5 2.7 %shard_map.107 = (bf16[128,2176]{1,0:T(8,128)(2,1)S(1)}, bf16[128,2176]{1,0:T(8,128)(2,1)S(1)}, bf16[160,768]{1,0:T(8,128)(2,1)S(1)}) custom-call(s32[2]{0:T(128)S(1)} %copy-done.3, bf16[80,1152]{1,0:T(8,128)(2,1)S(1)} %get-tuple-element.90.refs_0_, bf16[80,1152]{1,0:T(8,128)(2,1)S(1)} %collective-permute-done.12.refs_1_, ...), custom_call_target="tpu_custom_call" | custom-call | flops 1396703232 | bytes 6357000 | tf_op jit(solution)/shard_map/pallas_call | solution.py:31
  80.3 1.9 %shard_map.110 = (bf16[80,1152]{1,0:T(8,128)(2,1)S(1)}, bf16[80,1152]{1,0:T(8,128)(2,1)S(1)}, bf16[80,1152]{1,0:T(8,128)(2,1)S(1)}, bf16[80,1152]{1,0:T(8,128)(2...) custom-call(s32[2]{0:T(128)S(1)} %copy-done.3, ...), custom_call_target="tpu_custom_call" | custom-call | flops 922746880 | bytes 5832712 | tf_op jit(solution)/shard_map/pallas_call | solution.py:31
  82.2 0.5 collective-permute-start.25
  82.7 0.8 collective-permute-done.22.refs_1_
  83.5 1.5 %collective-permute-start.24 = (bf16[80,1152]{1,0:T(8,128)(2,1)S(1)}, bf16[80,1152]{1,0:T(8,128)(2,1)S(1)}, u32[]{:S(2)}, u32[]{:S(2)}) collective-permute-start(bf16[80,1152]{1,0:T(8,128)(2,1)S(1)} %get-tuple-element.107.refs_4_), channel_id=1, source_target_pairs={{0,16},{16,0},{1,17},{17,1},{2,18},{18,2},{3,19},{19,3},{4,20},{20... | collective-permute-start | bytes 552968 | tf_op jit(solution)/shard_map/ppermute | solution.py:201
  85.1 0.6 collective-permute-start.8
  85.8 1.6 %collective-permute-start.17 = (bf16[64,2176]{1,0:T(8,128)(2,1)S(1)}, bf16[64,2176]{1,0:T(8,128)(2,1)S(1)}, u32[]{:S(2)}, u32[]{:S(2)}) collective-permute-start(bf16[64,2176]{1,0:T(8,128)(2,1)S(1)} %add_convert_fusion.8), channel_id=1, source_target_pairs={{0,2},{1,3},{2,0},{3,1},{4,6},{5,7},{6,4},{7,5},{8,10},{9,11},{10,... | collective-permute-start | bytes 835592 | tf_op jit(solution)/shard_map/ppermute | solution.py:208
  87.3 7.4 %collective-permute-done.8 = bf16[64,2176]{1,0:T(8,128)(2,1)S(1)} collective-permute-done((bf16[64,2176]{1,0:T(8,128)(2,1)S(1)}, bf16[64,2176]{1,0:T(8,128)(2,1)S(1)}, u32[]{:S(2)}, u32[]{:S(2)}) %collective-permute-start.8) | collective-permute-done | bytes 278560 | tf_op jit(solution)/shard_map/ppermute | solution.py:208
  94.9 0.6 collective-permute-start.33
  95.5 1.5 %collective-permute-start.32 = (bf16[80,1152]{1,0:T(8,128)(2,1)S(1)}, bf16[80,1152]{1,0:T(8,128)(2,1)S(1)}, u32[]{:S(2)}, u32[]{:S(2)}) collective-permute-start(bf16[80,1152]{1,0:T(8,128)(2,1)S(1)} %get-tuple-element.117.refs_0_), channel_id=1, source_target_pairs={{0,16},{16,0},{1,17},{17,1},{2,18},{18,2},{3,19},{19,3},{4,20},{20... | collective-permute-start | bytes 552968 | tf_op jit(solution)/shard_map/ppermute | solution.py:201
  97.0 2.7 %shard_map.109 = (bf16[128,2176]{1,0:T(8,128)(2,1)S(1)}, bf16[128,2176]{1,0:T(8,128)(2,1)S(1)}, bf16[160,768]{1,0:T(8,128)(2,1)S(1)}) custom-call(s32[2]{0:T(128)S(1)} %copy-done.3, bf16[80,1152]{1,0:T(8,128)(2,1)S(1)} %get-tuple-element.103.refs_0_, bf16[80,1152]{1,0:T(8,128)(2,1)S(1)} %collective-permute-done.22.refs_1_, ...), custom_call_target="tpu_custom_call" | custom-call | flops 1396703232 | bytes 6357000 | tf_op jit(solution)/shard_map/pallas_call | solution.py:31
  99.7 0.8 collective-permute-done.33.refs_3_
  101.0 1.5 %collective-permute-done.32.refs_1_ = bf16[80,1152]{1,0:T(8,128)(2,1)S(1)} collective-permute-done((bf16[80,1152]{1,0:T(8,128)(2,1)S(1)}, bf16[80,1152]{1,0:T(8,128)(2,1)S(1)}, u32[]{:S(2)}, u32[]{:S(2)}) %collective-permute-start.32) | collective-permute-done | bytes 184352 | tf_op jit(solution)/shard_map/ppermute | solution.py:201
  103.3 4.7 %collective-permute-done.35.refs_7_ = bf16[80,1152]{1,0:T(8,128)(2,1)S(1)} collective-permute-done((bf16[80,1152]{1,0:T(8,128)(2,1)S(1)}, bf16[80,1152]{1,0:T(8,128)(2,1)S(1)}, u32[]{:S(2)}, u32[]{:S(2)}) %collective-permute-start.35) | collective-permute-done | bytes 184352 | tf_op jit(solution)/shard_map/ppermute | solution.py:201
  108.0 2.7 %collective-permute-done.34.refs_5_ = bf16[80,1152]{1,0:T(8,128)(2,1)S(1)} collective-permute-done((bf16[80,1152]{1,0:T(8,128)(2,1)S(1)}, bf16[80,1152]{1,0:T(8,128)(2,1)S(1)}, u32[]{:S(2)}, u32[]{:S(2)}) %collective-permute-start.34) | collective-permute-done | bytes 184352 | tf_op jit(solution)/shard_map/ppermute | solution.py:201
  110.7 2.7 %shard_map.111 = (bf16[128,2176]{1,0:T(8,128)(2,1)S(1)}, bf16[128,2176]{1,0:T(8,128)(2,1)S(1)}, bf16[160,768]{1,0:T(8,128)(2,1)S(1)}) custom-call(s32[2]{0:T(128)S(1)} %copy-done.3, bf16[80,1152]{1,0:T(8,128)(2,1)S(1)} %get-tuple-element.117.refs_0_, bf16[80,1152]{1,0:T(8,128)(2,1)S(1)} %collective-permute-done.32.refs_1_, ...), custom_call_target="tpu_custom_call" | custom-call | flops 1396703232 | bytes 6357000 | tf_op jit(solution)/shard_map/pallas_call | solution.py:31
  113.6 0.6 collective-permute-start.27
  114.2 1.3 collective-permute-done.36
  115.5 0.6 collective-permute-start.37
  116.1 7.0 %collective-permute-done.27 = bf16[64,2176]{1,0:T(8,128)(2,1)S(1)} collective-permute-done((bf16[64,2176]{1,0:T(8,128)(2,1)S(1)}, bf16[64,2176]{1,0:T(8,128)(2,1)S(1)}, u32[]{:S(2)}, u32[]{:S(2)}) %collective-permute-start.27) | collective-permute-done | bytes 278560 | tf_op jit(solution)/shard_map/ppermute | solution.py:208
  123.3 5.4 %collective-permute-done.37 = bf16[64,2176]{1,0:T(8,128)(2,1)S(1)} collective-permute-done((bf16[64,2176]{1,0:T(8,128)(2,1)S(1)}, bf16[64,2176]{1,0:T(8,128)(2,1)S(1)}, u32[]{:S(2)}, u32[]{:S(2)}) %collective-permute-start.37) | collective-permute-done | bytes 278560 | tf_op jit(solution)/shard_map/ppermute | solution.py:208
  129.1 2.0 %collective-permute-done.28 = bf16[64,2176]{1,0:T(8,128)(2,1)S(1)} collective-permute-done((bf16[64,2176]{1,0:T(8,128)(2,1)S(1)}, bf16[64,2176]{1,0:T(8,128)(2,1)S(1)}, u32[]{:S(2)}, u32[]{:S(2)}) %collective-permute-start.28) | collective-permute-done | bytes 278560 | tf_op jit(solution)/shard_map/ppermute | solution.py:205
  131.1 7.8 %collective-permute-done.38 = bf16[64,2176]{1,0:T(8,128)(2,1)S(1)} collective-permute-done((bf16[64,2176]{1,0:T(8,128)(2,1)S(1)}, bf16[64,2176]{1,0:T(8,128)(2,1)S(1)}, u32[]{:S(2)}, u32[]{:S(2)}) %collective-permute-start.38) | collective-permute-done | bytes 278560 | tf_op jit(solution)/shard_map/ppermute | solution.py:205
  139.0 0.6 collective-permute-start.39
  139.6 3.2 %shard_map.113 = bf16[1024,768]{1,0:T(8,128)(2,1)} custom-call(s32[2]{0:T(128)S(1)} %copy-done.3, bf16[160,1024]{1,0:T(8,128)(2,1)S(1)} %get-tuple-element.134.refs_0_, bf16[160,1024]{1,0:T(8,128)(2,1)S(1)} %get-tuple-element.135.refs_1_, bf16[160,1024]{1,0:T(8,128)(2,1)S(1)} %get-tuple-element.136.refs_2_, ...), custom_call_target="tpu_custom_call" | custom-call | flops 1006632960 | bytes 2293768 | tf_op jit(solution)/shard_map/pallas_call | solution.py:31
  142.8 1.3 collective-permute-done.39.refs_0_
  144.1 1.5 %shard_map.112 = (bf16[32,2048]{1,0:T(8,128)(2,1)}, bf16[32,2048]{1,0:T(8,128)(2,1)}, f32[8,32]{1,0:T(8,128)}) custom-call(s32[2]{0:T(128)S(1)} %copy-done.3, bf16[32,2176]{1,0:T(8,128)(2,1)S(1)} %slice.80.own, s32[8,32]{1,0:T(8,128)S(1)} %bitcast.13, bf16[32,2048]{1,0:T(8,128)(2,1)S(1)} %collective-permute-done.39.refs_0_), custom_call_target="tpu_custom_call" | custom-call | bytes 271368 | tf_op jit(solution)/shard_map/pallas_call | solution.py:31
  (58 shorter events, 4.8 us)
Async XLA Ops:
  3.6 6.9 %collective-permute-start = (bf16[32,2176]{1,0:T(8,128)(2,1)}, bf16[32,2176]{1,0:T(8,128)(2,1)S(1)}, u32[]{:S(2)}, u32[]{:S(2)}) collective-permute-start(bf16[32,2176]{1,0:T(8,128)(2,1)} %get-tuple-element.74), channel_id=1, source_target_pairs={{0,16},{16,0},{1,17},{17,1},{2,18},{18,2},{3,19},{19,3},{4,20},{20... | collective-permute-start | bytes 417800 | tf_op jit(solution)/shard_map/ppermute | solution.py:201
  10.6 14.8 %collective-permute-start.9 = (bf16[64,2176]{1,0:T(8,128)(2,1)S(1)}, bf16[64,2176]{1,0:T(8,128)(2,1)S(1)}, u32[]{:S(2)}, u32[]{:S(2)}) collective-permute-start(bf16[64,2176]{1,0:T(8,128)(2,1)S(1)} %constant_dynamic-update-slice_fusion.near), channel_id=1, source_target_pairs={{0,8},{1,9},{2,10},{3,11},{4,12},{5,13},{6,14},{7,15},{8,0},{9,1},... | collective-permute-start | bytes 835592 | tf_op jit(solution)/shard_map/ppermute | solution.py:205
  13.4 14.0 %collective-permute-start.1 = (bf16[64,2176]{1,0:T(8,128)(2,1)S(1)}, bf16[64,2176]{1,0:T(8,128)(2,1)S(1)}, u32[]{:S(2)}, u32[]{:S(2)}) collective-permute-start(bf16[64,2176]{1,0:T(8,128)(2,1)S(1)} %constant_dynamic-update-slice_fusion.near), channel_id=1, source_target_pairs={{0,2},{1,3},{2,0},{3,1},{4,6},{5,7},{6,4},{7,5},{8,10},{9,11},{10,... | collective-permute-start | bytes 835592 | tf_op jit(solution)/shard_map/ppermute | solution.py:208
  14.9 1.4 copy-start
  16.3 1.4 copy-start.1
  17.7 1.4 copy-start.2
  19.1 0.7 copy-start.3
  19.8 7.6 %copy-start.5 = (bf16[32,2176]{1,0:T(8,128)(2,1)S(1)}, bf16[32,2176]{1,0:T(8,128)(2,1)}, u32[]{:S(2)}) copy-start(bf16[32,2176]{1,0:T(8,128)(2,1)} %get-tuple-element.73) | copy-start | bytes 417796
  25.3 10.2 %collective-permute-start.19 = (bf16[64,2176]{1,0:T(8,128)(2,1)S(1)}, bf16[64,2176]{1,0:T(8,128)(2,1)S(1)}, u32[]{:S(2)}, u32[]{:S(2)}) collective-permute-start(bf16[64,2176]{1,0:T(8,128)(2,1)S(1)} %constant_dynamic-update-slice_fusion.near), channel_id=1, source_target_pairs={{0,4},{1,5},{2,6},{3,7},{4,8},{5,9},{6,10},{7,11},{8,12},{9,13},{1... | collective-permute-start | bytes 835592 | tf_op jit(solution)/shard_map/ppermute | solution.py:205
  25.9 12.9 %collective-permute-start.10 = (bf16[64,2176]{1,0:T(8,128)(2,1)S(1)}, bf16[64,2176]{1,0:T(8,128)(2,1)S(1)}, u32[]{:S(2)}, u32[]{:S(2)}) collective-permute-start(bf16[64,2176]{1,0:T(8,128)(2,1)S(1)} %collective-permute-done.9.near), channel_id=1, source_target_pairs={{0,2},{1,3},{2,0},{3,1},{4,6},{5,7},{6,4},{7,5},{8,10},{9,11},{10,... | collective-permute-start | bytes 835592 | tf_op jit(solution)/shard_map/ppermute | solution.py:208
  27.4 11.5 %collective-permute-start.2 = (bf16[128,2176]{1,0:T(8,128)(2,1)S(1)}, bf16[128,2176]{1,0:T(8,128)(2,1)S(1)}, u32[]{:S(2)}, u32[]{:S(2)}) collective-permute-start(bf16[128,2176]{1,0:T(8,128)(2,1)S(1)} %pad_maximum_fusion), channel_id=1, source_target_pairs={{0,1},{1,0},{2,3},{3,2},{4,5},{5,4},{6,7},{7,6},{8,9},{9,8},{10,11... | collective-permute-start | bytes 1671176 | tf_op jit(solution)/shard_map/ppermute | solution.py:208
  35.6 7.6 %collective-permute-start.29 = (bf16[64,2176]{1,0:T(8,128)(2,1)S(1)}, bf16[64,2176]{1,0:T(8,128)(2,1)S(1)}, u32[]{:S(2)}, u32[]{:S(2)}) collective-permute-start(bf16[64,2176]{1,0:T(8,128)(2,1)S(1)} %constant_dynamic-update-slice_fusion.near), channel_id=1, source_target_pairs={{0,12},{1,13},{2,14},{3,15},{4,0},{5,1},{6,2},{7,3},{8,4},{9,5},{1... | collective-permute-start | bytes 835592 | tf_op jit(solution)/shard_map/ppermute | solution.py:205
  37.3 7.5 %collective-permute-start.20 = (bf16[64,2176]{1,0:T(8,128)(2,1)S(1)}, bf16[64,2176]{1,0:T(8,128)(2,1)S(1)}, u32[]{:S(2)}, u32[]{:S(2)}) collective-permute-start(bf16[64,2176]{1,0:T(8,128)(2,1)S(1)} %collective-permute-done.19.near), channel_id=1, source_target_pairs={{0,2},{1,3},{2,0},{3,1},{4,6},{5,7},{6,4},{7,5},{8,10},{9,11},{10,... | collective-permute-start | bytes 835592 | tf_op jit(solution)/shard_map/ppermute | solution.py:208
  38.8 15.1 %collective-permute-start.11 = (bf16[128,2176]{1,0:T(8,128)(2,1)S(1)}, bf16[128,2176]{1,0:T(8,128)(2,1)S(1)}, u32[]{:S(2)}, u32[]{:S(2)}) collective-permute-start(bf16[128,2176]{1,0:T(8,128)(2,1)S(1)} %pad_maximum_fusion.1), channel_id=1, source_target_pairs={{0,1},{1,0},{2,3},{3,2},{4,5},{5,4},{6,7},{7,6},{8,9},{9,8},{10,11... | collective-permute-start | bytes 1671176 | tf_op jit(solution)/shard_map/ppermute | solution.py:208
  40.9 7.5 %collective-permute-start.4 = (bf16[80,1152]{1,0:T(8,128)(2,1)S(1)}, bf16[80,1152]{1,0:T(8,128)(2,1)S(1)}, u32[]{:S(2)}, u32[]{:S(2)}) collective-permute-start(bf16[80,1152]{1,0:T(8,128)(2,1)S(1)} %get-tuple-element.80.refs_2_), channel_id=1, source_target_pairs={{0,16},{16,0},{1,17},{17,1},{2,18},{18,2},{3,19},{19,3},{4,20},{20... | collective-permute-start | bytes 552968 | tf_op jit(solution)/shard_map/ppermute | solution.py:201
  42.4 9.9 %collective-permute-start.3 = (bf16[80,1152]{1,0:T(8,128)(2,1)S(1)}, bf16[80,1152]{1,0:T(8,128)(2,1)S(1)}, u32[]{:S(2)}, u32[]{:S(2)}) collective-permute-start(bf16[80,1152]{1,0:T(8,128)(2,1)S(1)} %get-tuple-element.79.refs_0_), channel_id=1, source_target_pairs={{0,16},{16,0},{1,17},{17,1},{2,18},{18,2},{3,19},{19,3},{4,20},{20... | collective-permute-start | bytes 552968 | tf_op jit(solution)/shard_map/ppermute | solution.py:201
  43.1 10.7 %collective-permute-start.30 = (bf16[64,2176]{1,0:T(8,128)(2,1)S(1)}, bf16[64,2176]{1,0:T(8,128)(2,1)S(1)}, u32[]{:S(2)}, u32[]{:S(2)}) collective-permute-start(bf16[64,2176]{1,0:T(8,128)(2,1)S(1)} %collective-permute-done.29.near), channel_id=1, source_target_pairs={{0,2},{1,3},{2,0},{3,1},{4,6},{5,7},{6,4},{7,5},{8,10},{9,11},{10,... | collective-permute-start | bytes 835592 | tf_op jit(solution)/shard_map/ppermute | solution.py:208
  44.8 24.8 %collective-permute-start.21 = (bf16[128,2176]{1,0:T(8,128)(2,1)S(1)}, bf16[128,2176]{1,0:T(8,128)(2,1)S(1)}, u32[]{:S(2)}, u32[]{:S(2)}) collective-permute-start(bf16[128,2176]{1,0:T(8,128)(2,1)S(1)} %pad_maximum_fusion.2), channel_id=1, source_target_pairs={{0,1},{1,0},{2,3},{3,2},{4,5},{5,4},{6,7},{7,6},{8,9},{9,8},{10,11... | collective-permute-start | bytes 1671176 | tf_op jit(solution)/shard_map/ppermute | solution.py:208
  48.4 7.9 %collective-permute-start.6 = (bf16[80,1152]{1,0:T(8,128)(2,1)S(1)}, bf16[80,1152]{1,0:T(8,128)(2,1)S(1)}, u32[]{:S(2)}, u32[]{:S(2)}) collective-permute-start(bf16[80,1152]{1,0:T(8,128)(2,1)S(1)} %get-tuple-element.84.refs_6_), channel_id=1, source_target_pairs={{0,16},{16,0},{1,17},{17,1},{2,18},{18,2},{3,19},{19,3},{4,20},{20... | collective-permute-start | bytes 552968 | tf_op jit(solution)/shard_map/ppermute | solution.py:201
  52.3 7.9 %collective-permute-start.5 = (bf16[80,1152]{1,0:T(8,128)(2,1)S(1)}, bf16[80,1152]{1,0:T(8,128)(2,1)S(1)}, u32[]{:S(2)}, u32[]{:S(2)}) collective-permute-start(bf16[80,1152]{1,0:T(8,128)(2,1)S(1)} %get-tuple-element.82.refs_4_), channel_id=1, source_target_pairs={{0,16},{16,0},{1,17},{17,1},{2,18},{18,2},{3,19},{19,3},{4,20},{20... | collective-permute-start | bytes 552968 | tf_op jit(solution)/shard_map/ppermute | solution.py:201
  53.9 26.4 %collective-permute-start.31 = (bf16[128,2176]{1,0:T(8,128)(2,1)S(1)}, bf16[128,2176]{1,0:T(8,128)(2,1)S(1)}, u32[]{:S(2)}, u32[]{:S(2)}) collective-permute-start(bf16[128,2176]{1,0:T(8,128)(2,1)S(1)} %pad_maximum_fusion.3), channel_id=1, source_target_pairs={{0,1},{1,0},{2,3},{3,2},{4,5},{5,4},{6,7},{7,6},{8,9},{9,8},{10,11... | collective-permute-start | bytes 1671176 | tf_op jit(solution)/shard_map/ppermute | solution.py:208
  56.3 8.2 %collective-permute-start.13 = (bf16[80,1152]{1,0:T(8,128)(2,1)S(1)}, bf16[80,1152]{1,0:T(8,128)(2,1)S(1)}, u32[]{:S(2)}, u32[]{:S(2)}) collective-permute-start(bf16[80,1152]{1,0:T(8,128)(2,1)S(1)} %get-tuple-element.92.refs_2_), channel_id=1, source_target_pairs={{0,16},{16,0},{1,17},{17,1},{2,18},{18,2},{3,19},{19,3},{4,20},{20... | collective-permute-start | bytes 552968 | tf_op jit(solution)/shard_map/ppermute | solution.py:201
  60.2 7.5 %collective-permute-start.12 = (bf16[80,1152]{1,0:T(8,128)(2,1)S(1)}, bf16[80,1152]{1,0:T(8,128)(2,1)S(1)}, u32[]{:S(2)}, u32[]{:S(2)}) collective-permute-start(bf16[80,1152]{1,0:T(8,128)(2,1)S(1)} %get-tuple-element.90.refs_0_), channel_id=1, source_target_pairs={{0,16},{16,0},{1,17},{17,1},{2,18},{18,2},{3,19},{19,3},{4,20},{20... | collective-permute-start | bytes 552968 | tf_op jit(solution)/shard_map/ppermute | solution.py:201
  64.4 20.6 %collective-permute-start.7 = (bf16[128,2176]{1,0:T(8,128)(2,1)S(1)}, bf16[128,2176]{1,0:T(8,128)(2,1)S(1)}, u32[]{:S(2)}, u32[]{:S(2)}) collective-permute-start(bf16[128,2176]{1,0:T(8,128)(2,1)S(1)} %get-tuple-element.88), channel_id=1, source_target_pairs={{0,1},{1,0},{2,3},{3,2},{4,5},{5,4},{6,7},{7,6},{8,9},{9,8},{10,11... | collective-permute-start | bytes 1671176 | tf_op jit(solution)/shard_map/ppermute | solution.py:208
  64.5 7.5 %collective-permute-start.15 = (bf16[80,1152]{1,0:T(8,128)(2,1)S(1)}, bf16[80,1152]{1,0:T(8,128)(2,1)S(1)}, u32[]{:S(2)}, u32[]{:S(2)}) collective-permute-start(bf16[80,1152]{1,0:T(8,128)(2,1)S(1)} %get-tuple-element.96.refs_6_), channel_id=1, source_target_pairs={{0,16},{16,0},{1,17},{17,1},{2,18},{18,2},{3,19},{19,3},{4,20},{20... | collective-permute-start | bytes 552968 | tf_op jit(solution)/shard_map/ppermute | solution.py:201
  67.8 8.2 %collective-permute-start.14 = (bf16[80,1152]{1,0:T(8,128)(2,1)S(1)}, bf16[80,1152]{1,0:T(8,128)(2,1)S(1)}, u32[]{:S(2)}, u32[]{:S(2)}) collective-permute-start(bf16[80,1152]{1,0:T(8,128)(2,1)S(1)} %get-tuple-element.94.refs_4_), channel_id=1, source_target_pairs={{0,16},{16,0},{1,17},{17,1},{2,18},{18,2},{3,19},{19,3},{4,20},{20... | collective-permute-start | bytes 552968 | tf_op jit(solution)/shard_map/ppermute | solution.py:201
  72.0 10.2 %collective-permute-start.23 = (bf16[80,1152]{1,0:T(8,128)(2,1)S(1)}, bf16[80,1152]{1,0:T(8,128)(2,1)S(1)}, u32[]{:S(2)}, u32[]{:S(2)}) collective-permute-start(bf16[80,1152]{1,0:T(8,128)(2,1)S(1)} %get-tuple-element.105.refs_2_), channel_id=1, source_target_pairs={{0,16},{16,0},{1,17},{17,1},{2,18},{18,2},{3,19},{19,3},{4,20},{20... | collective-permute-start | bytes 552968 | tf_op jit(solution)/shard_map/ppermute | solution.py:201
  76.0 7.6 %collective-permute-start.22 = (bf16[80,1152]{1,0:T(8,128)(2,1)S(1)}, bf16[80,1152]{1,0:T(8,128)(2,1)S(1)}, u32[]{:S(2)}, u32[]{:S(2)}) collective-permute-start(bf16[80,1152]{1,0:T(8,128)(2,1)S(1)} %get-tuple-element.103.refs_0_), channel_id=1, source_target_pairs={{0,16},{16,0},{1,17},{17,1},{2,18},{18,2},{3,19},{19,3},{4,20},{20... | collective-permute-start | bytes 552968 | tf_op jit(solution)/shard_map/ppermute | solution.py:201
  80.2 5.5 %collective-permute-start.16 = (bf16[128,2176]{1,0:T(8,128)(2,1)S(1)}, bf16[128,2176]{1,0:T(8,128)(2,1)S(1)}, u32[]{:S(2)}, u32[]{:S(2)}) collective-permute-start(bf16[128,2176]{1,0:T(8,128)(2,1)S(1)} %get-tuple-element.100), channel_id=1, source_target_pairs={{0,1},{1,0},{2,3},{3,2},{4,5},{5,4},{6,7},{7,6},{8,9},{9,8},{10,11... | collective-permute-start | bytes 1671176 | tf_op jit(solution)/shard_map/ppermute | solution.py:208
  82.2 12.6 %collective-permute-start.25 = (bf16[80,1152]{1,0:T(8,128)(2,1)S(1)}, bf16[80,1152]{1,0:T(8,128)(2,1)S(1)}, u32[]{:S(2)}, u32[]{:S(2)}) collective-permute-start(bf16[80,1152]{1,0:T(8,128)(2,1)S(1)} %get-tuple-element.109.refs_6_), channel_id=1, source_target_pairs={{0,16},{16,0},{1,17},{17,1},{2,18},{18,2},{3,19},{19,3},{4,20},{20... | collective-permute-start | bytes 552968 | tf_op jit(solution)/shard_map/ppermute | solution.py:201
  83.5 12.0 %collective-permute-start.24 = (bf16[80,1152]{1,0:T(8,128)(2,1)S(1)}, bf16[80,1152]{1,0:T(8,128)(2,1)S(1)}, u32[]{:S(2)}, u32[]{:S(2)}) collective-permute-start(bf16[80,1152]{1,0:T(8,128)(2,1)S(1)} %get-tuple-element.107.refs_4_), channel_id=1, source_target_pairs={{0,16},{16,0},{1,17},{17,1},{2,18},{18,2},{3,19},{19,3},{4,20},{20... | collective-permute-start | bytes 552968 | tf_op jit(solution)/shard_map/ppermute | solution.py:201
  85.1 9.7 %collective-permute-start.8 = (bf16[64,2176]{1,0:T(8,128)(2,1)S(1)}, bf16[64,2176]{1,0:T(8,128)(2,1)S(1)}, u32[]{:S(2)}, u32[]{:S(2)}) collective-permute-start(bf16[64,2176]{1,0:T(8,128)(2,1)S(1)} %add_convert_fusion.11), channel_id=1, source_target_pairs={{0,2},{1,3},{2,0},{3,1},{4,6},{5,7},{6,4},{7,5},{8,10},{9,11},{10,... | collective-permute-start | bytes 835592 | tf_op jit(solution)/shard_map/ppermute | solution.py:208
  85.8 17.2 %collective-permute-start.17 = (bf16[64,2176]{1,0:T(8,128)(2,1)S(1)}, bf16[64,2176]{1,0:T(8,128)(2,1)S(1)}, u32[]{:S(2)}, u32[]{:S(2)}) collective-permute-start(bf16[64,2176]{1,0:T(8,128)(2,1)S(1)} %add_convert_fusion.8), channel_id=1, source_target_pairs={{0,2},{1,3},{2,0},{3,1},{4,6},{5,7},{6,4},{7,5},{8,10},{9,11},{10,... | collective-permute-start | bytes 835592 | tf_op jit(solution)/shard_map/ppermute | solution.py:208
  94.9 5.6 %collective-permute-start.33 = (bf16[80,1152]{1,0:T(8,128)(2,1)S(1)}, bf16[80,1152]{1,0:T(8,128)(2,1)S(1)}, u32[]{:S(2)}, u32[]{:S(2)}) collective-permute-start(bf16[80,1152]{1,0:T(8,128)(2,1)S(1)} %get-tuple-element.120.refs_2_), channel_id=1, source_target_pairs={{0,16},{16,0},{1,17},{17,1},{2,18},{18,2},{3,19},{19,3},{4,20},{20... | collective-permute-start | bytes 552968 | tf_op jit(solution)/shard_map/ppermute | solution.py:201
  95.5 7.0 %collective-permute-start.32 = (bf16[80,1152]{1,0:T(8,128)(2,1)S(1)}, bf16[80,1152]{1,0:T(8,128)(2,1)S(1)}, u32[]{:S(2)}, u32[]{:S(2)}) collective-permute-start(bf16[80,1152]{1,0:T(8,128)(2,1)S(1)} %get-tuple-element.117.refs_0_), channel_id=1, source_target_pairs={{0,16},{16,0},{1,17},{17,1},{2,18},{18,2},{3,19},{19,3},{4,20},{20... | collective-permute-start | bytes 552968 | tf_op jit(solution)/shard_map/ppermute | solution.py:201
  99.7 13.8 %collective-permute-start.26 = (bf16[128,2176]{1,0:T(8,128)(2,1)S(1)}, bf16[128,2176]{1,0:T(8,128)(2,1)S(1)}, u32[]{:S(2)}, u32[]{:S(2)}) collective-permute-start(bf16[128,2176]{1,0:T(8,128)(2,1)S(1)} %get-tuple-element.113), channel_id=1, source_target_pairs={{0,1},{1,0},{2,3},{3,2},{4,5},{5,4},{6,7},{7,6},{8,9},{9,8},{10,11... | collective-permute-start | bytes 1671176 | tf_op jit(solution)/shard_map/ppermute | solution.py:208
  100.5 7.5 %collective-permute-start.35 = (bf16[80,1152]{1,0:T(8,128)(2,1)S(1)}, bf16[80,1152]{1,0:T(8,128)(2,1)S(1)}, u32[]{:S(2)}, u32[]{:S(2)}) collective-permute-start(bf16[80,1152]{1,0:T(8,128)(2,1)S(1)} %get-tuple-element.126.refs_6_), channel_id=1, source_target_pairs={{0,16},{16,0},{1,17},{17,1},{2,18},{18,2},{3,19},{19,3},{4,20},{20... | collective-permute-start | bytes 552968 | tf_op jit(solution)/shard_map/ppermute | solution.py:201
  102.5 8.3 %collective-permute-start.34 = (bf16[80,1152]{1,0:T(8,128)(2,1)S(1)}, bf16[80,1152]{1,0:T(8,128)(2,1)S(1)}, u32[]{:S(2)}, u32[]{:S(2)}) collective-permute-start(bf16[80,1152]{1,0:T(8,128)(2,1)S(1)} %get-tuple-element.123.refs_4_), channel_id=1, source_target_pairs={{0,16},{16,0},{1,17},{17,1},{2,18},{18,2},{3,19},{19,3},{4,20},{20... | collective-permute-start | bytes 552968 | tf_op jit(solution)/shard_map/ppermute | solution.py:201
  103.3 25.8 %collective-permute-start.18 = (bf16[64,2176]{1,0:T(8,128)(2,1)S(1)}, bf16[64,2176]{1,0:T(8,128)(2,1)S(1)}, u32[]{:S(2)}, u32[]{:S(2)}) collective-permute-start(bf16[64,2176]{1,0:T(8,128)(2,1)S(1)} %add_convert_fusion.7), channel_id=1, source_target_pairs={{0,8},{1,9},{2,10},{3,11},{4,12},{5,13},{6,14},{7,15},{8,0},{9,1},... | collective-permute-start | bytes 835592 | tf_op jit(solution)/shard_map/ppermute | solution.py:205
  113.4 2.0 %collective-permute-start.36 = (bf16[128,2176]{1,0:T(8,128)(2,1)S(1)}, bf16[128,2176]{1,0:T(8,128)(2,1)S(1)}, u32[]{:S(2)}, u32[]{:S(2)}) collective-permute-start(bf16[128,2176]{1,0:T(8,128)(2,1)S(1)} %get-tuple-element.130), channel_id=1, source_target_pairs={{0,1},{1,0},{2,3},{3,2},{4,5},{5,4},{6,7},{7,6},{8,9},{9,8},{10,11... | collective-permute-start | bytes 1671176 | tf_op jit(solution)/shard_map/ppermute | solution.py:208
  113.6 9.5 %collective-permute-start.27 = (bf16[64,2176]{1,0:T(8,128)(2,1)S(1)}, bf16[64,2176]{1,0:T(8,128)(2,1)S(1)}, u32[]{:S(2)}, u32[]{:S(2)}) collective-permute-start(bf16[64,2176]{1,0:T(8,128)(2,1)S(1)} %add_convert_fusion.5), channel_id=1, source_target_pairs={{0,2},{1,3},{2,0},{3,1},{4,6},{5,7},{6,4},{7,5},{8,10},{9,11},{10,... | collective-permute-start | bytes 835592 | tf_op jit(solution)/shard_map/ppermute | solution.py:208
  115.5 13.2 %collective-permute-start.37 = (bf16[64,2176]{1,0:T(8,128)(2,1)S(1)}, bf16[64,2176]{1,0:T(8,128)(2,1)S(1)}, u32[]{:S(2)}, u32[]{:S(2)}) collective-permute-start(bf16[64,2176]{1,0:T(8,128)(2,1)S(1)} %add_convert_fusion.2), channel_id=1, source_target_pairs={{0,2},{1,3},{2,0},{3,1},{4,6},{5,7},{6,4},{7,5},{8,10},{9,11},{10,... | collective-permute-start | bytes 835592 | tf_op jit(solution)/shard_map/ppermute | solution.py:208
  123.2 7.9 %collective-permute-start.28 = (bf16[64,2176]{1,0:T(8,128)(2,1)S(1)}, bf16[64,2176]{1,0:T(8,128)(2,1)S(1)}, u32[]{:S(2)}, u32[]{:S(2)}) collective-permute-start(bf16[64,2176]{1,0:T(8,128)(2,1)S(1)} %add_convert_fusion.4), channel_id=1, source_target_pairs={{0,12},{1,13},{2,14},{3,15},{4,0},{5,1},{6,2},{7,3},{8,4},{9,5},{1... | collective-permute-start | bytes 835592 | tf_op jit(solution)/shard_map/ppermute | solution.py:205
  128.8 10.1 %collective-permute-start.38 = (bf16[64,2176]{1,0:T(8,128)(2,1)S(1)}, bf16[64,2176]{1,0:T(8,128)(2,1)S(1)}, u32[]{:S(2)}, u32[]{:S(2)}) collective-permute-start(bf16[64,2176]{1,0:T(8,128)(2,1)S(1)} %add_convert_fusion.1), channel_id=1, source_target_pairs={{0,4},{1,5},{2,6},{3,7},{4,8},{5,9},{6,10},{7,11},{8,12},{9,13},{1... | collective-permute-start | bytes 835592 | tf_op jit(solution)/shard_map/ppermute | solution.py:205
  139.0 5.0 %collective-permute-start.39 = (bf16[32,2048]{1,0:T(8,128)(2,1)S(1)}, bf16[32,2048]{1,0:T(8,128)(2,1)S(1)}, u32[]{:S(2)}, u32[]{:S(2)}) collective-permute-start(bf16[32,2048]{1,0:T(8,128)(2,1)S(1)} %slice.81), channel_id=1, source_target_pairs={{0,16},{16,0},{1,17},{17,1},{2,18},{18,2},{3,19},{19,3},{4,20},{20... | collective-permute-start | bytes 393224 | tf_op jit(solution)/shard_map/ppermute | solution.py:201
  139.6 4.5 %copy-start.4 = (s32[32,8]{0,1:T(8,128)S(1)}, s32[32,8]{0,1:T(8,128)}, u32[]{:S(2)}) copy-start(s32[32,8]{0,1:T(8,128)} %param.10) | copy-start | bytes 3076

commit v3 on v2

--- a/solution.py
+++ b/solution.py
@@ -204,6 +204,12 @@
         step = SIDE * CORE * k
         return lax.ppermute(x, "expert", [(i, (i + step) % n_experts) for i in range(n_experts)])
 
+    def joint(x, s, moved):
+        pairs = [
+            (d * n_experts + e, (d + s) % n_dp * n_experts + moved(e)) for d in range(n_dp) for e in range(n_experts)
+        ]
+        return lax.ppermute(x, ("dp", "expert"), pairs)
+
     def swap(x, bit):
         return lax.ppermute(x, "expert", [(i, i ^ bit) for i in range(n_experts)])
 
@@ -231,10 +237,18 @@
         return [part] + others
 
     def forward(i):
-        sides.append(swap(near[i], CORE))
+        if i == 0:
+            sides.append(jnp.concatenate([joint(blocks[s], s, lambda e: e ^ CORE) for s in range(n_dp)], axis=0))
+        else:
+            sides.append(swap(near[i], CORE))
         both = jnp.concatenate([near[i], sides[i]], axis=0)
         if i + 1 < layers:
-            near.append(layer_shift(after(mine, near[i]) if i else mine, order[i + 1]))
+            if i == 0:
+                step = SIDE * CORE * order[1]
+                direct = [joint(blocks[s], s, lambda e: (e + step) % n_experts) for s in range(n_dp)]
+                near.append(jnp.concatenate(direct, axis=0))
+            else:
+                near.append(layer_shift(after(mine, near[i]), order[i + 1]))
         if i == 0:
             both = after(both, wg, wu, wd)
         core = swap(both, 1)
@@ -250,12 +264,12 @@
             flops=2 * rows * half * 3 * ff + 4 * rows * total * half,
         )
         kept.append((up_rows, sel, weight))
-        if i >= 3:
-            pieces = [after(piece, partials[i - 3]) for piece in pieces]
         parts.append(sum([over_dp(piece) for piece in pieces], []))
 
     def backward(i):
         up_rows, sel, weight = kept[i]
+        if i + 1 < len(kept):
+            weight = after(weight, kept[i + 1][2])
         keep, send, hidden = call(
             functools.partial(backward_kernel, n_experts, n_dp),
             [((total // 2, wide), BF16), ((total // 2, wide), BF16), ((rows, ff), BF16)],

time: 146 us -> 142 us (0.973)
  waiting for transfers between devices: 72 us -> 58.9 us
  starting transfers between devices: 38.8 us -> 47.5 us
    ppermute x6 -> x5, waiting for transfers between devices: 22.6 us -> 8.1 us  [layer_shift(): lax.ppermute(x, 'expert', [(i, (i + step) % n_experts) for i in range(n_e...]
    ppermute x6 -> x5, starting transfers between devices: 5.66 us -> 13.8 us  [layer_shift(): lax.ppermute(x, 'expert', [(i, (i + step) % n_experts) for i in range(n_e...]
    ppermute x16 -> x15, waiting for transfers between devices: 21.1 us -> 13.4 us  [swap(): return lax.ppermute(x, 'expert', [(i, i ^ bit) for i in range(n_experts)])]
    ppermute x0 -> x4, starting transfers between devices: none -> 7.36 us  [joint(): return lax.ppermute(x, ('dp', 'expert'), pairs)]
    ppermute x18, starting transfers between devices: 23.1 us -> 16.2 us  [dp_shift(): return lax.ppermute(x, 'dp', [(i, (i + s) % n_dp) for i in range(n_dp)])]
    ppermute x18, waiting for transfers between devices: 28.2 us -> 35 us  [dp_shift(): return lax.ppermute(x, 'dp', [(i, (i + s) % n_dp) for i in range(n_dp)])]
    ppermute x0 -> x4, waiting for transfers between devices: none -> 2.33 us  [joint(): return lax.ppermute(x, ('dp', 'expert'), pairs)]
    ppermute x16 -> x15, starting transfers between devices: 10 us -> 10.2 us  [swap(): return lax.ppermute(x, 'expert', [(i, i ^ bit) for i in range(n_experts)])]
  transfers between devices with their start and end apart: 40 -> 42, of which waited for: 23 -> 21; matrix products, arithmetic and copies ran while one was open for 1% -> 1% of each run, Pallas kernels for 15% -> 16%
where the time goes in v3:
time: 142 us; the launch traced here: 141 us
  waiting for transfers between devices  58.9 us (41%)
  starting transfers between devices  47.5 us (33%)
  Pallas kernels  26.5 us (19%)
  local copies, waits for them, and re-layouts  5.9 us (4%)
  other arithmetic  1.59 us (1%)
    ppermute x18, waiting for transfers between devices, dp_shift(): return lax.ppermute(x, 'dp', [(i, (i + s) % n_dp) for i in range(n_dp)])  35 us
    pallas_call x12, Pallas kernels, call(): pl.pallas_call(body, out_shape=[jax.ShapeDtypeStruct(s, t) for s, t in ou...  26.5 us
    ppermute x18, starting transfers between devices, dp_shift(): return lax.ppermute(x, 'dp', [(i, (i + s) % n_dp) for i in range(n_dp)])  16.2 us
    ppermute x5, starting transfers between devices, layer_shift(): lax.ppermute(x, 'expert', [(i, (i + step) % n_experts) for i in range(n_e...  13.8 us
    ppermute x15, waiting for transfers between devices, swap(): return lax.ppermute(x, 'expert', [(i, i ^ bit) for i in range(n_experts)])  13.4 us
    ppermute x15, starting transfers between devices, swap(): return lax.ppermute(x, 'expert', [(i, i ^ bit) for i in range(n_experts)])  10.2 us
    ppermute x5, waiting for transfers between devices, layer_shift(): lax.ppermute(x, 'expert', [(i, (i + step) % n_experts) for i in range(n_e...  8.1 us
    ppermute x4, starting transfers between devices, joint(): return lax.ppermute(x, ('dp', 'expert'), pairs)  7.36 us
  transfers between devices with their start and end apart: 42, of which 21 were waited for; matrix products, arithmetic and copies ran while one was open for 1% of the time, Pallas kernels for 16%

profile of v3, /device:TPU:0, one launch (start us, length us, event | category | flops | bytes accessed | tf_op | source)
XLA Modules:
  0.0 141.3 jit_solution(10646161761512646193)
XLA Ops:
  1.2 2.4 %shard_map.102 = (bf16[32,2176]{1,0:T(8,128)(2,1)}, bf16[32,2176]{1,0:T(8,128)(2,1)}) custom-call(s32[2]{0:T(128)} %pad_add_fusion.ids, f32[8,32]{1,0:T(8,128)} %bitcast.15, s32[8,32]{1,0:T(8,128)} %bitcast.12, bf16[32,2048]{1,0:T(8,128)(2,1)} %tok_ref.1, bf16[32,2048]{1,0:T(8,128)(2,1)} %up_ref.1), custom_call_target="tpu_custom_call" | custom-call | bytes 264200 | tf_op jit(solution)/shard_map/pallas_call | solution.py:31
  3.6 5.1 %collective-permute-start.9 = (bf16[32,2176]{1,0:T(8,128)(2,1)}, bf16[32,2176]{1,0:T(8,128)(2,1)S(1)}, u32[]{:S(2)}, u32[]{:S(2)}) collective-permute-start(bf16[32,2176]{1,0:T(8,128)(2,1)} %get-tuple-element.73), channel_id=1, source_target_pairs={{0,24},{1,25},{2,26},{3,27},{4,28},{5,29},{6,30},{7,31},{8,16},{9,... | collective-permute-start | bytes 417800 | tf_op jit(solution)/shard_map/ppermute | solution.py:211
  8.7 1.4 %collective-permute-start.2 = (bf16[32,2176]{1,0:T(8,128)(2,1)}, bf16[32,2176]{1,0:T(8,128)(2,1)S(1)}, u32[]{:S(2)}, u32[]{:S(2)}) collective-permute-start(bf16[32,2176]{1,0:T(8,128)(2,1)} %get-tuple-element.73), channel_id=1, source_target_pairs={{0,18},{1,19},{2,16},{3,17},{4,22},{5,23},{6,20},{7,21},{8,26},{9,... | collective-permute-start | bytes 417800 | tf_op jit(solution)/shard_map/ppermute | solution.py:211
  10.1 1.5 %collective-permute-start = (bf16[32,2176]{1,0:T(8,128)(2,1)}, bf16[32,2176]{1,0:T(8,128)(2,1)S(1)}, u32[]{:S(2)}, u32[]{:S(2)}) collective-permute-start(bf16[32,2176]{1,0:T(8,128)(2,1)} %get-tuple-element.73), channel_id=1, source_target_pairs={{0,16},{16,0},{1,17},{17,1},{2,18},{18,2},{3,19},{19,3},{4,20},{20... | collective-permute-start | bytes 417800 | tf_op jit(solution)/shard_map/ppermute | solution.py:201
  12.5 1.0 constant_dynamic-update-slice_fusion.1
  13.5 1.4 copy-done
  14.9 1.4 copy-done.1
  16.3 1.4 copy-done.2
  17.7 0.7 copy-done.3
  18.4 0.9 shard_map.103
  19.2 2.3 %collective-permute-done.8 = bf16[32,2176]{1,0:T(8,128)(2,1)S(1)} collective-permute-done((bf16[32,2176]{1,0:T(8,128)(2,1)}, bf16[32,2176]{1,0:T(8,128)(2,1)S(1)}, u32[]{:S(2)}, u32[]{:S(2)}) %collective-permute-start.8) | collective-permute-done | bytes 139296 | tf_op jit(solution)/shard_map/ppermute | solution.py:211
  21.6 1.6 %collective-permute-start.10 = (bf16[64,2176]{1,0:T(8,128)(2,1)S(1)}, bf16[64,2176]{1,0:T(8,128)(2,1)S(1)}, u32[]{:S(2)}, u32[]{:S(2)}) collective-permute-start(bf16[64,2176]{1,0:T(8,128)(2,1)S(1)} %constant_dynamic-update-slice_fusion.2.near), channel_id=1, source_target_pairs={{0,2},{1,3},{2,0},{3,1},{4,6},{5,7},{6,4},{7,5},{8,10},{9,11},{10,... | collective-permute-start | bytes 835592 | tf_op jit(solution)/shard_map/ppermute | solution.py:214
  23.2 0.8 collective-permute-start.18
  24.2 5.1 %collective-permute-done.10.side = bf16[64,2176]{1,0:T(8,128)(2,1)S(1)} collective-permute-done((bf16[64,2176]{1,0:T(8,128)(2,1)S(1)}, bf16[64,2176]{1,0:T(8,128)(2,1)S(1)}, u32[]{:S(2)}, u32[]{:S(2)}) %collective-permute-start.10) | collective-permute-done | bytes 278560 | tf_op jit(solution)/shard_map/ppermute | solution.py:214
  29.4 1.9 %shard_map.104 = (bf16[80,1152]{1,0:T(8,128)(2,1)S(1)}, bf16[80,1152]{1,0:T(8,128)(2,1)S(1)}, bf16[80,1152]{1,0:T(8,128)(2,1)S(1)}, bf16[80,1152]{1,0:T(8,128)(2...) custom-call(s32[2]{0:T(128)S(1)} %copy-done.3, ...), custom_call_target="tpu_custom_call" | custom-call | flops 922746880 | bytes 5832712 | tf_op jit(solution)/shard_map/pallas_call | solution.py:31
  31.3 0.9 collective-permute-start.4
  32.2 1.2 collective-permute-start.5
  33.4 4.5 %collective-permute-start.28 = (bf16[64,2176]{1,0:T(8,128)(2,1)S(1)}, bf16[64,2176]{1,0:T(8,128)(2,1)S(1)}, u32[]{:S(2)}, u32[]{:S(2)}) collective-permute-start(bf16[64,2176]{1,0:T(8,128)(2,1)S(1)} %constant_dynamic-update-slice_fusion.near), channel_id=1, source_target_pairs={{0,12},{1,13},{2,14},{3,15},{4,0},{5,1},{6,2},{7,3},{8,4},{9,5},{1... | collective-permute-start | bytes 835592 | tf_op jit(solution)/shard_map/ppermute | solution.py:205
  37.9 1.5 %collective-permute-start.19 = (bf16[64,2176]{1,0:T(8,128)(2,1)S(1)}, bf16[64,2176]{1,0:T(8,128)(2,1)S(1)}, u32[]{:S(2)}, u32[]{:S(2)}) collective-permute-start(bf16[64,2176]{1,0:T(8,128)(2,1)S(1)} %collective-permute-done.18.near), channel_id=1, source_target_pairs={{0,2},{1,3},{2,0},{3,1},{4,6},{5,7},{6,4},{7,5},{8,10},{9,11},{10,... | collective-permute-start | bytes 835592 | tf_op jit(solution)/shard_map/ppermute | solution.py:214
  39.9 2.8 %collective-permute-done.5.refs_3_ = bf16[80,1152]{1,0:T(8,128)(2,1)S(1)} collective-permute-done((bf16[80,1152]{1,0:T(8,128)(2,1)S(1)}, bf16[80,1152]{1,0:T(8,128)(2,1)S(1)}, u32[]{:S(2)}, u32[]{:S(2)}) %collective-permute-start.5) | collective-permute-done | bytes 184352 | tf_op jit(solution)/shard_map/ppermute | solution.py:201
  42.8 0.8 collective-permute-start.7
  43.9 1.5 %collective-permute-start.29 = (bf16[64,2176]{1,0:T(8,128)(2,1)S(1)}, bf16[64,2176]{1,0:T(8,128)(2,1)S(1)}, u32[]{:S(2)}, u32[]{:S(2)}) collective-permute-start(bf16[64,2176]{1,0:T(8,128)(2,1)S(1)} %collective-permute-done.28.near), channel_id=1, source_target_pairs={{0,2},{1,3},{2,0},{3,1},{4,6},{5,7},{6,4},{7,5},{8,10},{9,11},{10,... | collective-permute-start | bytes 835592 | tf_op jit(solution)/shard_map/ppermute | solution.py:214
  45.4 1.9 %shard_map.105 = (bf16[80,1152]{1,0:T(8,128)(2,1)S(1)}, bf16[80,1152]{1,0:T(8,128)(2,1)S(1)}, bf16[80,1152]{1,0:T(8,128)(2,1)S(1)}, bf16[80,1152]{1,0:T(8,128)(2...) custom-call(s32[2]{0:T(128)S(1)} %copy-done.3, ...), custom_call_target="tpu_custom_call" | custom-call | flops 922746880 | bytes 5832712 | tf_op jit(solution)/shard_map/pallas_call | solution.py:31
  47.3 1.0 collective-permute-start.14
  48.3 2.6 %collective-permute-done.7.refs_7_ = bf16[80,1152]{1,0:T(8,128)(2,1)S(1)} collective-permute-done((bf16[80,1152]{1,0:T(8,128)(2,1)S(1)}, bf16[80,1152]{1,0:T(8,128)(2,1)S(1)}, u32[]{:S(2)}, u32[]{:S(2)}) %collective-permute-start.7) | collective-permute-done | bytes 184352 | tf_op jit(solution)/shard_map/ppermute | solution.py:201
  51.6 3.3 %collective-permute-done.14.refs_1_ = bf16[80,1152]{1,0:T(8,128)(2,1)S(1)} collective-permute-done((bf16[80,1152]{1,0:T(8,128)(2,1)S(1)}, bf16[80,1152]{1,0:T(8,128)(2,1)S(1)}, u32[]{:S(2)}, u32[]{:S(2)}) %collective-permute-start.14) | collective-permute-done | bytes 184352 | tf_op jit(solution)/shard_map/ppermute | solution.py:201
  55.0 0.9 collective-permute-start.16
  55.9 3.0 %collective-permute-done.15.refs_3_ = bf16[80,1152]{1,0:T(8,128)(2,1)S(1)} collective-permute-done((bf16[80,1152]{1,0:T(8,128)(2,1)S(1)}, bf16[80,1152]{1,0:T(8,128)(2,1)S(1)}, u32[]{:S(2)}, u32[]{:S(2)}) %collective-permute-start.15) | collective-permute-done | bytes 184352 | tf_op jit(solution)/shard_map/ppermute | solution.py:201
  58.9 0.9 collective-permute-start.17
  60.0 1.9 %shard_map.107 = (bf16[80,1152]{1,0:T(8,128)(2,1)S(1)}, bf16[80,1152]{1,0:T(8,128)(2,1)S(1)}, bf16[80,1152]{1,0:T(8,128)(2,1)S(1)}, bf16[80,1152]{1,0:T(8,128)(2...) custom-call(s32[2]{0:T(128)S(1)} %copy-done.3, ...), custom_call_target="tpu_custom_call" | custom-call | flops 922746880 | bytes 5832712 | tf_op jit(solution)/shard_map/pallas_call | solution.py:31
  61.9 1.0 collective-permute-done.16.refs_5_
  62.9 3.2 %collective-permute-done.17.refs_7_ = bf16[80,1152]{1,0:T(8,128)(2,1)S(1)} collective-permute-done((bf16[80,1152]{1,0:T(8,128)(2,1)S(1)}, bf16[80,1152]{1,0:T(8,128)(2,1)S(1)}, u32[]{:S(2)}, u32[]{:S(2)}) %collective-permute-start.17) | collective-permute-done | bytes 184352 | tf_op jit(solution)/shard_map/ppermute | solution.py:201
  66.1 2.7 %shard_map.108 = (bf16[128,2176]{1,0:T(8,128)(2,1)S(1)}, bf16[128,2176]{1,0:T(8,128)(2,1)S(1)}, bf16[160,768]{1,0:T(8,128)(2,1)S(1)}) custom-call(s32[2]{0:T(128)S(1)} %copy-done.3, bf16[80,1152]{1,0:T(8,128)(2,1)S(1)} %get-tuple-element.91.refs_0_, bf16[80,1152]{1,0:T(8,128)(2,1)S(1)} %collective-permute-done.14.refs_1_, ...), custom_call_target="tpu_custom_call" | custom-call | flops 1396703232 | bytes 6357000 | tf_op jit(solution)/shard_map/pallas_call | solution.py:31
  68.8 0.9 collective-permute-start.24
  69.7 1.2 collective-permute-start.25
  70.9 5.4 %collective-permute-done.24.refs_1_ = bf16[80,1152]{1,0:T(8,128)(2,1)S(1)} collective-permute-done((bf16[80,1152]{1,0:T(8,128)(2,1)S(1)}, bf16[80,1152]{1,0:T(8,128)(2,1)S(1)}, u32[]{:S(2)}, u32[]{:S(2)}) %collective-permute-start.24) | collective-permute-done | bytes 184352 | tf_op jit(solution)/shard_map/ppermute | solution.py:201
  76.3 0.8 collective-permute-start.26
  77.1 3.1 %collective-permute-done.25.refs_3_ = bf16[80,1152]{1,0:T(8,128)(2,1)S(1)} collective-permute-done((bf16[80,1152]{1,0:T(8,128)(2,1)S(1)}, bf16[80,1152]{1,0:T(8,128)(2,1)S(1)}, u32[]{:S(2)}, u32[]{:S(2)}) %collective-permute-start.25) | collective-permute-done | bytes 184352 | tf_op jit(solution)/shard_map/ppermute | solution.py:201
  80.3 0.8 collective-permute-start.27
  81.1 1.9 %shard_map.109 = (bf16[80,1152]{1,0:T(8,128)(2,1)S(1)}, bf16[80,1152]{1,0:T(8,128)(2,1)S(1)}, bf16[80,1152]{1,0:T(8,128)(2,1)S(1)}, bf16[80,1152]{1,0:T(8,128)(2...) custom-call(s32[2]{0:T(128)S(1)} %copy-done.3, ...), custom_call_target="tpu_custom_call" | custom-call | flops 922746880 | bytes 5832712 | tf_op jit(solution)/shard_map/pallas_call | solution.py:31
  83.0 1.2 collective-permute-done.26.refs_5_
  84.2 0.8 collective-permute-start.34
  85.0 3.1 %collective-permute-done.27.refs_7_ = bf16[80,1152]{1,0:T(8,128)(2,1)S(1)} collective-permute-done((bf16[80,1152]{1,0:T(8,128)(2,1)S(1)}, bf16[80,1152]{1,0:T(8,128)(2,1)S(1)}, u32[]{:S(2)}, u32[]{:S(2)}) %collective-permute-start.27) | collective-permute-done | bytes 184352 | tf_op jit(solution)/shard_map/ppermute | solution.py:201
  88.2 0.8 collective-permute-start.35
  89.0 2.7 %shard_map.106 = (bf16[128,2176]{1,0:T(8,128)(2,1)S(1)}, bf16[128,2176]{1,0:T(8,128)(2,1)S(1)}, bf16[160,768]{1,0:T(8,128)(2,1)S(1)}) custom-call(s32[2]{0:T(128)S(1)} %copy-done.3, bf16[80,1152]{1,0:T(8,128)(2,1)S(1)} %get-tuple-element.78.refs_0_, bf16[80,1152]{1,0:T(8,128)(2,1)S(1)} %collective-permute-done.4.refs_1_, ...), custom_call_target="tpu_custom_call" | custom-call | flops 1396703232 | bytes 6357000 | tf_op jit(solution)/shard_map/pallas_call | solution.py:31
  92.1 0.9 collective-permute-start.36
  93.0 3.0 %collective-permute-done.35.refs_3_ = bf16[80,1152]{1,0:T(8,128)(2,1)S(1)} collective-permute-done((bf16[80,1152]{1,0:T(8,128)(2,1)S(1)}, bf16[80,1152]{1,0:T(8,128)(2,1)S(1)}, u32[]{:S(2)}, u32[]{:S(2)}) %collective-permute-start.35) | collective-permute-done | bytes 184352 | tf_op jit(solution)/shard_map/ppermute | solution.py:201
  96.1 0.7 collective-permute-start.37
  96.8 1.0 collective-permute-start.22
  97.8 1.2 collective-permute-start.13
  99.0 2.7 %shard_map.110 = (bf16[128,2176]{1,0:T(8,128)(2,1)S(1)}, bf16[128,2176]{1,0:T(8,128)(2,1)S(1)}, bf16[160,768]{1,0:T(8,128)(2,1)S(1)}) custom-call(s32[2]{0:T(128)S(1)} %copy-done.3, bf16[80,1152]{1,0:T(8,128)(2,1)S(1)} %get-tuple-element.105.refs_0_, bf16[80,1152]{1,0:T(8,128)(2,1)S(1)} %collective-permute-done.24.refs_1_, ...), custom_call_target="tpu_custom_call" | custom-call | flops 1396703232 | bytes 6357000 | tf_op jit(solution)/shard_map/pallas_call | solution.py:31
  101.8 1.7 %collective-permute-done.37.refs_7_ = bf16[80,1152]{1,0:T(8,128)(2,1)S(1)} collective-permute-done((bf16[80,1152]{1,0:T(8,128)(2,1)S(1)}, bf16[80,1152]{1,0:T(8,128)(2,1)S(1)}, u32[]{:S(2)}, u32[]{:S(2)}) %collective-permute-start.37) | collective-permute-done | bytes 184352 | tf_op jit(solution)/shard_map/ppermute | solution.py:201
  103.5 2.9 %shard_map.111 = (bf16[128,2176]{1,0:T(8,128)(2,1)S(1)}, bf16[128,2176]{1,0:T(8,128)(2,1)S(1)}, bf16[160,768]{1,0:T(8,128)(2,1)S(1)}) custom-call(s32[2]{0:T(128)S(1)} %copy-done.3, bf16[80,1152]{1,0:T(8,128)(2,1)S(1)} %get-tuple-element.119.refs_0_, bf16[80,1152]{1,0:T(8,128)(2,1)S(1)} %collective-permute-done.34.refs_1_, ...), custom_call_target="tpu_custom_call" | custom-call | flops 1396703232 | bytes 6357000 | tf_op jit(solution)/shard_map/pallas_call | solution.py:31
  106.9 1.5 %collective-permute-start.32 = (bf16[64,2176]{1,0:T(8,128)(2,1)S(1)}, bf16[64,2176]{1,0:T(8,128)(2,1)S(1)}, u32[]{:S(2)}, u32[]{:S(2)}) collective-permute-start(bf16[64,2176]{1,0:T(8,128)(2,1)S(1)} %add_convert_fusion.5), channel_id=1, source_target_pairs={{0,2},{1,3},{2,0},{3,1},{4,6},{5,7},{6,4},{7,5},{8,10},{9,11},{10,... | collective-permute-start | bytes 835592 | tf_op jit(solution)/shard_map/ppermute | solution.py:214
  108.5 1.6 %collective-permute-start.39 = (bf16[64,2176]{1,0:T(8,128)(2,1)S(1)}, bf16[64,2176]{1,0:T(8,128)(2,1)S(1)}, u32[]{:S(2)}, u32[]{:S(2)}) collective-permute-start(bf16[64,2176]{1,0:T(8,128)(2,1)S(1)} %add_convert_fusion.2), channel_id=1, source_target_pairs={{0,2},{1,3},{2,0},{3,1},{4,6},{5,7},{6,4},{7,5},{8,10},{9,11},{10,... | collective-permute-start | bytes 835592 | tf_op jit(solution)/shard_map/ppermute | solution.py:214
  110.1 6.8 %collective-permute-done.32 = bf16[64,2176]{1,0:T(8,128)(2,1)S(1)} collective-permute-done((bf16[64,2176]{1,0:T(8,128)(2,1)S(1)}, bf16[64,2176]{1,0:T(8,128)(2,1)S(1)}, u32[]{:S(2)}, u32[]{:S(2)}) %collective-permute-start.32) | collective-permute-done | bytes 278560 | tf_op jit(solution)/shard_map/ppermute | solution.py:214
  117.0 4.0 %collective-permute-start.33 = (bf16[64,2176]{1,0:T(8,128)(2,1)S(1)}, bf16[64,2176]{1,0:T(8,128)(2,1)S(1)}, u32[]{:S(2)}, u32[]{:S(2)}) collective-permute-start(bf16[64,2176]{1,0:T(8,128)(2,1)S(1)} %add_convert_fusion.4), channel_id=1, source_target_pairs={{0,12},{1,13},{2,14},{3,15},{4,0},{5,1},{6,2},{7,3},{8,4},{9,5},{1... | collective-permute-start | bytes 835592 | tf_op jit(solution)/shard_map/ppermute | solution.py:205
  121.0 1.4 collective-permute-done.39
  122.5 4.3 %collective-permute-start.40 = (bf16[64,2176]{1,0:T(8,128)(2,1)S(1)}, bf16[64,2176]{1,0:T(8,128)(2,1)S(1)}, u32[]{:S(2)}, u32[]{:S(2)}) collective-permute-start(bf16[64,2176]{1,0:T(8,128)(2,1)S(1)} %add_convert_fusion.1), channel_id=1, source_target_pairs={{0,4},{1,5},{2,6},{3,7},{4,8},{5,9},{6,10},{7,11},{8,12},{9,13},{1... | collective-permute-start | bytes 835592 | tf_op jit(solution)/shard_map/ppermute | solution.py:205
  126.8 7.8 %collective-permute-done.33 = bf16[64,2176]{1,0:T(8,128)(2,1)S(1)} collective-permute-done((bf16[64,2176]{1,0:T(8,128)(2,1)S(1)}, bf16[64,2176]{1,0:T(8,128)(2,1)S(1)}, u32[]{:S(2)}, u32[]{:S(2)}) %collective-permute-start.33) | collective-permute-done | bytes 278560 | tf_op jit(solution)/shard_map/ppermute | solution.py:205
  134.8 0.9 collective-permute-start.41
  135.7 3.2 %shard_map.113 = bf16[1024,768]{1,0:T(8,128)(2,1)} custom-call(s32[2]{0:T(128)S(1)} %copy-done.3, bf16[160,1024]{1,0:T(8,128)(2,1)S(1)} %get-tuple-element.132.refs_0_, bf16[160,1024]{1,0:T(8,128)(2,1)S(1)} %get-tuple-element.133.refs_1_, bf16[160,1024]{1,0:T(8,128)(2,1)S(1)} %get-tuple-element.134.refs_2_, ...), custom_call_target="tpu_custom_call" | custom-call | flops 1006632960 | bytes 2293768 | tf_op jit(solution)/shard_map/pallas_call | solution.py:31
  138.9 1.0 collective-permute-done.41.refs_0_
  139.9 1.5 %shard_map.112 = (bf16[32,2048]{1,0:T(8,128)(2,1)}, bf16[32,2048]{1,0:T(8,128)(2,1)}, f32[8,32]{1,0:T(8,128)}) custom-call(s32[2]{0:T(128)S(1)} %copy-done.3, bf16[32,2176]{1,0:T(8,128)(2,1)S(1)} %slice.80.own, s32[8,32]{1,0:T(8,128)S(1)} %bitcast.13, bf16[32,2048]{1,0:T(8,128)(2,1)S(1)} %collective-permute-done.41.refs_0_), custom_call_target="tpu_custom_call" | custom-call | bytes 271368 | tf_op jit(solution)/shard_map/pallas_call | solution.py:31
  (64 shorter events, 5.3 us)
Async XLA Ops:
  3.6 18.0 %collective-permute-start.9 = (bf16[32,2176]{1,0:T(8,128)(2,1)}, bf16[32,2176]{1,0:T(8,128)(2,1)S(1)}, u32[]{:S(2)}, u32[]{:S(2)}) collective-permute-start(bf16[32,2176]{1,0:T(8,128)(2,1)} %get-tuple-element.73), channel_id=1, source_target_pairs={{0,24},{1,25},{2,26},{3,27},{4,28},{5,29},{6,30},{7,31},{8,16},{9,... | collective-permute-start | bytes 417800 | tf_op jit(solution)/shard_map/ppermute | solution.py:211
  8.7 15.3 %collective-permute-start.2 = (bf16[32,2176]{1,0:T(8,128)(2,1)}, bf16[32,2176]{1,0:T(8,128)(2,1)S(1)}, u32[]{:S(2)}, u32[]{:S(2)}) collective-permute-start(bf16[32,2176]{1,0:T(8,128)(2,1)} %get-tuple-element.73), channel_id=1, source_target_pairs={{0,18},{1,19},{2,16},{3,17},{4,22},{5,23},{6,20},{7,21},{8,26},{9,... | collective-permute-start | bytes 417800 | tf_op jit(solution)/shard_map/ppermute | solution.py:211
  10.1 13.1 %collective-permute-start = (bf16[32,2176]{1,0:T(8,128)(2,1)}, bf16[32,2176]{1,0:T(8,128)(2,1)S(1)}, u32[]{:S(2)}, u32[]{:S(2)}) collective-permute-start(bf16[32,2176]{1,0:T(8,128)(2,1)} %get-tuple-element.73), channel_id=1, source_target_pairs={{0,16},{16,0},{1,17},{17,1},{2,18},{18,2},{3,19},{19,3},{4,20},{20... | collective-permute-start | bytes 417800 | tf_op jit(solution)/shard_map/ppermute | solution.py:201
  11.6 9.9 %collective-permute-start.8 = (bf16[32,2176]{1,0:T(8,128)(2,1)}, bf16[32,2176]{1,0:T(8,128)(2,1)S(1)}, u32[]{:S(2)}, u32[]{:S(2)}) collective-permute-start(bf16[32,2176]{1,0:T(8,128)(2,1)} %get-tuple-element.72), channel_id=1, source_target_pairs={{0,8},{1,9},{2,10},{3,11},{4,12},{5,13},{6,14},{7,15},{8,0},{9,1},... | collective-permute-start | bytes 417800 | tf_op jit(solution)/shard_map/ppermute | solution.py:211
  12.0 12.1 %collective-permute-start.1 = (bf16[32,2176]{1,0:T(8,128)(2,1)}, bf16[32,2176]{1,0:T(8,128)(2,1)S(1)}, u32[]{:S(2)}, u32[]{:S(2)}) collective-permute-start(bf16[32,2176]{1,0:T(8,128)(2,1)} %get-tuple-element.72), channel_id=1, source_target_pairs={{0,2},{1,3},{2,0},{3,1},{4,6},{5,7},{6,4},{7,5},{8,10},{9,11},{10,... | collective-permute-start | bytes 417800 | tf_op jit(solution)/shard_map/ppermute | solution.py:211
  13.5 1.4 copy-start
  14.9 1.4 copy-start.1
  16.3 1.4 copy-start.2
  17.7 0.7 copy-start.3
  18.3 5.7 %copy-start.5 = (bf16[32,2176]{1,0:T(8,128)(2,1)S(1)}, bf16[32,2176]{1,0:T(8,128)(2,1)}, u32[]{:S(2)}) copy-start(bf16[32,2176]{1,0:T(8,128)(2,1)} %get-tuple-element.72) | copy-start | bytes 417796
  21.6 7.6 %collective-permute-start.10 = (bf16[64,2176]{1,0:T(8,128)(2,1)S(1)}, bf16[64,2176]{1,0:T(8,128)(2,1)S(1)}, u32[]{:S(2)}, u32[]{:S(2)}) collective-permute-start(bf16[64,2176]{1,0:T(8,128)(2,1)S(1)} %constant_dynamic-update-slice_fusion.2.near), channel_id=1, source_target_pairs={{0,2},{1,3},{2,0},{3,1},{4,6},{5,7},{6,4},{7,5},{8,10},{9,11},{10,... | collective-permute-start | bytes 835592 | tf_op jit(solution)/shard_map/ppermute | solution.py:214
  23.2 10.2 %collective-permute-start.18 = (bf16[64,2176]{1,0:T(8,128)(2,1)S(1)}, bf16[64,2176]{1,0:T(8,128)(2,1)S(1)}, u32[]{:S(2)}, u32[]{:S(2)}) collective-permute-start(bf16[64,2176]{1,0:T(8,128)(2,1)S(1)} %constant_dynamic-update-slice_fusion.near), channel_id=1, source_target_pairs={{0,4},{1,5},{2,6},{3,7},{4,8},{5,9},{6,10},{7,11},{8,12},{9,13},{1... | collective-permute-start | bytes 835592 | tf_op jit(solution)/shard_map/ppermute | solution.py:205
  24.1 5.3 %collective-permute-start.3 = (bf16[128,2176]{1,0:T(8,128)(2,1)S(1)}, bf16[128,2176]{1,0:T(8,128)(2,1)S(1)}, u32[]{:S(2)}, u32[]{:S(2)}) collective-permute-start(bf16[128,2176]{1,0:T(8,128)(2,1)S(1)} %pad_maximum_fusion), channel_id=1, source_target_pairs={{0,1},{1,0},{2,3},{3,2},{4,5},{5,4},{6,7},{7,6},{8,9},{9,8},{10,11... | collective-permute-start | bytes 1671176 | tf_op jit(solution)/shard_map/ppermute | solution.py:214
  29.3 16.1 %collective-permute-start.11 = (bf16[128,2176]{1,0:T(8,128)(2,1)S(1)}, bf16[128,2176]{1,0:T(8,128)(2,1)S(1)}, u32[]{:S(2)}, u32[]{:S(2)}) collective-permute-start(bf16[128,2176]{1,0:T(8,128)(2,1)S(1)} %pad_maximum_fusion.1), channel_id=1, source_target_pairs={{0,1},{1,0},{2,3},{3,2},{4,5},{5,4},{6,7},{7,6},{8,9},{9,8},{10,11... | collective-permute-start | bytes 1671176 | tf_op jit(solution)/shard_map/ppermute | solution.py:214
  31.3 8.0 %collective-permute-start.4 = (bf16[80,1152]{1,0:T(8,128)(2,1)S(1)}, bf16[80,1152]{1,0:T(8,128)(2,1)S(1)}, u32[]{:S(2)}, u32[]{:S(2)}) collective-permute-start(bf16[80,1152]{1,0:T(8,128)(2,1)S(1)} %get-tuple-element.78.refs_0_), channel_id=1, source_target_pairs={{0,16},{16,0},{1,17},{17,1},{2,18},{18,2},{3,19},{19,3},{4,20},{20... | collective-permute-start | bytes 552968 | tf_op jit(solution)/shard_map/ppermute | solution.py:201
  32.2 10.6 %collective-permute-start.5 = (bf16[80,1152]{1,0:T(8,128)(2,1)S(1)}, bf16[80,1152]{1,0:T(8,128)(2,1)S(1)}, u32[]{:S(2)}, u32[]{:S(2)}) collective-permute-start(bf16[80,1152]{1,0:T(8,128)(2,1)S(1)} %get-tuple-element.79.refs_2_), channel_id=1, source_target_pairs={{0,16},{16,0},{1,17},{17,1},{2,18},{18,2},{3,19},{19,3},{4,20},{20... | collective-permute-start | bytes 552968 | tf_op jit(solution)/shard_map/ppermute | solution.py:201
  33.4 10.5 %collective-permute-start.28 = (bf16[64,2176]{1,0:T(8,128)(2,1)S(1)}, bf16[64,2176]{1,0:T(8,128)(2,1)S(1)}, u32[]{:S(2)}, u32[]{:S(2)}) collective-permute-start(bf16[64,2176]{1,0:T(8,128)(2,1)S(1)} %constant_dynamic-update-slice_fusion.near), channel_id=1, source_target_pairs={{0,12},{1,13},{2,14},{3,15},{4,0},{5,1},{6,2},{7,3},{8,4},{9,5},{1... | collective-permute-start | bytes 835592 | tf_op jit(solution)/shard_map/ppermute | solution.py:205
  37.9 13.6 %collective-permute-start.19 = (bf16[64,2176]{1,0:T(8,128)(2,1)S(1)}, bf16[64,2176]{1,0:T(8,128)(2,1)S(1)}, u32[]{:S(2)}, u32[]{:S(2)}) collective-permute-start(bf16[64,2176]{1,0:T(8,128)(2,1)S(1)} %collective-permute-done.18.near), channel_id=1, source_target_pairs={{0,2},{1,3},{2,0},{3,1},{4,6},{5,7},{6,4},{7,5},{8,10},{9,11},{10,... | collective-permute-start | bytes 835592 | tf_op jit(solution)/shard_map/ppermute | solution.py:214
  39.4 7.9 %collective-permute-start.6 = (bf16[80,1152]{1,0:T(8,128)(2,1)S(1)}, bf16[80,1152]{1,0:T(8,128)(2,1)S(1)}, u32[]{:S(2)}, u32[]{:S(2)}) collective-permute-start(bf16[80,1152]{1,0:T(8,128)(2,1)S(1)} %get-tuple-element.81.refs_4_), channel_id=1, source_target_pairs={{0,16},{16,0},{1,17},{17,1},{2,18},{18,2},{3,19},{19,3},{4,20},{20... | collective-permute-start | bytes 552968 | tf_op jit(solution)/shard_map/ppermute | solution.py:201
  42.8 8.1 %collective-permute-start.7 = (bf16[80,1152]{1,0:T(8,128)(2,1)S(1)}, bf16[80,1152]{1,0:T(8,128)(2,1)S(1)}, u32[]{:S(2)}, u32[]{:S(2)}) collective-permute-start(bf16[80,1152]{1,0:T(8,128)(2,1)S(1)} %get-tuple-element.83.refs_6_), channel_id=1, source_target_pairs={{0,16},{16,0},{1,17},{17,1},{2,18},{18,2},{3,19},{19,3},{4,20},{20... | collective-permute-start | bytes 552968 | tf_op jit(solution)/shard_map/ppermute | solution.py:201
  43.9 15.9 %collective-permute-start.29 = (bf16[64,2176]{1,0:T(8,128)(2,1)S(1)}, bf16[64,2176]{1,0:T(8,128)(2,1)S(1)}, u32[]{:S(2)}, u32[]{:S(2)}) collective-permute-start(bf16[64,2176]{1,0:T(8,128)(2,1)S(1)} %collective-permute-done.28.near), channel_id=1, source_target_pairs={{0,2},{1,3},{2,0},{3,1},{4,6},{5,7},{6,4},{7,5},{8,10},{9,11},{10,... | collective-permute-start | bytes 835592 | tf_op jit(solution)/shard_map/ppermute | solution.py:214
  47.3 7.6 %collective-permute-start.14 = (bf16[80,1152]{1,0:T(8,128)(2,1)S(1)}, bf16[80,1152]{1,0:T(8,128)(2,1)S(1)}, u32[]{:S(2)}, u32[]{:S(2)}) collective-permute-start(bf16[80,1152]{1,0:T(8,128)(2,1)S(1)} %get-tuple-element.91.refs_0_), channel_id=1, source_target_pairs={{0,16},{16,0},{1,17},{17,1},{2,18},{18,2},{3,19},{19,3},{4,20},{20... | collective-permute-start | bytes 552968 | tf_op jit(solution)/shard_map/ppermute | solution.py:201
  50.9 8.0 %collective-permute-start.15 = (bf16[80,1152]{1,0:T(8,128)(2,1)S(1)}, bf16[80,1152]{1,0:T(8,128)(2,1)S(1)}, u32[]{:S(2)}, u32[]{:S(2)}) collective-permute-start(bf16[80,1152]{1,0:T(8,128)(2,1)S(1)} %get-tuple-element.93.refs_2_), channel_id=1, source_target_pairs={{0,16},{16,0},{1,17},{17,1},{2,18},{18,2},{3,19},{19,3},{4,20},{20... | collective-permute-start | bytes 552968 | tf_op jit(solution)/shard_map/ppermute | solution.py:201
  51.5 8.4 %collective-permute-start.20 = (bf16[128,2176]{1,0:T(8,128)(2,1)S(1)}, bf16[128,2176]{1,0:T(8,128)(2,1)S(1)}, u32[]{:S(2)}, u32[]{:S(2)}) collective-permute-start(bf16[128,2176]{1,0:T(8,128)(2,1)S(1)} %pad_maximum_fusion.2), channel_id=1, source_target_pairs={{0,1},{1,0},{2,3},{3,2},{4,5},{5,4},{6,7},{7,6},{8,9},{9,8},{10,11... | collective-permute-start | bytes 1671176 | tf_op jit(solution)/shard_map/ppermute | solution.py:214
  55.0 7.9 %collective-permute-start.16 = (bf16[80,1152]{1,0:T(8,128)(2,1)S(1)}, bf16[80,1152]{1,0:T(8,128)(2,1)S(1)}, u32[]{:S(2)}, u32[]{:S(2)}) collective-permute-start(bf16[80,1152]{1,0:T(8,128)(2,1)S(1)} %get-tuple-element.95.refs_4_), channel_id=1, source_target_pairs={{0,16},{16,0},{1,17},{17,1},{2,18},{18,2},{3,19},{19,3},{4,20},{20... | collective-permute-start | bytes 552968 | tf_op jit(solution)/shard_map/ppermute | solution.py:201
  58.9 7.2 %collective-permute-start.17 = (bf16[80,1152]{1,0:T(8,128)(2,1)S(1)}, bf16[80,1152]{1,0:T(8,128)(2,1)S(1)}, u32[]{:S(2)}, u32[]{:S(2)}) collective-permute-start(bf16[80,1152]{1,0:T(8,128)(2,1)S(1)} %get-tuple-element.97.refs_6_), channel_id=1, source_target_pairs={{0,16},{16,0},{1,17},{17,1},{2,18},{18,2},{3,19},{19,3},{4,20},{20... | collective-permute-start | bytes 552968 | tf_op jit(solution)/shard_map/ppermute | solution.py:201
  59.9 21.2 %collective-permute-start.30 = (bf16[128,2176]{1,0:T(8,128)(2,1)S(1)}, bf16[128,2176]{1,0:T(8,128)(2,1)S(1)}, u32[]{:S(2)}, u32[]{:S(2)}) collective-permute-start(bf16[128,2176]{1,0:T(8,128)(2,1)S(1)} %pad_maximum_fusion.3), channel_id=1, source_target_pairs={{0,1},{1,0},{2,3},{3,2},{4,5},{5,4},{6,7},{7,6},{8,9},{9,8},{10,11... | collective-permute-start | bytes 1671176 | tf_op jit(solution)/shard_map/ppermute | solution.py:214
  68.7 28.0 %collective-permute-start.21 = (bf16[128,2176]{1,0:T(8,128)(2,1)S(1)}, bf16[128,2176]{1,0:T(8,128)(2,1)S(1)}, u32[]{:S(2)}, u32[]{:S(2)}) collective-permute-start(bf16[128,2176]{1,0:T(8,128)(2,1)S(1)} %get-tuple-element.103), channel_id=1, source_target_pairs={{0,1},{1,0},{2,3},{3,2},{4,5},{5,4},{6,7},{7,6},{8,9},{9,8},{10,11... | collective-permute-start | bytes 1671176 | tf_op jit(solution)/shard_map/ppermute | solution.py:214
  68.8 7.5 %collective-permute-start.24 = (bf16[80,1152]{1,0:T(8,128)(2,1)S(1)}, bf16[80,1152]{1,0:T(8,128)(2,1)S(1)}, u32[]{:S(2)}, u32[]{:S(2)}) collective-permute-start(bf16[80,1152]{1,0:T(8,128)(2,1)S(1)} %get-tuple-element.105.refs_0_), channel_id=1, source_target_pairs={{0,16},{16,0},{1,17},{17,1},{2,18},{18,2},{3,19},{19,3},{4,20},{20... | collective-permute-start | bytes 552968 | tf_op jit(solution)/shard_map/ppermute | solution.py:201
  69.7 10.6 %collective-permute-start.25 = (bf16[80,1152]{1,0:T(8,128)(2,1)S(1)}, bf16[80,1152]{1,0:T(8,128)(2,1)S(1)}, u32[]{:S(2)}, u32[]{:S(2)}) collective-permute-start(bf16[80,1152]{1,0:T(8,128)(2,1)S(1)} %get-tuple-element.107.refs_2_), channel_id=1, source_target_pairs={{0,16},{16,0},{1,17},{17,1},{2,18},{18,2},{3,19},{19,3},{4,20},{20... | collective-permute-start | bytes 552968 | tf_op jit(solution)/shard_map/ppermute | solution.py:201
  76.3 7.9 %collective-permute-start.26 = (bf16[80,1152]{1,0:T(8,128)(2,1)S(1)}, bf16[80,1152]{1,0:T(8,128)(2,1)S(1)}, u32[]{:S(2)}, u32[]{:S(2)}) collective-permute-start(bf16[80,1152]{1,0:T(8,128)(2,1)S(1)} %get-tuple-element.109.refs_4_), channel_id=1, source_target_pairs={{0,16},{16,0},{1,17},{17,1},{2,18},{18,2},{3,19},{19,3},{4,20},{20... | collective-permute-start | bytes 552968 | tf_op jit(solution)/shard_map/ppermute | solution.py:201
  80.3 7.9 %collective-permute-start.27 = (bf16[80,1152]{1,0:T(8,128)(2,1)S(1)}, bf16[80,1152]{1,0:T(8,128)(2,1)S(1)}, u32[]{:S(2)}, u32[]{:S(2)}) collective-permute-start(bf16[80,1152]{1,0:T(8,128)(2,1)S(1)} %get-tuple-element.111.refs_6_), channel_id=1, source_target_pairs={{0,16},{16,0},{1,17},{17,1},{2,18},{18,2},{3,19},{19,3},{4,20},{20... | collective-permute-start | bytes 552968 | tf_op jit(solution)/shard_map/ppermute | solution.py:201
  84.2 7.9 %collective-permute-start.34 = (bf16[80,1152]{1,0:T(8,128)(2,1)S(1)}, bf16[80,1152]{1,0:T(8,128)(2,1)S(1)}, u32[]{:S(2)}, u32[]{:S(2)}) collective-permute-start(bf16[80,1152]{1,0:T(8,128)(2,1)S(1)} %get-tuple-element.119.refs_0_), channel_id=1, source_target_pairs={{0,16},{16,0},{1,17},{17,1},{2,18},{18,2},{3,19},{19,3},{4,20},{20... | collective-permute-start | bytes 552968 | tf_op jit(solution)/shard_map/ppermute | solution.py:201
  88.2 7.9 %collective-permute-start.35 = (bf16[80,1152]{1,0:T(8,128)(2,1)S(1)}, bf16[80,1152]{1,0:T(8,128)(2,1)S(1)}, u32[]{:S(2)}, u32[]{:S(2)}) collective-permute-start(bf16[80,1152]{1,0:T(8,128)(2,1)S(1)} %get-tuple-element.121.refs_2_), channel_id=1, source_target_pairs={{0,16},{16,0},{1,17},{17,1},{2,18},{18,2},{3,19},{19,3},{4,20},{20... | collective-permute-start | bytes 552968 | tf_op jit(solution)/shard_map/ppermute | solution.py:201
  91.7 6.1 %collective-permute-start.12 = (bf16[128,2176]{1,0:T(8,128)(2,1)S(1)}, bf16[128,2176]{1,0:T(8,128)(2,1)S(1)}, u32[]{:S(2)}, u32[]{:S(2)}) collective-permute-start(bf16[128,2176]{1,0:T(8,128)(2,1)S(1)} %get-tuple-element.89), channel_id=1, source_target_pairs={{0,1},{1,0},{2,3},{3,2},{4,5},{5,4},{6,7},{7,6},{8,9},{9,8},{10,11... | collective-permute-start | bytes 1671176 | tf_op jit(solution)/shard_map/ppermute | solution.py:214
  92.1 9.7 %collective-permute-start.36 = (bf16[80,1152]{1,0:T(8,128)(2,1)S(1)}, bf16[80,1152]{1,0:T(8,128)(2,1)S(1)}, u32[]{:S(2)}, u32[]{:S(2)}) collective-permute-start(bf16[80,1152]{1,0:T(8,128)(2,1)S(1)} %get-tuple-element.123.refs_4_), channel_id=1, source_target_pairs={{0,16},{16,0},{1,17},{17,1},{2,18},{18,2},{3,19},{19,3},{4,20},{20... | collective-permute-start | bytes 552968 | tf_op jit(solution)/shard_map/ppermute | solution.py:201
  96.1 7.4 %collective-permute-start.37 = (bf16[80,1152]{1,0:T(8,128)(2,1)S(1)}, bf16[80,1152]{1,0:T(8,128)(2,1)S(1)}, u32[]{:S(2)}, u32[]{:S(2)}) collective-permute-start(bf16[80,1152]{1,0:T(8,128)(2,1)S(1)} %get-tuple-element.125.refs_6_), channel_id=1, source_target_pairs={{0,16},{16,0},{1,17},{17,1},{2,18},{18,2},{3,19},{19,3},{4,20},{20... | collective-permute-start | bytes 552968 | tf_op jit(solution)/shard_map/ppermute | solution.py:201
  96.8 9.7 %collective-permute-start.22 = (bf16[64,2176]{1,0:T(8,128)(2,1)S(1)}, bf16[64,2176]{1,0:T(8,128)(2,1)S(1)}, u32[]{:S(2)}, u32[]{:S(2)}) collective-permute-start(bf16[64,2176]{1,0:T(8,128)(2,1)S(1)} %add_convert_fusion.8), channel_id=1, source_target_pairs={{0,2},{1,3},{2,0},{3,1},{4,6},{5,7},{6,4},{7,5},{8,10},{9,11},{10,... | collective-permute-start | bytes 835592 | tf_op jit(solution)/shard_map/ppermute | solution.py:214
  97.8 28.9 %collective-permute-start.13 = (bf16[64,2176]{1,0:T(8,128)(2,1)S(1)}, bf16[64,2176]{1,0:T(8,128)(2,1)S(1)}, u32[]{:S(2)}, u32[]{:S(2)}) collective-permute-start(bf16[64,2176]{1,0:T(8,128)(2,1)S(1)} %add_convert_fusion.11), channel_id=1, source_target_pairs={{0,2},{1,3},{2,0},{3,1},{4,6},{5,7},{6,4},{7,5},{8,10},{9,11},{10,... | collective-permute-start | bytes 835592 | tf_op jit(solution)/shard_map/ppermute | solution.py:214
  101.7 5.1 %collective-permute-start.31 = (bf16[128,2176]{1,0:T(8,128)(2,1)S(1)}, bf16[128,2176]{1,0:T(8,128)(2,1)S(1)}, u32[]{:S(2)}, u32[]{:S(2)}) collective-permute-start(bf16[128,2176]{1,0:T(8,128)(2,1)S(1)} %get-tuple-element.117), channel_id=1, source_target_pairs={{0,1},{1,0},{2,3},{3,2},{4,5},{5,4},{6,7},{7,6},{8,9},{9,8},{10,11... | collective-permute-start | bytes 1671176 | tf_op jit(solution)/shard_map/ppermute | solution.py:214
  106.4 2.0 %collective-permute-start.38 = (bf16[128,2176]{1,0:T(8,128)(2,1)S(1)}, bf16[128,2176]{1,0:T(8,128)(2,1)S(1)}, u32[]{:S(2)}, u32[]{:S(2)}) collective-permute-start(bf16[128,2176]{1,0:T(8,128)(2,1)S(1)} %get-tuple-element.128), channel_id=1, source_target_pairs={{0,1},{1,0},{2,3},{3,2},{4,5},{5,4},{6,7},{7,6},{8,9},{9,8},{10,11... | collective-permute-start | bytes 1671176 | tf_op jit(solution)/shard_map/ppermute | solution.py:214
  106.6 20.2 %collective-permute-start.23 = (bf16[64,2176]{1,0:T(8,128)(2,1)S(1)}, bf16[64,2176]{1,0:T(8,128)(2,1)S(1)}, u32[]{:S(2)}, u32[]{:S(2)}) collective-permute-start(bf16[64,2176]{1,0:T(8,128)(2,1)S(1)} %add_convert_fusion.7), channel_id=1, source_target_pairs={{0,8},{1,9},{2,10},{3,11},{4,12},{5,13},{6,14},{7,15},{8,0},{9,1},... | collective-permute-start | bytes 835592 | tf_op jit(solution)/shard_map/ppermute | solution.py:205
  106.9 10.0 %collective-permute-start.32 = (bf16[64,2176]{1,0:T(8,128)(2,1)S(1)}, bf16[64,2176]{1,0:T(8,128)(2,1)S(1)}, u32[]{:S(2)}, u32[]{:S(2)}) collective-permute-start(bf16[64,2176]{1,0:T(8,128)(2,1)S(1)} %add_convert_fusion.5), channel_id=1, source_target_pairs={{0,2},{1,3},{2,0},{3,1},{4,6},{5,7},{6,4},{7,5},{8,10},{9,11},{10,... | collective-permute-start | bytes 835592 | tf_op jit(solution)/shard_map/ppermute | solution.py:214
  108.5 13.9 %collective-permute-start.39 = (bf16[64,2176]{1,0:T(8,128)(2,1)S(1)}, bf16[64,2176]{1,0:T(8,128)(2,1)S(1)}, u32[]{:S(2)}, u32[]{:S(2)}) collective-permute-start(bf16[64,2176]{1,0:T(8,128)(2,1)S(1)} %add_convert_fusion.2), channel_id=1, source_target_pairs={{0,2},{1,3},{2,0},{3,1},{4,6},{5,7},{6,4},{7,5},{8,10},{9,11},{10,... | collective-permute-start | bytes 835592 | tf_op jit(solution)/shard_map/ppermute | solution.py:214
  117.0 17.5 %collective-permute-start.33 = (bf16[64,2176]{1,0:T(8,128)(2,1)S(1)}, bf16[64,2176]{1,0:T(8,128)(2,1)S(1)}, u32[]{:S(2)}, u32[]{:S(2)}) collective-permute-start(bf16[64,2176]{1,0:T(8,128)(2,1)S(1)} %add_convert_fusion.4), channel_id=1, source_target_pairs={{0,12},{1,13},{2,14},{3,15},{4,0},{5,1},{6,2},{7,3},{8,4},{9,5},{1... | collective-permute-start | bytes 835592 | tf_op jit(solution)/shard_map/ppermute | solution.py:205
  122.5 12.0 %collective-permute-start.40 = (bf16[64,2176]{1,0:T(8,128)(2,1)S(1)}, bf16[64,2176]{1,0:T(8,128)(2,1)S(1)}, u32[]{:S(2)}, u32[]{:S(2)}) collective-permute-start(bf16[64,2176]{1,0:T(8,128)(2,1)S(1)} %add_convert_fusion.1), channel_id=1, source_target_pairs={{0,4},{1,5},{2,6},{3,7},{4,8},{5,9},{6,10},{7,11},{8,12},{9,13},{1... | collective-permute-start | bytes 835592 | tf_op jit(solution)/shard_map/ppermute | solution.py:205
  134.8 5.0 %collective-permute-start.41 = (bf16[32,2048]{1,0:T(8,128)(2,1)S(1)}, bf16[32,2048]{1,0:T(8,128)(2,1)S(1)}, u32[]{:S(2)}, u32[]{:S(2)}) collective-permute-start(bf16[32,2048]{1,0:T(8,128)(2,1)S(1)} %slice.81), channel_id=1, source_target_pairs={{0,16},{16,0},{1,17},{17,1},{2,18},{18,2},{3,19},{19,3},{4,20},{20... | collective-permute-start | bytes 393224 | tf_op jit(solution)/shard_map/ppermute | solution.py:201
  135.7 4.2 %copy-start.4 = (s32[32,8]{0,1:T(8,128)S(1)}, s32[32,8]{0,1:T(8,128)}, u32[]{:S(2)}) copy-start(s32[32,8]{0,1:T(8,128)} %param.10) | copy-start | bytes 3076
